TPU v7x, 32 devices: a whole 2x2x4 slice. The times are simulated.
32 devices in a mesh: row: 4 (over y, core), col: 8 (over z, x).
Axes of the slice: x: 2, y: 2, z: 4, core: 2. Of those that a mesh axis runs over, the one named last changes fastest.
Arguments:
- ancestor: bfloat16 [32, 32, 256, 256], P('row', 'col'), may hold values from -6 to 6
- tile_mask: int32 [32, 32], P('row', 'col'), may hold values 0 or 1
- member_one: int32 [32], replicated, may hold values 0 or 1
- member_two: int32 [32], replicated, may hold values 0 or 1
- factor_one: bfloat16 [32, 256, 256], P('row'), may hold values from -0.0625 to 0.0625
- factor_two: bfloat16 [32, 256, 256], P('row'), may hold values from -0.0625 to 0.0625
- link_block: bfloat16 [256, 256], replicated, may hold values from -0.375 to 0.375
- inverse_one: float32 [256, 256], replicated, may hold values from -6 to 6
- inverse_two: float32 [256, 256], replicated, may hold values from -6 to 6
Outputs:
- column_one: bfloat16 [32, 256, 256], P(('row', 'col'))
- column_two: bfloat16 [32, 256, 256], P(('row', 'col'))
- diag_one: bfloat16 [256, 256], replicated
- cross_block: bfloat16 [256, 256], replicated
- diag_two: bfloat16 [256, 256], replicated
All inputs are finite; a program needn't handle non-finite values. No bound on the sum of `tile_mask` on one device may be relied on, other than what follows from the above.
Results may differ from a plain program's by a relative error of at most 0.01.
Values may be sent and summed in bfloat16 or wider, within the bound.
No kernel may reach another device: no remote copies, remote signals or barrier semaphores. Data moves between devices by JAX's collectives and lax.ppermute only.
A program may use at most 128 MiB of HBM per device.

v0:
```python
import jax
import jax.numpy as jnp
from jax import lax
from jax.experimental import pallas as pl
from jax.experimental.pallas import tpu as pltpu
from jax.sharding import PartitionSpec as P

F32, BF16 = jnp.float32, jnp.bfloat16
BOTH = ("row", "col")


def transposed_dot(a, b):
    return lax.dot_general(a, b, (((0,), (0,)), ((), ())), preferred_element_type=F32)


def column_kernel(first, second, place, link, keep_one, got_one, keep_two, got_two, column_one, column_two):
    member_one, member_two = (m[place[0]].astype(F32) for m in (first, second))
    one = keep_one[...].astype(F32) + got_one[...].astype(F32)
    column_one[...] = (-member_one * one).astype(BF16)
    two = keep_two[...].astype(F32) + got_two[...].astype(F32)
    two += jnp.dot(column_one[...], link[...], preferred_element_type=F32)
    column_two[...] = (-member_two * two).astype(BF16)


def diagonal_kernel(sums, link, inverse_one, inverse_two, diag_one, cross, diag_two):
    diag_one[...] = (inverse_one[...] + sums[0].astype(F32)).astype(BF16)
    step = jnp.dot(diag_one[...], link[...], preferred_element_type=F32)
    cross[...] = (sums[1].astype(F32) - step).astype(BF16)
    two = inverse_two[...] + sums[2].astype(F32) - transposed_dot(sums[1], link[...])
    diag_two[...] = (two - transposed_dot(link[...], cross[...])).astype(BF16)


def small_kernel(body, n_out, n_dots, tile, operands, scalars=0):
    memory = [pltpu.SMEM] * scalars + [pltpu.VMEM] * (len(operands) - scalars)
    return pl.pallas_call(
        body,
        out_shape=(jax.ShapeDtypeStruct((tile, tile), BF16),) * n_out,
        in_specs=[pl.BlockSpec(memory_space=space) for space in memory],
        out_specs=[pl.BlockSpec(memory_space=pltpu.VMEM)] * n_out,
        cost_estimate=pl.CostEstimate(
            flops=2 * n_dots * tile**3,
            bytes_accessed=4 * len(operands) * tile**2,
            transcendentals=0,
        ),
    )(*operands)


def after(array, *earlier):
    return lax.optimization_barrier((array, *earlier))[0]


def shards(
    ancestor,
    tile_mask,
    member_one,
    member_two,
    factor_one,
    factor_two,
    link_block,
    inverse_one,
    inverse_two,
):
    nrow, ncol = lax.axis_size("row"), lax.axis_size("col")
    row, col = lax.axis_index("row"), lax.axis_index("col")
    rows, cols, tile = ancestor.shape[0], ancestor.shape[1], ancestor.shape[-1]
    group = ncol // nrow
    bits, row_bits = ncol.bit_length() - 1, nrow.bit_length() - 1
    owner = col // group
    at = lambda r, c: r * ncol + c
    everyone = [(r, c) for r in range(nrow) for c in range(ncol)]

    def over_chips(piece, *earlier):
        have = piece
        for k in range(2, nrow, 2):
            perm = [(at(c // group, c), at((c // group + k) % nrow, c)) for c in range(ncol)]
            got = after(lax.ppermute(piece, BOTH, perm), *earlier)
            have = jnp.where((row - owner) % nrow == k, got, have)
        return have

    def over_cores(have):
        perm = [
            (at(2 * y + c // group % 2, c), at(2 * y + 1 - c // group % 2, c))
            for y in range(nrow // 2)
            for c in range(ncol)
        ]
        return jnp.where((row - owner) % 2 == 0, have, lax.ppermute(have, BOTH, perm))

    def swap(array, bit):
        return lax.ppermute(array, BOTH, [(at(r, c), at(r, c ^ (1 << bit))) for r, c in everyone])

    def swap_rows(array, bit):
        return lax.ppermute(array, BOTH, [(at(r, c), at(r ^ (1 << bit), c)) for r, c in everyone])

    def pick(array, bit, other):
        split = array.reshape(array.shape[0] // 2, 2, *array.shape[1:])
        return lax.dynamic_slice_in_dim(split, (col >> bit & 1) ^ other, 1, 1)[:, 0].astype(F32)

    def merged(keep, got, bit, other):
        return pick(keep, bit, other) + pick(got, bit, other)

    def part_of(array, start, size):
        return lax.dynamic_slice_in_dim(array, start, size, 0)

    def masked(marks, array):
        return jnp.where(marks.reshape(marks.shape + (1, 1)) > 0, array, jnp.zeros((), BF16))

    def products(marks, column):
        kept = masked(marks, ancestor)
        return jnp.einsum("ijab,jbc->iac", kept, column, preferred_element_type=F32).astype(BF16)

    def contraction(a, b):
        return jnp.einsum("sab,sac->bc", a, b, preferred_element_type=F32)

    flags_one, flags_two = (part_of(m, row * rows, rows) for m in (member_one, member_two))
    marks = [tile_mask * part_of(m, col * cols, cols)[None] for m in (member_one, member_two)]
    first, second = masked(flags_one, factor_one), masked(flags_two, factor_two)
    second_in_one = masked(flags_one, second)

    piece_one, piece_two = (part_of(f, col % group * cols, cols) for f in (factor_one, factor_two))
    have_one, have_two = over_chips(piece_one, *marks), over_chips(piece_two)
    keep_one = products(marks[0], over_cores(have_one))
    one = [swap(pick(keep_one, 0, 1).astype(BF16), 0)]
    sums_one = contraction(first, keep_one), contraction(keep_one, second_in_one)
    keep_two = products(marks[1], over_cores(after(have_two, keep_one)))
    two = [swap(pick(keep_two, 0, 1).astype(BF16), 0)]
    sums_two = contraction(second, keep_two)
    keep_one, keep_two = pick(keep_one, 0, 0), pick(keep_two, 0, 0)

    for bit in range(1, bits):
        away = merged(keep_one, one[-1], bit, 1).astype(BF16)
        keep_one = merged(keep_one, one[-1], bit, 0)
        one.append(swap(away, bit))
        away = merged(keep_two, two[-1], bit, 1).astype(BF16)
        keep_two = merged(keep_two, two[-1], bit, 0)
        two.append(swap(away, bit))

    sums = jnp.stack([*sums_one, sums_two])
    shape = sums.shape
    part = sums.reshape(-1, tile)
    for bit in range(row_bits):
        half = part.shape[0] // 2
        mine = row >> bit & 1
        if bit == row_bits - 1:
            part = after(part, one[0])
        got = swap_rows(lax.dynamic_slice_in_dim(part, (1 - mine) * half, half, 0).astype(BF16), bit)
        part = lax.dynamic_slice_in_dim(part, mine * half, half, 0) + got.astype(F32)
    part = part.astype(BF16)
    for bit in (*range(1, bits), 0):
        if bit != 1:
            part = after(part, one[1] if bit == 0 else two[0])
        got = swap(part, bit)
        part = (part.astype(F32) + got.astype(F32)).astype(BF16)
    for bit in reversed(range(row_bits)):
        got = swap_rows(after(part, two[-1], one[-1]) if bit == 0 else after(part, two[-2]), bit)
        low = (row >> bit & 1) == 0
        part = jnp.concatenate([jnp.where(low, part, got), jnp.where(low, got, part)])

    column_one, column_two = small_kernel(
        column_kernel,
        2,
        1,
        tile,
        (
            member_one,
            member_two,
            (row * rows + col)[None],
            link_block,
            *(a[0] for a in (keep_one, one[-1], keep_two, two[-1])),
        ),
        3,
    )
    diag_one, cross_block, diag_two = small_kernel(
        diagonal_kernel, 3, 3, tile, (part.reshape(shape), link_block, inverse_one, inverse_two)
    )
    return (column_one[None], column_two[None], diag_one, cross_block, diag_two)


def solution(mesh):
    in_specs = (
        P("row", "col", None, None),
        P("row", "col"),
        P(),
        P(),
        P("row", None, None),
        P("row", None, None),
        P(),
        P(),
        P(),
    )
    out_specs = (P(("row", "col"), None, None), P(("row", "col"), None, None), P(), P(), P())
    return jax.shard_map(shards, mesh=mesh, in_specs=in_specs, out_specs=out_specs, check_vma=False)
```

profile of v0, /device:TPU:0, one launch (start us, length us, event | category | flops | bytes accessed | tf_op | source)
XLA Modules:
  0.0 79.7 jit_solution(16795685520266346511)
XLA Ops:
  0.7 1.2 %constant_dynamic-slice_fusion.3 = bf16[4,256,256]{2,1,0:T(8,128)(2,1)S(1)} fusion(bf16[8,256,256]{2,1,0:T(8,128)(2,1)} %param.13, s32[]{:T(128)S(6)} %select_n.152), kind=kLoop, calls=%fused_computation.65 | loop fusion | bytes 1048580 | tf_op jit(solution)/shard_map/dynamic_slice | solution.py:102
  1.8 4.9 %collective-permute-start = (bf16[4,256,256]{2,1,0:T(8,128)(2,1)S(1)}, bf16[4,256,256]{2,1,0:T(8,128)(2,1)S(1)}, u32[]{:S(2)}, u32[]{:S(2)}) collective-permute-start(bf16[4,256,256]{2,1,0:T(8,128)(2,1)S(1)} %constant_dynamic-slice_fusion.3), channel_id=1, source_target_pairs={{0,16},{1,17},{10,26},{11,27},{20,4},{21,5},{30,14},{31,15}} | collective-permute-start | bytes 1572872 | tf_op jit(solution)/shard_map/ppermute | solution.py:76
  6.7 1.1 %constant_dynamic-slice_fusion.1 = bf16[4,256,256]{2,1,0:T(8,128)(2,1)S(1)} fusion(bf16[8,256,256]{2,1,0:T(8,128)(2,1)} %param.14, s32[]{:T(128)S(6)} %select_n.152), kind=kLoop, calls=%fused_computation.63 | loop fusion | bytes 1048580 | tf_op jit(solution)/shard_map/dynamic_slice | solution.py:102
  7.8 1.3 %collective-permute-start.5 = (bf16[4,256,256]{2,1,0:T(8,128)(2,1)S(1)}, bf16[4,256,256]{2,1,0:T(8,128)(2,1)S(1)}, u32[]{:S(2)}, u32[]{:S(2)}) collective-permute-start(bf16[4,256,256]{2,1,0:T(8,128)(2,1)S(1)} %constant_dynamic-slice_fusion.1), channel_id=1, source_target_pairs={{0,16},{1,17},{10,26},{11,27},{20,4},{21,5},{30,14},{31,15}} | collective-permute-start | bytes 1572872 | tf_op jit(solution)/shard_map/ppermute | solution.py:76
  10.7 0.8 broadcast_compare_fusion
  11.4 2.0 %collective-permute-done = bf16[4,256,256]{2,1,0:T(8,128)(2,1)S(1)} collective-permute-done((bf16[4,256,256]{2,1,0:T(8,128)(2,1)S(1)}, bf16[4,256,256]{2,1,0:T(8,128)(2,1)S(1)}, u32[]{:S(2)}, u32[]{:S(2)}) %collective-permute-start) | collective-permute-done | bytes 524320 | tf_op jit(solution)/shard_map/ppermute | solution.py:76
  13.4 1.1 %broadcast_select_fusion.2 = bf16[4,256,256]{2,1,0:T(8,128)(2,1)S(1)} fusion(bf16[4,256,256]{2,1,0:T(8,128)(2,1)S(1)} %collective-permute-done, pred[]{:T(512)S(6)} %eq.22, bf16[8,256,256]{2,1,0:T(8,128)(2,1)} %param.13, s32[]{:T(128)S(6)} %select_n.152), kind=kLoop, calls=%fused_computation.36 | loop fusion | flops 262144 | bytes 1572869 | tf_op jit(solution)/shard_map/jit(_where)/select_n | solution.py:77
  14.5 1.3 %collective-permute-start.1 = (bf16[4,256,256]{2,1,0:T(8,128)(2,1)S(1)}, bf16[4,256,256]{2,1,0:T(8,128)(2,1)S(1)}, u32[]{:S(2)}, u32[]{:S(2)}) collective-permute-start(bf16[4,256,256]{2,1,0:T(8,128)(2,1)S(1)} %broadcast_select_fusion.2), channel_id=1, source_target_pairs={{0,8},{1,9},{10,2},{11,3},{4,12},{5,13},{14,6},{15,7},{16,24},{17,... | collective-permute-start | bytes 1572872 | tf_op jit(solution)/shard_map/ppermute | solution.py:86
  16.8 2.2 %collective-permute-done.5 = bf16[4,256,256]{2,1,0:T(8,128)(2,1)S(1)} collective-permute-done((bf16[4,256,256]{2,1,0:T(8,128)(2,1)S(1)}, bf16[4,256,256]{2,1,0:T(8,128)(2,1)S(1)}, u32[]{:S(2)}, u32[]{:S(2)}) %collective-permute-start.5) | collective-permute-done | bytes 524320 | tf_op jit(solution)/shard_map/ppermute | solution.py:76
  19.1 3.6 %bitcast_convert_fusion.1 = bf16[8,256,256]{2,1,0:T(8,128)(2,1)S(1)} fusion(bf16[8,4,256,256]{3,2,1,0:T(8,128)(2,1)} %param.9, pred[8,4]{1,0:T(8,128)(4,1)S(1)} %copy.19, bf16[4,256,256]{2,1,0:T(8,128)(2,1)S(1)} %broadcast_select_fusion.2, bf16[4,256,256]{2,1,0:T(8,128)(2,1)S(1)} %collective-permute-done.1, pred[]{:T(512)S(6)} %eq.21), kind=kOutput, calls=%fused_computation.7 | convolution fusion | flops 1076625408 | bytes 6291489 | tf_op jit(solution)/shard_map/ijab,jbc->iac/dot_general | solution.py:109
  23.4 1.6 %collective-permute-start.6 = (bf16[4,256,256]{2,1,0:T(8,128)(2,1)S(1)}, bf16[4,256,256]{2,1,0:T(8,128)(2,1)S(1)}, u32[]{:S(2)}, u32[]{:S(2)}) collective-permute-start(bf16[4,256,256]{2,1,0:T(8,128)(2,1)S(1)} %broadcast_select_fusion.1), channel_id=1, source_target_pairs={{0,8},{1,9},{10,2},{11,3},{4,12},{5,13},{14,6},{15,7},{16,24},{17,... | collective-permute-start | bytes 1572872 | tf_op jit(solution)/shard_map/ppermute | solution.py:86
  25.0 1.6 %collective-permute-start.2 = (bf16[4,256,256]{2,1,0:T(8,128)(2,1)S(1)}, bf16[4,256,256]{2,1,0:T(8,128)(2,1)S(1)}, u32[]{:S(2)}, u32[]{:S(2)}) collective-permute-start(bf16[4,256,256]{2,1,0:T(8,128)(2,1)S(1)} %get-tuple-element.35), channel_id=1, source_target_pairs={{0,1},{1,0},{2,3},{3,2},{4,5},{5,4},{6,7},{7,6},{8,9},{9,8},{10,11... | collective-permute-start | bytes 1572872 | tf_op jit(solution)/shard_map/ppermute | solution.py:89
  27.3 1.3 %bitcast_convert_fusion = bf16[8,256,256]{2,1,0:T(8,128)(2,1)S(1)} fusion(bf16[8,4,256,256]{3,2,1,0:T(8,128)(2,1)S(1)} %copy-done.4, pred[8,4]{1,0:T(8,128)(4,1)S(1)} %copy.23, bf16[4,256,256]{2,1,0:T(8,128)(2,1)S(1)} %broadcast_select_fusion.1, bf16[4,256,256]{2,1,0:T(8,128)(2,1)S(1)} %collective-permute-done.6, pred[]{:T(512)S(6)} %eq.21), kind=kOutput, calls=%fused_computation.6 | convolution fusion | flops 1076625408 | bytes 6291489 | tf_op jit(solution)/shard_map/ijab,jbc->iac/dot_general | solution.py:109
  29.5 1.1 %collective-permute-start.7 = (bf16[4,256,256]{2,1,0:T(8,128)(2,1)S(1)}, bf16[4,256,256]{2,1,0:T(8,128)(2,1)S(1)}, u32[]{:S(2)}, u32[]{:S(2)}) collective-permute-start(bf16[4,256,256]{2,1,0:T(8,128)(2,1)S(1)} %get-tuple-element.33), channel_id=1, source_target_pairs={{0,1},{1,0},{2,3},{3,2},{4,5},{5,4},{6,7},{7,6},{8,9},{9,8},{10,11... | collective-permute-start | bytes 1572872 | tf_op jit(solution)/shard_map/ppermute | solution.py:89
  30.6 9.3 %collective-permute-done.2 = bf16[4,256,256]{2,1,0:T(8,128)(2,1)S(1)} collective-permute-done((bf16[4,256,256]{2,1,0:T(8,128)(2,1)S(1)}, bf16[4,256,256]{2,1,0:T(8,128)(2,1)S(1)}, u32[]{:S(2)}, u32[]{:S(2)}) %collective-permute-start.2) | collective-permute-done | bytes 524320 | tf_op jit(solution)/shard_map/ppermute | solution.py:89
  40.3 2.5 %collective-permute-start.11 = (bf16[192,256]{1,0:T(8,128)(2,1)S(1)}, bf16[192,256]{1,0:T(8,128)(2,1)S(1)}, u32[]{:S(2)}, u32[]{:S(2)}) collective-permute-start(bf16[192,256]{1,0:T(8,128)(2,1)S(1)} %dynamic-slice_convert_fusion.1), channel_id=1, source_target_pairs={{0,16},{1,17},{2,18},{3,19},{4,20},{5,21},{6,22},{7,23},{8,24},{9,... | collective-permute-start | bytes 294920 | tf_op jit(solution)/shard_map/ppermute | solution.py:92
  42.9 2.5 %collective-permute-done.11 = bf16[192,256]{1,0:T(8,128)(2,1)S(1)} collective-permute-done((bf16[192,256]{1,0:T(8,128)(2,1)S(1)}, bf16[192,256]{1,0:T(8,128)(2,1)S(1)}, u32[]{:S(2)}, u32[]{:S(2)}) %collective-permute-start.11) | collective-permute-done | bytes 98336 | tf_op jit(solution)/shard_map/ppermute | solution.py:92
  45.5 2.1 %collective-permute-start.12 = (bf16[192,256]{1,0:T(8,128)(2,1)S(1)}, bf16[192,256]{1,0:T(8,128)(2,1)S(1)}, u32[]{:S(2)}, u32[]{:S(2)}) collective-permute-start(bf16[192,256]{1,0:T(8,128)(2,1)S(1)} %add_convert_fusion.3), channel_id=1, source_target_pairs={{0,2},{1,3},{2,0},{3,1},{4,6},{5,7},{6,4},{7,5},{8,10},{9,11},{10,... | collective-permute-start | bytes 294920 | tf_op jit(solution)/shard_map/ppermute | solution.py:89
  47.5 0.8 fusion.30
  48.3 3.1 %collective-permute-start.4 = (bf16[1,256,256]{2,1,0:T(8,128)(2,1)S(1)}, bf16[1,256,256]{2,1,0:T(8,128)(2,1)S(1)}, u32[]{:S(2)}, u32[]{:S(2)}) collective-permute-start(bf16[1,256,256]{2,1,0:T(8,128)(2,1)S(1)} %get-tuple-element.39), channel_id=1, source_target_pairs={{0,4},{1,5},{2,6},{3,7},{4,0},{5,1},{6,2},{7,3},{8,12},{9,13},{10,... | collective-permute-start | bytes 393224 | tf_op jit(solution)/shard_map/ppermute | solution.py:89
  51.4 3.1 %collective-permute-start.13 = (bf16[192,256]{1,0:T(8,128)(2,1)S(1)}, bf16[192,256]{1,0:T(8,128)(2,1)S(1)}, u32[]{:S(2)}, u32[]{:S(2)}) collective-permute-start(bf16[192,256]{1,0:T(8,128)(2,1)S(1)} %add_convert_fusion.2), channel_id=1, source_target_pairs={{0,4},{1,5},{2,6},{3,7},{4,0},{5,1},{6,2},{7,3},{8,12},{9,13},{10,... | collective-permute-start | bytes 294920 | tf_op jit(solution)/shard_map/ppermute | solution.py:89
  54.6 2.7 %collective-permute-start.8 = (bf16[2,256,256]{2,1,0:T(8,128)(2,1)S(1)}, bf16[2,256,256]{2,1,0:T(8,128)(2,1)S(1)}, u32[]{:S(2)}, u32[]{:S(2)}) collective-permute-start(bf16[2,256,256]{2,1,0:T(8,128)(2,1)S(1)} %fusion.27), channel_id=1, source_target_pairs={{0,2},{1,3},{2,0},{3,1},{4,6},{5,7},{6,4},{7,5},{8,10},{9,11},{10,... | collective-permute-start | bytes 786440 | tf_op jit(solution)/shard_map/ppermute | solution.py:89
  57.3 1.3 %collective-permute-done.13 = bf16[192,256]{1,0:T(8,128)(2,1)S(1)} collective-permute-done((bf16[192,256]{1,0:T(8,128)(2,1)S(1)}, bf16[192,256]{1,0:T(8,128)(2,1)S(1)}, u32[]{:S(2)}, u32[]{:S(2)}) %collective-permute-start.13) | collective-permute-done | bytes 98336 | tf_op jit(solution)/shard_map/ppermute | solution.py:89
  58.6 1.5 %collective-permute-start.14 = (bf16[192,256]{1,0:T(8,128)(2,1)S(1)}, bf16[192,256]{1,0:T(8,128)(2,1)S(1)}, u32[]{:S(2)}, u32[]{:S(2)}) collective-permute-start(bf16[192,256]{1,0:T(8,128)(2,1)S(1)} %add_convert_fusion.1), channel_id=1, source_target_pairs={{0,1},{1,0},{2,3},{3,2},{4,5},{5,4},{6,7},{7,6},{8,9},{9,8},{10,11... | collective-permute-start | bytes 294920 | tf_op jit(solution)/shard_map/ppermute | solution.py:89
  60.2 3.1 %collective-permute-done.14 = bf16[192,256]{1,0:T(8,128)(2,1)S(1)} collective-permute-done((bf16[192,256]{1,0:T(8,128)(2,1)S(1)}, bf16[192,256]{1,0:T(8,128)(2,1)S(1)}, u32[]{:S(2)}, u32[]{:S(2)}) %collective-permute-start.14) | collective-permute-done | bytes 98336 | tf_op jit(solution)/shard_map/ppermute | solution.py:89
  63.3 2.6 %collective-permute-start.15 = (bf16[192,256]{1,0:T(8,128)(2,1)S(1)}, bf16[192,256]{1,0:T(8,128)(2,1)S(1)}, u32[]{:S(2)}, u32[]{:S(2)}) collective-permute-start(bf16[192,256]{1,0:T(8,128)(2,1)S(1)} %add_convert_fusion), channel_id=1, source_target_pairs={{0,16},{1,17},{2,18},{3,19},{4,20},{5,21},{6,22},{7,23},{8,24},{9,... | collective-permute-start | bytes 294920 | tf_op jit(solution)/shard_map/ppermute | solution.py:92
  65.9 0.8 fusion.28
  66.8 1.8 %collective-permute-done.15 = bf16[192,256]{1,0:T(8,128)(2,1)S(1)} collective-permute-done((bf16[192,256]{1,0:T(8,128)(2,1)S(1)}, bf16[192,256]{1,0:T(8,128)(2,1)S(1)}, u32[]{:S(2)}, u32[]{:S(2)}) %collective-permute-start.15) | collective-permute-done | bytes 98336 | tf_op jit(solution)/shard_map/ppermute | solution.py:92
  68.6 5.4 %collective-permute-done.9 = bf16[1,256,256]{2,1,0:T(8,128)(2,1)S(1)} collective-permute-done((bf16[1,256,256]{2,1,0:T(8,128)(2,1)S(1)}, bf16[1,256,256]{2,1,0:T(8,128)(2,1)S(1)}, u32[]{:S(2)}, u32[]{:S(2)}) %collective-permute-start.9) | collective-permute-done | bytes 131104 | tf_op jit(solution)/shard_map/ppermute | solution.py:89
  74.6 2.0 %shard_map.128 = (bf16[256,256]{1,0:T(8,128)(2,1)}, bf16[256,256]{1,0:T(8,128)(2,1)}) custom-call(s32[32]{0:T(128)} %first.1, s32[32]{0:T(128)} %second.1, s32[1]{0:T(128)} %bitcast.place, bf16[256,256]{1,0:T(8,128)(2,1)} %link.3, f32[256,256]{1,0:T(8,128)} %get-tuple-element.40.keep_one, bf16[256,256]{1,0:T(8,128)(2,1)} %bitcast.102, ...), custom_call_target="tpu_custom_call" | custom-call | flops 33554432 | bytes 2097152 | tf_op jit(solution)/shard_map/pallas_call | solution.py:35
  76.7 0.8 pad_maximum_fusion.1
  77.5 2.3 %shard_map.129 = (bf16[256,256]{1,0:T(8,128)(2,1)}, bf16[256,256]{1,0:T(8,128)(2,1)}, bf16[256,256]{1,0:T(8,128)(2,1)}) custom-call(bf16[3,256,256]{2,1,0:T(8,128)(2,1)} %bitcast.95, bf16[256,256]{1,0:T(8,128)(2,1)} %link.3, f32[256,256]{1,0:T(8,128)} %inverse_one.1, f32[256,256]{1,0:T(8,128)} %inverse_two.1), custom_call_target="tpu_custom_call" | custom-call | flops 100663296 | bytes 1048576 | tf_op jit(solution)/shard_map/pallas_call | solution.py:35
  (51 shorter events, 6.1 us)
Async XLA Ops:
  0.6 18.4 %copy-start.1 = (bf16[8,256,256]{2,1,0:T(8,128)(2,1)S(1)}, bf16[8,256,256]{2,1,0:T(8,128)(2,1)}, u32[]{:S(2)}) copy-start(bf16[8,256,256]{2,1,0:T(8,128)(2,1)} %param.14) | copy-start | bytes 3145732
  1.8 11.6 %collective-permute-start = (bf16[4,256,256]{2,1,0:T(8,128)(2,1)S(1)}, bf16[4,256,256]{2,1,0:T(8,128)(2,1)S(1)}, u32[]{:S(2)}, u32[]{:S(2)}) collective-permute-start(bf16[4,256,256]{2,1,0:T(8,128)(2,1)S(1)} %constant_dynamic-slice_fusion.3), channel_id=1, source_target_pairs={{0,16},{1,17},{10,26},{11,27},{20,4},{21,5},{30,14},{31,15}} | collective-permute-start | bytes 1572872 | tf_op jit(solution)/shard_map/ppermute | solution.py:76
  7.8 11.2 %collective-permute-start.5 = (bf16[4,256,256]{2,1,0:T(8,128)(2,1)S(1)}, bf16[4,256,256]{2,1,0:T(8,128)(2,1)S(1)}, u32[]{:S(2)}, u32[]{:S(2)}) collective-permute-start(bf16[4,256,256]{2,1,0:T(8,128)(2,1)S(1)} %constant_dynamic-slice_fusion.1), channel_id=1, source_target_pairs={{0,16},{1,17},{10,26},{11,27},{20,4},{21,5},{30,14},{31,15}} | collective-permute-start | bytes 1572872 | tf_op jit(solution)/shard_map/ppermute | solution.py:76
  14.5 4.6 %collective-permute-start.1 = (bf16[4,256,256]{2,1,0:T(8,128)(2,1)S(1)}, bf16[4,256,256]{2,1,0:T(8,128)(2,1)S(1)}, u32[]{:S(2)}, u32[]{:S(2)}) collective-permute-start(bf16[4,256,256]{2,1,0:T(8,128)(2,1)S(1)} %broadcast_select_fusion.2), channel_id=1, source_target_pairs={{0,8},{1,9},{10,2},{11,3},{4,12},{5,13},{14,6},{15,7},{16,24},{17,... | collective-permute-start | bytes 1572872 | tf_op jit(solution)/shard_map/ppermute | solution.py:86
  19.1 3.6 %copy-start = (bf16[8,256,256]{2,1,0:T(8,128)(2,1)S(1)}, bf16[8,256,256]{2,1,0:T(8,128)(2,1)}, u32[]{:S(2)}) copy-start(bf16[8,256,256]{2,1,0:T(8,128)(2,1)} %param.13) | copy-start | bytes 3145732
  23.4 3.9 %copy-start.4 = (bf16[8,4,256,256]{3,2,1,0:T(8,128)(2,1)S(1)}, bf16[8,4,256,256]{3,2,1,0:T(8,128)(2,1)}, u32[]{:S(2)}) copy-start(bf16[8,4,256,256]{3,2,1,0:T(8,128)(2,1)} %param.9) | copy-start | bytes 12582916
  23.4 3.9 %collective-permute-start.6 = (bf16[4,256,256]{2,1,0:T(8,128)(2,1)S(1)}, bf16[4,256,256]{2,1,0:T(8,128)(2,1)S(1)}, u32[]{:S(2)}, u32[]{:S(2)}) collective-permute-start(bf16[4,256,256]{2,1,0:T(8,128)(2,1)S(1)} %broadcast_select_fusion.1), channel_id=1, source_target_pairs={{0,8},{1,9},{10,2},{11,3},{4,12},{5,13},{14,6},{15,7},{16,24},{17,... | collective-permute-start | bytes 1572872 | tf_op jit(solution)/shard_map/ppermute | solution.py:86
  25.0 14.9 %collective-permute-start.2 = (bf16[4,256,256]{2,1,0:T(8,128)(2,1)S(1)}, bf16[4,256,256]{2,1,0:T(8,128)(2,1)S(1)}, u32[]{:S(2)}, u32[]{:S(2)}) collective-permute-start(bf16[4,256,256]{2,1,0:T(8,128)(2,1)S(1)} %get-tuple-element.35), channel_id=1, source_target_pairs={{0,1},{1,0},{2,3},{3,2},{4,5},{5,4},{6,7},{7,6},{8,9},{9,8},{10,11... | collective-permute-start | bytes 1572872 | tf_op jit(solution)/shard_map/ppermute | solution.py:89
  29.4 10.8 %collective-permute-start.10 = (bf16[384,256]{1,0:T(8,128)(2,1)S(1)}, bf16[384,256]{1,0:T(8,128)(2,1)S(1)}, u32[]{:S(2)}, u32[]{:S(2)}) collective-permute-start(bf16[384,256]{1,0:T(8,128)(2,1)S(1)} %dynamic-slice_convert_fusion), channel_id=1, source_target_pairs={{0,8},{1,9},{2,10},{3,11},{4,12},{5,13},{6,14},{7,15},{8,0},{9,1},... | collective-permute-start | bytes 589832 | tf_op jit(solution)/shard_map/ppermute | solution.py:92
  29.5 21.9 %collective-permute-start.7 = (bf16[4,256,256]{2,1,0:T(8,128)(2,1)S(1)}, bf16[4,256,256]{2,1,0:T(8,128)(2,1)S(1)}, u32[]{:S(2)}, u32[]{:S(2)}) collective-permute-start(bf16[4,256,256]{2,1,0:T(8,128)(2,1)S(1)} %get-tuple-element.33), channel_id=1, source_target_pairs={{0,1},{1,0},{2,3},{3,2},{4,5},{5,4},{6,7},{7,6},{8,9},{9,8},{10,11... | collective-permute-start | bytes 1572872 | tf_op jit(solution)/shard_map/ppermute | solution.py:89
  40.0 7.5 %collective-permute-start.3 = (bf16[2,256,256]{2,1,0:T(8,128)(2,1)S(1)}, bf16[2,256,256]{2,1,0:T(8,128)(2,1)S(1)}, u32[]{:S(2)}, u32[]{:S(2)}) collective-permute-start(bf16[2,256,256]{2,1,0:T(8,128)(2,1)S(1)} %fusion.26), channel_id=1, source_target_pairs={{0,2},{1,3},{2,0},{3,1},{4,6},{5,7},{6,4},{7,5},{8,10},{9,11},{10,... | collective-permute-start | bytes 786440 | tf_op jit(solution)/shard_map/ppermute | solution.py:89
  40.3 5.1 %collective-permute-start.11 = (bf16[192,256]{1,0:T(8,128)(2,1)S(1)}, bf16[192,256]{1,0:T(8,128)(2,1)S(1)}, u32[]{:S(2)}, u32[]{:S(2)}) collective-permute-start(bf16[192,256]{1,0:T(8,128)(2,1)S(1)} %dynamic-slice_convert_fusion.1), channel_id=1, source_target_pairs={{0,16},{1,17},{2,18},{3,19},{4,20},{5,21},{6,22},{7,23},{8,24},{9,... | collective-permute-start | bytes 294920 | tf_op jit(solution)/shard_map/ppermute | solution.py:92
  45.5 5.9 %collective-permute-start.12 = (bf16[192,256]{1,0:T(8,128)(2,1)S(1)}, bf16[192,256]{1,0:T(8,128)(2,1)S(1)}, u32[]{:S(2)}, u32[]{:S(2)}) collective-permute-start(bf16[192,256]{1,0:T(8,128)(2,1)S(1)} %add_convert_fusion.3), channel_id=1, source_target_pairs={{0,2},{1,3},{2,0},{3,1},{4,6},{5,7},{6,4},{7,5},{8,10},{9,11},{10,... | collective-permute-start | bytes 294920 | tf_op jit(solution)/shard_map/ppermute | solution.py:89
  48.3 20.2 %collective-permute-start.4 = (bf16[1,256,256]{2,1,0:T(8,128)(2,1)S(1)}, bf16[1,256,256]{2,1,0:T(8,128)(2,1)S(1)}, u32[]{:S(2)}, u32[]{:S(2)}) collective-permute-start(bf16[1,256,256]{2,1,0:T(8,128)(2,1)S(1)} %get-tuple-element.39), channel_id=1, source_target_pairs={{0,4},{1,5},{2,6},{3,7},{4,0},{5,1},{6,2},{7,3},{8,12},{9,13},{10,... | collective-permute-start | bytes 393224 | tf_op jit(solution)/shard_map/ppermute | solution.py:89
  51.4 7.1 %collective-permute-start.13 = (bf16[192,256]{1,0:T(8,128)(2,1)S(1)}, bf16[192,256]{1,0:T(8,128)(2,1)S(1)}, u32[]{:S(2)}, u32[]{:S(2)}) collective-permute-start(bf16[192,256]{1,0:T(8,128)(2,1)S(1)} %add_convert_fusion.2), channel_id=1, source_target_pairs={{0,4},{1,5},{2,6},{3,7},{4,0},{5,1},{6,2},{7,3},{8,12},{9,13},{10,... | collective-permute-start | bytes 294920 | tf_op jit(solution)/shard_map/ppermute | solution.py:89
  54.6 8.8 %collective-permute-start.8 = (bf16[2,256,256]{2,1,0:T(8,128)(2,1)S(1)}, bf16[2,256,256]{2,1,0:T(8,128)(2,1)S(1)}, u32[]{:S(2)}, u32[]{:S(2)}) collective-permute-start(bf16[2,256,256]{2,1,0:T(8,128)(2,1)S(1)} %fusion.27), channel_id=1, source_target_pairs={{0,2},{1,3},{2,0},{3,1},{4,6},{5,7},{6,4},{7,5},{8,10},{9,11},{10,... | collective-permute-start | bytes 786440 | tf_op jit(solution)/shard_map/ppermute | solution.py:89
  58.6 4.7 %collective-permute-start.14 = (bf16[192,256]{1,0:T(8,128)(2,1)S(1)}, bf16[192,256]{1,0:T(8,128)(2,1)S(1)}, u32[]{:S(2)}, u32[]{:S(2)}) collective-permute-start(bf16[192,256]{1,0:T(8,128)(2,1)S(1)} %add_convert_fusion.1), channel_id=1, source_target_pairs={{0,1},{1,0},{2,3},{3,2},{4,5},{5,4},{6,7},{7,6},{8,9},{9,8},{10,11... | collective-permute-start | bytes 294920 | tf_op jit(solution)/shard_map/ppermute | solution.py:89
  63.3 5.2 %collective-permute-start.15 = (bf16[192,256]{1,0:T(8,128)(2,1)S(1)}, bf16[192,256]{1,0:T(8,128)(2,1)S(1)}, u32[]{:S(2)}, u32[]{:S(2)}) collective-permute-start(bf16[192,256]{1,0:T(8,128)(2,1)S(1)} %add_convert_fusion), channel_id=1, source_target_pairs={{0,16},{1,17},{2,18},{3,19},{4,20},{5,21},{6,22},{7,23},{8,24},{9,... | collective-permute-start | bytes 294920 | tf_op jit(solution)/shard_map/ppermute | solution.py:92
  66.7 7.3 %collective-permute-start.9 = (bf16[1,256,256]{2,1,0:T(8,128)(2,1)S(1)}, bf16[1,256,256]{2,1,0:T(8,128)(2,1)S(1)}, u32[]{:S(2)}, u32[]{:S(2)}) collective-permute-start(bf16[1,256,256]{2,1,0:T(8,128)(2,1)S(1)} %get-tuple-element.37), channel_id=1, source_target_pairs={{0,4},{1,5},{2,6},{3,7},{4,0},{5,1},{6,2},{7,3},{8,12},{9,13},{10,... | collective-permute-start | bytes 393224 | tf_op jit(solution)/shard_map/ppermute | solution.py:89
  68.6 5.4 %copy-start.2 = (bf16[1,256,256]{2,1,0:T(8,128)(2,1)}, bf16[1,256,256]{2,1,0:T(8,128)(2,1)S(1)}, u32[]{:S(2)}) copy-start(bf16[1,256,256]{2,1,0:T(8,128)(2,1)S(1)} %collective-permute-done.4) | copy-start | bytes 393220
  74.0 0.7 copy-start.3
  74.0 2.7 %collective-permute-start.16 = (bf16[384,256]{1,0:T(8,128)(2,1)S(1)}, bf16[384,256]{1,0:T(8,128)(2,1)S(1)}, u32[]{:S(2)}, u32[]{:S(2)}) collective-permute-start(bf16[384,256]{1,0:T(8,128)(2,1)S(1)} %pad_maximum_fusion.2), channel_id=1, source_target_pairs={{0,8},{1,9},{2,10},{3,11},{4,12},{5,13},{6,14},{7,15},{8,0},{9,1},... | collective-permute-start | bytes 589832 | tf_op jit(solution)/shard_map/ppermute | solution.py:92
where the time goes:
time: 80.1 us; the launch traced here: 79.7 us
  starting transfers between devices  29.6 us (37%)
  waiting for transfers between devices  27.6 us (34%)
  matrix products  6.78 us (8%)
  other arithmetic  5.71 us (7%)
  local copies, waits for them, and re-layouts  4.78 us (6%)
  Pallas kernels  4.27 us (5%)
  between operations  1.06 us (1%)
    ppermute x9, waiting for transfers between devices, swap(): lax.ppermute(array, BOTH, [(at(r, c), at(r, c ^ 1 << bit)) for r, c in ev...  19.1 us
    ppermute x9, starting transfers between devices, swap(): lax.ppermute(array, BOTH, [(at(r, c), at(r, c ^ 1 << bit)) for r, c in ev...  15.2 us
    ppermute x2, starting transfers between devices, over_chips(): got = after(lax.ppermute(piece, BOTH, perm), *earlier)  6.23 us
    ppermute x4, starting transfers between devices, swap_rows(): lax.ppermute(array, BOTH, [(at(r, c), at(r ^ 1 << bit, c)) for r, c in ev...  5.2 us
    dot_general x2, matrix products, products(): jnp.einsum('ijab,jbc->iac', kept, column, preferred_element_type=F32)  4.9 us
    ppermute x4, waiting for transfers between devices, swap_rows(): lax.ppermute(array, BOTH, [(at(r, c), at(r ^ 1 << bit, c)) for r, c in ev...  4.3 us
    pallas_call x2, Pallas kernels, small_kernel(): pl.pallas_call(body, out_shape=(jax.ShapeDtypeStruct((tile, tile), BF16),...  4.27 us
    ppermute x2, waiting for transfers between devices, over_chips(): got = after(lax.ppermute(piece, BOTH, perm), *earlier)  4.15 us
  transfers between devices with their start and end apart: 17, of which 8 were waited for; matrix products, arithmetic and copies ran while one was open for 13% of the time, Pallas kernels for 3%

commit v1 on v0

--- a/solution.py
+++ b/solution.py
@@ -11,15 +11,6 @@
 
 def transposed_dot(a, b):
     return lax.dot_general(a, b, (((0,), (0,)), ((), ())), preferred_element_type=F32)
-
-
-def column_kernel(first, second, place, link, keep_one, got_one, keep_two, got_two, column_one, column_two):
-    member_one, member_two = (m[place[0]].astype(F32) for m in (first, second))
-    one = keep_one[...].astype(F32) + got_one[...].astype(F32)
-    column_one[...] = (-member_one * one).astype(BF16)
-    two = keep_two[...].astype(F32) + got_two[...].astype(F32)
-    two += jnp.dot(column_one[...], link[...], preferred_element_type=F32)
-    column_two[...] = (-member_two * two).astype(BF16)
 
 
 def diagonal_kernel(sums, link, inverse_one, inverse_two, diag_one, cross, diag_two):
@@ -91,12 +82,25 @@
     def swap_rows(array, bit):
         return lax.ppermute(array, BOTH, [(at(r, c), at(r ^ (1 << bit), c)) for r, c in everyone])
 
-    def pick(array, bit, other):
-        split = array.reshape(array.shape[0] // 2, 2, *array.shape[1:])
-        return lax.dynamic_slice_in_dim(split, (col >> bit & 1) ^ other, 1, 1)[:, 0].astype(F32)
+    def pick(array, bits_left, bit, other):
+        lower = 1 << bits_left.index(bit)
+        split = array.reshape(-1, 2, lower, tile, tile)
+        return lax.dynamic_slice_in_dim(split, (col >> bit & 1) ^ other, 1, 1).reshape(-1, tile, tile).astype(F32)
 
-    def merged(keep, got, bit, other):
-        return pick(keep, bit, other) + pick(got, bit, other)
+    def first_swap(array, order):
+        left = list(range(bits))
+        away, keep = (pick(array, left, order[0], other) for other in (1, 0))
+        left.remove(order[0])
+        return left, keep, [swap(away.astype(BF16), order[0])]
+
+    def next_swap(left, keep, arrived, order):
+        bit = order[len(arrived)]
+        away, keep = (
+            pick(keep, left, bit, other) + pick(arrived[-1], left, bit, other) for other in (1, 0)
+        )
+        left.remove(bit)
+        arrived.append(swap(away.astype(BF16), bit))
+        return keep
 
     def part_of(array, start, size):
         return lax.dynamic_slice_in_dim(array, start, size, 0)
@@ -117,58 +121,42 @@
     second_in_one = masked(flags_one, second)
 
     piece_one, piece_two = (part_of(f, col % group * cols, cols) for f in (factor_one, factor_two))
+    piece_one, piece_two = after(piece_one), after(piece_two)
+    order_one, order_two = list(range(bits)), [1, 0, *range(2, bits)]
     have_one, have_two = over_chips(piece_one, *marks), over_chips(piece_two)
-    keep_one = products(marks[0], over_cores(have_one))
-    one = [swap(pick(keep_one, 0, 1).astype(BF16), 0)]
-    sums_one = contraction(first, keep_one), contraction(keep_one, second_in_one)
-    keep_two = products(marks[1], over_cores(after(have_two, keep_one)))
-    two = [swap(pick(keep_two, 0, 1).astype(BF16), 0)]
-    sums_two = contraction(second, keep_two)
-    keep_one, keep_two = pick(keep_one, 0, 0), pick(keep_two, 0, 0)
+    all_one = products(marks[0], over_cores(have_one))
+    left_one, keep_one, one = first_swap(all_one, order_one)
+    column = over_cores(after(have_two, all_one))
+    all_two = products(marks[1], column)
+    left_two, keep_two, two = first_swap(all_two, order_two)
+    all_one = after(all_one, all_two)
+    sums = contraction(first, all_one), contraction(all_one, second_in_one), contraction(second, all_two)
+    for _ in range(1, bits):
+        keep_one = next_swap(left_one, keep_one, one, order_one)
+        keep_two = next_swap(left_two, keep_two, two, order_two)
 
-    for bit in range(1, bits):
-        away = merged(keep_one, one[-1], bit, 1).astype(BF16)
-        keep_one = merged(keep_one, one[-1], bit, 0)
-        one.append(swap(away, bit))
-        away = merged(keep_two, two[-1], bit, 1).astype(BF16)
-        keep_two = merged(keep_two, two[-1], bit, 0)
-        two.append(swap(away, bit))
-
-    sums = jnp.stack([*sums_one, sums_two])
+    sums = jnp.stack(sums)
     shape = sums.shape
     part = sums.reshape(-1, tile)
     for bit in range(row_bits):
         half = part.shape[0] // 2
         mine = row >> bit & 1
-        if bit == row_bits - 1:
-            part = after(part, one[0])
         got = swap_rows(lax.dynamic_slice_in_dim(part, (1 - mine) * half, half, 0).astype(BF16), bit)
         part = lax.dynamic_slice_in_dim(part, mine * half, half, 0) + got.astype(F32)
     part = part.astype(BF16)
-    for bit in (*range(1, bits), 0):
-        if bit != 1:
-            part = after(part, one[1] if bit == 0 else two[0])
-        got = swap(part, bit)
+    gates = [one[0], two[0], *one[1:]]
+    for bit in range(bits):
+        got = swap(after(part, gates[bit]), bit)
         part = (part.astype(F32) + got.astype(F32)).astype(BF16)
     for bit in reversed(range(row_bits)):
-        got = swap_rows(after(part, two[-1], one[-1]) if bit == 0 else after(part, two[-2]), bit)
+        got = swap_rows(after(part, one[-1] if bit == 0 else two[-2]), bit)
         low = (row >> bit & 1) == 0
         part = jnp.concatenate([jnp.where(low, part, got), jnp.where(low, got, part)])
 
-    column_one, column_two = small_kernel(
-        column_kernel,
-        2,
-        1,
-        tile,
-        (
-            member_one,
-            member_two,
-            (row * rows + col)[None],
-            link_block,
-            *(a[0] for a in (keep_one, one[-1], keep_two, two[-1])),
-        ),
-        3,
-    )
+    member_one, member_two = (m[row * rows + col].astype(F32) for m in (member_one, member_two))
+    column_one = (-member_one * (keep_one[0] + one[-1][0].astype(F32))).astype(BF16)
+    linked = jnp.dot(column_one, link_block, preferred_element_type=F32) + keep_two[0]
+    column_two = (-member_two * (linked + two[-1][0].astype(F32))).astype(BF16)
     diag_one, cross_block, diag_two = small_kernel(
         diagonal_kernel, 3, 3, tile, (part.reshape(shape), link_block, inverse_one, inverse_two)
     )

time: 80.1 us -> 81.4 us (1.016)
  waiting for transfers between devices: 27.6 us -> 37.5 us
  starting transfers between devices: 29.6 us -> 21.3 us
  other arithmetic: 5.71 us -> 2.56 us
  matrix products: 6.78 us -> 9.73 us
  Pallas kernels: 4.27 us -> 2.27 us
  between operations: 1.06 us -> 2.41 us
    ppermute x9, starting transfers between devices: 15.2 us -> 8.06 us  [swap(): lax.ppermute(array, BOTH, [(at(r, c), at(r, c ^ 1 << bit)) for r, c in ev...]
    ppermute x9, waiting for transfers between devices: 19.1 us -> 25.5 us  [swap(): lax.ppermute(array, BOTH, [(at(r, c), at(r, c ^ 1 << bit)) for r, c in ev...]
    dot_general x2, matrix products: 4.9 us -> 6.99 us  [products(): jnp.einsum('ijab,jbc->iac', kept, column, preferred_element_type=F32)]
    pallas_call x2 -> x1, Pallas kernels: 4.27 us -> 2.27 us  [small_kernel(): pl.pallas_call(body, out_shape=(jax.ShapeDtypeStruct((tile, tile), BF16),...]
    ppermute x2, waiting for transfers between devices: 4.15 us -> 6.09 us  [over_chips(): got = after(lax.ppermute(piece, BOTH, perm), *earlier)]
    ppermute x4, waiting for transfers between devices: 4.3 us -> 5.89 us  [swap_rows(): lax.ppermute(array, BOTH, [(at(r, c), at(r ^ 1 << bit, c)) for r, c in ev...]
    convert_element_type x6 -> x7, other arithmetic: 1.84 us -> 0.52 us  [the longest x4 0.29 us: next_swap(): arrived.append(swap(away.astype(BF16), bit))]
    dynamic_slice x0 -> x3, local copies, waits for them, and re-layouts: none -> 1.25 us  [the longest x2 1.17 us: shards(): m[row * rows + col].astype(F32)]
  transfers between devices with their start and end apart: 17 -> 17, of which waited for: 8 -> 11; matrix products, arithmetic and copies ran while one was open for 13% -> 15% of each run, Pallas kernels for 3% -> 0%
where the time goes in v1:
time: 81.4 us; the launch traced here: 81 us
  waiting for transfers between devices  37.5 us (46%)
  starting transfers between devices  21.3 us (26%)
  matrix products  9.73 us (12%)
  local copies, waits for them, and re-layouts  5.22 us (6%)
  other arithmetic  2.56 us (3%)
  between operations  2.41 us (3%)
  Pallas kernels  2.27 us (3%)
    ppermute x9, waiting for transfers between devices, swap(): lax.ppermute(array, BOTH, [(at(r, c), at(r, c ^ 1 << bit)) for r, c in ev...  25.5 us
    ppermute x9, starting transfers between devices, swap(): lax.ppermute(array, BOTH, [(at(r, c), at(r, c ^ 1 << bit)) for r, c in ev...  8.06 us
    dot_general x2, matrix products, products(): jnp.einsum('ijab,jbc->iac', kept, column, preferred_element_type=F32)  6.99 us
    ppermute x2, starting transfers between devices, over_chips(): got = after(lax.ppermute(piece, BOTH, perm), *earlier)  6.23 us
    ppermute x2, waiting for transfers between devices, over_chips(): got = after(lax.ppermute(piece, BOTH, perm), *earlier)  6.09 us
    ppermute x4, waiting for transfers between devices, swap_rows(): lax.ppermute(array, BOTH, [(at(r, c), at(r ^ 1 << bit, c)) for r, c in ev...  5.89 us
    ppermute x4, starting transfers between devices, swap_rows(): lax.ppermute(array, BOTH, [(at(r, c), at(r ^ 1 << bit, c)) for r, c in ev...  4.35 us
    dynamic_slice x4, local copies, waits for them, and re-layouts, part_of(): return lax.dynamic_slice_in_dim(array, start, size, 0)  3.62 us
  transfers between devices with their start and end apart: 17, of which 11 were waited for; matrix products, arithmetic and copies ran while one was open for 15% of the time, Pallas kernels for 0%

profile of v1, /device:TPU:0, one launch (start us, length us, event | category | flops | bytes accessed | tf_op | source)
XLA Modules:
  0.0 81.0 jit_solution(2389301696802752298)
XLA Ops:
  0.6 1.1 %constant_dynamic-slice_fusion.4 = bf16[4,256,256]{2,1,0:T(8,128)(2,1)S(1)} fusion(bf16[8,256,256]{2,1,0:T(8,128)(2,1)} %param.13, s32[]{:T(128)S(6)} %select_n.157), kind=kLoop, calls=%fused_computation.71 | loop fusion | bytes 1048580 | tf_op jit(solution)/shard_map/dynamic_slice | solution.py:106
  1.7 4.9 %collective-permute-start = (bf16[4,256,256]{2,1,0:T(8,128)(2,1)S(1)}, bf16[4,256,256]{2,1,0:T(8,128)(2,1)S(1)}, u32[]{:S(2)}, u32[]{:S(2)}) collective-permute-start(bf16[4,256,256]{2,1,0:T(8,128)(2,1)S(1)} %constant_dynamic-slice_fusion.4), channel_id=1, source_target_pairs={{0,16},{1,17},{10,26},{11,27},{20,4},{21,5},{30,14},{31,15}} | collective-permute-start | bytes 1572872 | tf_op jit(solution)/shard_map/ppermute | solution.py:67
  6.6 1.1 %constant_dynamic-slice_fusion.2 = bf16[4,256,256]{2,1,0:T(8,128)(2,1)S(1)} fusion(bf16[8,256,256]{2,1,0:T(8,128)(2,1)} %param.14, s32[]{:T(128)S(6)} %select_n.157), kind=kLoop, calls=%fused_computation.69 | loop fusion | bytes 1048580 | tf_op jit(solution)/shard_map/dynamic_slice | solution.py:106
  7.7 1.3 %collective-permute-start.5 = (bf16[4,256,256]{2,1,0:T(8,128)(2,1)S(1)}, bf16[4,256,256]{2,1,0:T(8,128)(2,1)S(1)}, u32[]{:S(2)}, u32[]{:S(2)}) collective-permute-start(bf16[4,256,256]{2,1,0:T(8,128)(2,1)S(1)} %constant_dynamic-slice_fusion.2), channel_id=1, source_target_pairs={{0,16},{1,17},{10,26},{11,27},{20,4},{21,5},{30,14},{31,15}} | collective-permute-start | bytes 1572872 | tf_op jit(solution)/shard_map/ppermute | solution.py:67
  9.1 0.7 dynamic_slice.105
  9.8 0.7 dynamic_slice.107
  10.6 0.8 broadcast_compare_fusion
  11.3 2.0 %collective-permute-done = bf16[4,256,256]{2,1,0:T(8,128)(2,1)S(1)} collective-permute-done((bf16[4,256,256]{2,1,0:T(8,128)(2,1)S(1)}, bf16[4,256,256]{2,1,0:T(8,128)(2,1)S(1)}, u32[]{:S(2)}, u32[]{:S(2)}) %collective-permute-start) | collective-permute-done | bytes 524320 | tf_op jit(solution)/shard_map/ppermute | solution.py:67
  13.4 1.3 %collective-permute-start.1 = (bf16[4,256,256]{2,1,0:T(8,128)(2,1)S(1)}, bf16[4,256,256]{2,1,0:T(8,128)(2,1)S(1)}, u32[]{:S(2)}, u32[]{:S(2)}) collective-permute-start(bf16[4,256,256]{2,1,0:T(8,128)(2,1)S(1)} %broadcast_select_fusion.2), channel_id=1, source_target_pairs={{0,8},{1,9},{10,2},{11,3},{4,12},{5,13},{14,6},{15,7},{16,24},{17,... | collective-permute-start | bytes 1572872 | tf_op jit(solution)/shard_map/ppermute | solution.py:77
  14.8 4.1 %collective-permute-done.5 = bf16[4,256,256]{2,1,0:T(8,128)(2,1)S(1)} collective-permute-done((bf16[4,256,256]{2,1,0:T(8,128)(2,1)S(1)}, bf16[4,256,256]{2,1,0:T(8,128)(2,1)S(1)}, u32[]{:S(2)}, u32[]{:S(2)}) %collective-permute-start.5) | collective-permute-done | bytes 524320 | tf_op jit(solution)/shard_map/ppermute | solution.py:67
  19.0 3.5 %bitcast_convert_fusion.1 = bf16[8,256,256]{2,1,0:T(8,128)(2,1)S(1)} fusion(bf16[8,4,256,256]{3,2,1,0:T(8,128)(2,1)} %param.9, pred[8,4]{1,0:T(8,128)(4,1)S(1)} %copy.19, bf16[4,256,256]{2,1,0:T(8,128)(2,1)S(1)} %broadcast_select_fusion.2, bf16[4,256,256]{2,1,0:T(8,128)(2,1)S(1)} %collective-permute-done.1, pred[]{:T(512)S(6)} %eq.21), kind=kOutput, calls=%fused_computation.7 | convolution fusion | flops 1076625408 | bytes 6291489 | tf_op jit(solution)/shard_map/ijab,jbc->iac/dot_general | solution.py:113
  22.5 1.3 %collective-permute-start.6 = (bf16[4,256,256]{2,1,0:T(8,128)(2,1)S(1)}, bf16[4,256,256]{2,1,0:T(8,128)(2,1)S(1)}, u32[]{:S(2)}, u32[]{:S(2)}) collective-permute-start(bf16[4,256,256]{2,1,0:T(8,128)(2,1)S(1)} %broadcast_select_fusion.1), channel_id=1, source_target_pairs={{0,8},{1,9},{10,2},{11,3},{4,12},{5,13},{14,6},{15,7},{16,24},{17,... | collective-permute-start | bytes 1572872 | tf_op jit(solution)/shard_map/ppermute | solution.py:77
  26.7 1.5 %collective-permute-start.2 = (bf16[4,256,256]{2,1,0:T(8,128)(2,1)S(1)}, bf16[4,256,256]{2,1,0:T(8,128)(2,1)S(1)}, u32[]{:S(2)}, u32[]{:S(2)}) collective-permute-start(bf16[4,256,256]{2,1,0:T(8,128)(2,1)S(1)} %get-tuple-element.37), channel_id=1, source_target_pairs={{0,1},{1,0},{2,3},{3,2},{4,5},{5,4},{6,7},{7,6},{8,9},{9,8},{10,11... | collective-permute-start | bytes 1572872 | tf_op jit(solution)/shard_map/ppermute | solution.py:80
  28.2 3.5 %bitcast_convert_fusion = bf16[8,256,256]{2,1,0:T(8,128)(2,1)S(1)} fusion(bf16[8,4,256,256]{3,2,1,0:T(8,128)(2,1)} %param.9, pred[8,4]{1,0:T(8,128)(4,1)S(1)} %copy.21, bf16[4,256,256]{2,1,0:T(8,128)(2,1)S(1)} %broadcast_select_fusion.1, bf16[4,256,256]{2,1,0:T(8,128)(2,1)S(1)} %collective-permute-done.6, pred[]{:T(512)S(6)} %eq.21), kind=kOutput, calls=%fused_computation.6 | convolution fusion | flops 1076625408 | bytes 6291489 | tf_op jit(solution)/shard_map/ijab,jbc->iac/dot_general | solution.py:113
  31.7 0.7 convolution_bitcast_fusion.2
  33.0 0.7 convolution_bitcast_fusion
  34.3 0.9 %collective-permute-done.10 = bf16[384,256]{1,0:T(8,128)(2,1)S(1)} collective-permute-done((bf16[384,256]{1,0:T(8,128)(2,1)S(1)}, bf16[384,256]{1,0:T(8,128)(2,1)S(1)}, u32[]{:S(2)}, u32[]{:S(2)}) %collective-permute-start.10) | collective-permute-done | bytes 196640 | tf_op jit(solution)/shard_map/ppermute | solution.py:83
  35.3 2.6 %collective-permute-start.11 = (bf16[192,256]{1,0:T(8,128)(2,1)S(1)}, bf16[192,256]{1,0:T(8,128)(2,1)S(1)}, u32[]{:S(2)}, u32[]{:S(2)}) collective-permute-start(bf16[192,256]{1,0:T(8,128)(2,1)S(1)} %dynamic-slice_convert_fusion.1), channel_id=1, source_target_pairs={{0,16},{1,17},{2,18},{3,19},{4,20},{5,21},{6,22},{7,23},{8,24},{9,... | collective-permute-start | bytes 294920 | tf_op jit(solution)/shard_map/ppermute | solution.py:83
  38.2 0.7 collective-permute-start.3
  38.9 2.0 %collective-permute-done.11 = bf16[192,256]{1,0:T(8,128)(2,1)S(1)} collective-permute-done((bf16[192,256]{1,0:T(8,128)(2,1)S(1)}, bf16[192,256]{1,0:T(8,128)(2,1)S(1)}, u32[]{:S(2)}, u32[]{:S(2)}) %collective-permute-start.11) | collective-permute-done | bytes 98336 | tf_op jit(solution)/shard_map/ppermute | solution.py:83
  41.7 4.0 %collective-permute-done.12 = bf16[192,256]{1,0:T(8,128)(2,1)S(1)} collective-permute-done((bf16[192,256]{1,0:T(8,128)(2,1)S(1)}, bf16[192,256]{1,0:T(8,128)(2,1)S(1)}, u32[]{:S(2)}, u32[]{:S(2)}) %collective-permute-start.12) | collective-permute-done | bytes 98336 | tf_op jit(solution)/shard_map/ppermute | solution.py:80
  45.7 3.1 %collective-permute-done.7 = bf16[4,256,256]{2,1,0:T(8,128)(2,1)S(1)} collective-permute-done((bf16[4,256,256]{2,1,0:T(8,128)(2,1)S(1)}, bf16[4,256,256]{2,1,0:T(8,128)(2,1)S(1)}, u32[]{:S(2)}, u32[]{:S(2)}) %collective-permute-start.7) | collective-permute-done | bytes 524320 | tf_op jit(solution)/shard_map/ppermute | solution.py:80
  49.2 0.8 collective-permute-start.8
  50.0 6.2 %collective-permute-done.13 = bf16[192,256]{1,0:T(8,128)(2,1)S(1)} collective-permute-done((bf16[192,256]{1,0:T(8,128)(2,1)S(1)}, bf16[192,256]{1,0:T(8,128)(2,1)S(1)}, u32[]{:S(2)}, u32[]{:S(2)}) %collective-permute-start.13) | collective-permute-done | bytes 98336 | tf_op jit(solution)/shard_map/ppermute | solution.py:80
  56.2 3.6 %collective-permute-start.14 = (bf16[192,256]{1,0:T(8,128)(2,1)S(1)}, bf16[192,256]{1,0:T(8,128)(2,1)S(1)}, u32[]{:S(2)}, u32[]{:S(2)}) collective-permute-start(bf16[192,256]{1,0:T(8,128)(2,1)S(1)} %add_convert_fusion.3), channel_id=1, source_target_pairs={{0,4},{1,5},{2,6},{3,7},{4,0},{5,1},{6,2},{7,3},{8,12},{9,13},{10,... | collective-permute-start | bytes 294920 | tf_op jit(solution)/shard_map/ppermute | solution.py:80
  59.9 8.9 %collective-permute-done.14 = bf16[192,256]{1,0:T(8,128)(2,1)S(1)} collective-permute-done((bf16[192,256]{1,0:T(8,128)(2,1)S(1)}, bf16[192,256]{1,0:T(8,128)(2,1)S(1)}, u32[]{:S(2)}, u32[]{:S(2)}) %collective-permute-start.14) | collective-permute-done | bytes 98336 | tf_op jit(solution)/shard_map/ppermute | solution.py:80
  68.8 1.6 %collective-permute-start.15 = (bf16[192,256]{1,0:T(8,128)(2,1)S(1)}, bf16[192,256]{1,0:T(8,128)(2,1)S(1)}, u32[]{:S(2)}, u32[]{:S(2)}) collective-permute-start(bf16[192,256]{1,0:T(8,128)(2,1)S(1)} %add_convert_fusion.2), channel_id=1, source_target_pairs={{0,16},{1,17},{2,18},{3,19},{4,20},{5,21},{6,22},{7,23},{8,24},{9,... | collective-permute-start | bytes 294920 | tf_op jit(solution)/shard_map/ppermute | solution.py:83
  70.6 2.9 %collective-permute-done.15 = bf16[192,256]{1,0:T(8,128)(2,1)S(1)} collective-permute-done((bf16[192,256]{1,0:T(8,128)(2,1)S(1)}, bf16[192,256]{1,0:T(8,128)(2,1)S(1)}, u32[]{:S(2)}, u32[]{:S(2)}) %collective-permute-start.15) | collective-permute-done | bytes 98336 | tf_op jit(solution)/shard_map/ppermute | solution.py:83
  73.7 3.2 %collective-permute-done.9 = bf16[1,256,256]{2,1,0:T(8,128)(2,1)S(1)} collective-permute-done((bf16[1,256,256]{2,1,0:T(8,128)(2,1)S(1)}, bf16[1,256,256]{2,1,0:T(8,128)(2,1)S(1)}, u32[]{:S(2)}, u32[]{:S(2)}) %collective-permute-start.9) | collective-permute-done | bytes 131104 | tf_op jit(solution)/shard_map/ppermute | solution.py:80
  77.0 0.9 %fusion.33 = bf16[1,256,256]{2,1,0:T(8,128)(2,1)} fusion(f32[2,1,1,256,256]{4,3,0,2,1:T(8,128)S(1)} %get-tuple-element.32, s32[]{:T(128)S(6)} %select_n.163, bf16[1,256,256]{2,1,0:T(8,128)(2,1)S(1)} %collective-permute-done.9, bf16[256,256]{1,0:T(8,128)(2,1)S(1)} %copy-done.1, bf16[1,256,256]{2,1,0:T(8,128)(2,1)S(1)} %fusion.32, ...), kind=kOutput, calls=%fused_computation.62 | convolution fusion | flops 34013184 | bytes 917512 | tf_op jit(solution)/shard_map/dot_general | solution.py:158
  77.9 0.8 pad_maximum_fusion.1
  78.7 2.3 %shard_map.128 = (bf16[256,256]{1,0:T(8,128)(2,1)}, bf16[256,256]{1,0:T(8,128)(2,1)}, bf16[256,256]{1,0:T(8,128)(2,1)}) custom-call(bf16[3,256,256]{2,1,0:T(8,128)(2,1)} %bitcast.91, bf16[256,256]{1,0:T(8,128)(2,1)} %link.1, f32[256,256]{1,0:T(8,128)} %inverse_one.1, f32[256,256]{1,0:T(8,128)} %inverse_two.1), custom_call_target="tpu_custom_call" | custom-call | flops 100663296 | bytes 1048576 | tf_op jit(solution)/shard_map/pallas_call | solution.py:26
  (54 shorter events, 4.9 us)
Async XLA Ops:
  1.7 11.6 %collective-permute-start = (bf16[4,256,256]{2,1,0:T(8,128)(2,1)S(1)}, bf16[4,256,256]{2,1,0:T(8,128)(2,1)S(1)}, u32[]{:S(2)}, u32[]{:S(2)}) collective-permute-start(bf16[4,256,256]{2,1,0:T(8,128)(2,1)S(1)} %constant_dynamic-slice_fusion.4), channel_id=1, source_target_pairs={{0,16},{1,17},{10,26},{11,27},{20,4},{21,5},{30,14},{31,15}} | collective-permute-start | bytes 1572872 | tf_op jit(solution)/shard_map/ppermute | solution.py:67
  7.7 11.2 %collective-permute-start.5 = (bf16[4,256,256]{2,1,0:T(8,128)(2,1)S(1)}, bf16[4,256,256]{2,1,0:T(8,128)(2,1)S(1)}, u32[]{:S(2)}, u32[]{:S(2)}) collective-permute-start(bf16[4,256,256]{2,1,0:T(8,128)(2,1)S(1)} %constant_dynamic-slice_fusion.2), channel_id=1, source_target_pairs={{0,16},{1,17},{10,26},{11,27},{20,4},{21,5},{30,14},{31,15}} | collective-permute-start | bytes 1572872 | tf_op jit(solution)/shard_map/ppermute | solution.py:67
  13.4 5.6 %collective-permute-start.1 = (bf16[4,256,256]{2,1,0:T(8,128)(2,1)S(1)}, bf16[4,256,256]{2,1,0:T(8,128)(2,1)S(1)}, u32[]{:S(2)}, u32[]{:S(2)}) collective-permute-start(bf16[4,256,256]{2,1,0:T(8,128)(2,1)S(1)} %broadcast_select_fusion.2), channel_id=1, source_target_pairs={{0,8},{1,9},{10,2},{11,3},{4,12},{5,13},{14,6},{15,7},{16,24},{17,... | collective-permute-start | bytes 1572872 | tf_op jit(solution)/shard_map/ppermute | solution.py:77
  19.0 4.9 %copy-start.5 = (s32[32]{0:T(128)S(1)}, s32[32]{0:T(128)}, u32[]{:S(2)}) copy-start(s32[32]{0:T(128)} %param.11) | copy-start | bytes 388
  19.0 5.5 %copy-start.4 = (s32[32]{0:T(128)S(1)}, s32[32]{0:T(128)}, u32[]{:S(2)}) copy-start(s32[32]{0:T(128)} %param.12) | copy-start | bytes 388
  22.5 5.7 %collective-permute-start.6 = (bf16[4,256,256]{2,1,0:T(8,128)(2,1)S(1)}, bf16[4,256,256]{2,1,0:T(8,128)(2,1)S(1)}, u32[]{:S(2)}, u32[]{:S(2)}) collective-permute-start(bf16[4,256,256]{2,1,0:T(8,128)(2,1)S(1)} %broadcast_select_fusion.1), channel_id=1, source_target_pairs={{0,8},{1,9},{10,2},{11,3},{4,12},{5,13},{14,6},{15,7},{16,24},{17,... | collective-permute-start | bytes 1572872 | tf_op jit(solution)/shard_map/ppermute | solution.py:77
  26.7 5.1 %copy-start.2 = (bf16[8,256,256]{2,1,0:T(8,128)(2,1)S(1)}, bf16[8,256,256]{2,1,0:T(8,128)(2,1)}, u32[]{:S(2)}) copy-start(bf16[8,256,256]{2,1,0:T(8,128)(2,1)} %param.13) | copy-start | bytes 3145732
  26.7 5.7 %copy-start.3 = (bf16[8,256,256]{2,1,0:T(8,128)(2,1)S(1)}, bf16[8,256,256]{2,1,0:T(8,128)(2,1)}, u32[]{:S(2)}) copy-start(bf16[8,256,256]{2,1,0:T(8,128)(2,1)} %param.14) | copy-start | bytes 3145732
  26.7 11.4 %collective-permute-start.2 = (bf16[4,256,256]{2,1,0:T(8,128)(2,1)S(1)}, bf16[4,256,256]{2,1,0:T(8,128)(2,1)S(1)}, u32[]{:S(2)}, u32[]{:S(2)}) collective-permute-start(bf16[4,256,256]{2,1,0:T(8,128)(2,1)S(1)} %get-tuple-element.37), channel_id=1, source_target_pairs={{0,1},{1,0},{2,3},{3,2},{4,5},{5,4},{6,7},{7,6},{8,9},{9,8},{10,11... | collective-permute-start | bytes 1572872 | tf_op jit(solution)/shard_map/ppermute | solution.py:80
  33.7 1.5 %collective-permute-start.10 = (bf16[384,256]{1,0:T(8,128)(2,1)S(1)}, bf16[384,256]{1,0:T(8,128)(2,1)S(1)}, u32[]{:S(2)}, u32[]{:S(2)}) collective-permute-start(bf16[384,256]{1,0:T(8,128)(2,1)S(1)} %dynamic-slice_convert_fusion), channel_id=1, source_target_pairs={{0,8},{1,9},{2,10},{3,11},{4,12},{5,13},{6,14},{7,15},{8,0},{9,1},... | collective-permute-start | bytes 589832 | tf_op jit(solution)/shard_map/ppermute | solution.py:83
  34.0 14.8 %collective-permute-start.7 = (bf16[4,256,256]{2,1,0:T(8,128)(2,1)S(1)}, bf16[4,256,256]{2,1,0:T(8,128)(2,1)S(1)}, u32[]{:S(2)}, u32[]{:S(2)}) collective-permute-start(bf16[4,256,256]{2,1,0:T(8,128)(2,1)S(1)} %bitcast.96), channel_id=1, source_target_pairs={{0,2},{1,3},{2,0},{3,1},{4,6},{5,7},{6,4},{7,5},{8,10},{9,11},{10,... | collective-permute-start | bytes 1572872 | tf_op jit(solution)/shard_map/ppermute | solution.py:80
  35.3 5.7 %collective-permute-start.11 = (bf16[192,256]{1,0:T(8,128)(2,1)S(1)}, bf16[192,256]{1,0:T(8,128)(2,1)S(1)}, u32[]{:S(2)}, u32[]{:S(2)}) collective-permute-start(bf16[192,256]{1,0:T(8,128)(2,1)S(1)} %dynamic-slice_convert_fusion.1), channel_id=1, source_target_pairs={{0,16},{1,17},{2,18},{3,19},{4,20},{5,21},{6,22},{7,23},{8,24},{9,... | collective-permute-start | bytes 294920 | tf_op jit(solution)/shard_map/ppermute | solution.py:83
  38.2 38.8 %copy-start.1 = (bf16[256,256]{1,0:T(8,128)(2,1)S(1)}, bf16[256,256]{1,0:T(8,128)(2,1)}, u32[]{:S(2)}) copy-start(bf16[256,256]{1,0:T(8,128)(2,1)} %link.1) | copy-start | bytes 393220
  38.2 17.9 %collective-permute-start.3 = (bf16[2,256,256]{2,1,0:T(8,128)(2,1)S(1)}, bf16[2,256,256]{2,1,0:T(8,128)(2,1)S(1)}, u32[]{:S(2)}, u32[]{:S(2)}) collective-permute-start(bf16[2,256,256]{2,1,0:T(8,128)(2,1)S(1)} %get-tuple-element.33), channel_id=1, source_target_pairs={{0,2},{1,3},{2,0},{3,1},{4,6},{5,7},{6,4},{7,5},{8,10},{9,11},{10,... | collective-permute-start | bytes 786440 | tf_op jit(solution)/shard_map/ppermute | solution.py:80
  41.0 4.7 %collective-permute-start.12 = (bf16[192,256]{1,0:T(8,128)(2,1)S(1)}, bf16[192,256]{1,0:T(8,128)(2,1)S(1)}, u32[]{:S(2)}, u32[]{:S(2)}) collective-permute-start(bf16[192,256]{1,0:T(8,128)(2,1)S(1)} %add_convert_fusion.5), channel_id=1, source_target_pairs={{0,1},{1,0},{2,3},{3,2},{4,5},{5,4},{6,7},{7,6},{8,9},{9,8},{10,11... | collective-permute-start | bytes 294920 | tf_op jit(solution)/shard_map/ppermute | solution.py:80
  48.8 7.3 %collective-permute-start.13 = (bf16[192,256]{1,0:T(8,128)(2,1)S(1)}, bf16[192,256]{1,0:T(8,128)(2,1)S(1)}, u32[]{:S(2)}, u32[]{:S(2)}) collective-permute-start(bf16[192,256]{1,0:T(8,128)(2,1)S(1)} %add_convert_fusion.4), channel_id=1, source_target_pairs={{0,2},{1,3},{2,0},{3,1},{4,6},{5,7},{6,4},{7,5},{8,10},{9,11},{10,... | collective-permute-start | bytes 294920 | tf_op jit(solution)/shard_map/ppermute | solution.py:80
  49.2 19.6 %collective-permute-start.8 = (bf16[2,256,256]{2,1,0:T(8,128)(2,1)S(1)}, bf16[2,256,256]{2,1,0:T(8,128)(2,1)S(1)}, u32[]{:S(2)}, u32[]{:S(2)}) collective-permute-start(bf16[2,256,256]{2,1,0:T(8,128)(2,1)S(1)} %get-tuple-element.31), channel_id=1, source_target_pairs={{0,1},{1,0},{2,3},{3,2},{4,5},{5,4},{6,7},{7,6},{8,9},{9,8},{10,11... | collective-permute-start | bytes 786440 | tf_op jit(solution)/shard_map/ppermute | solution.py:80
  56.2 12.6 %collective-permute-start.14 = (bf16[192,256]{1,0:T(8,128)(2,1)S(1)}, bf16[192,256]{1,0:T(8,128)(2,1)S(1)}, u32[]{:S(2)}, u32[]{:S(2)}) collective-permute-start(bf16[192,256]{1,0:T(8,128)(2,1)S(1)} %add_convert_fusion.3), channel_id=1, source_target_pairs={{0,4},{1,5},{2,6},{3,7},{4,0},{5,1},{6,2},{7,3},{8,12},{9,13},{10,... | collective-permute-start | bytes 294920 | tf_op jit(solution)/shard_map/ppermute | solution.py:80
  59.8 13.8 %collective-permute-start.4 = (bf16[1,256,256]{2,1,0:T(8,128)(2,1)S(1)}, bf16[1,256,256]{2,1,0:T(8,128)(2,1)S(1)}, u32[]{:S(2)}, u32[]{:S(2)}) collective-permute-start(bf16[1,256,256]{2,1,0:T(8,128)(2,1)S(1)} %fusion.29), channel_id=1, source_target_pairs={{0,4},{1,5},{2,6},{3,7},{4,0},{5,1},{6,2},{7,3},{8,12},{9,13},{10,... | collective-permute-start | bytes 393224 | tf_op jit(solution)/shard_map/ppermute | solution.py:80
  68.8 4.7 %collective-permute-start.15 = (bf16[192,256]{1,0:T(8,128)(2,1)S(1)}, bf16[192,256]{1,0:T(8,128)(2,1)S(1)}, u32[]{:S(2)}, u32[]{:S(2)}) collective-permute-start(bf16[192,256]{1,0:T(8,128)(2,1)S(1)} %add_convert_fusion.2), channel_id=1, source_target_pairs={{0,16},{1,17},{2,18},{3,19},{4,20},{5,21},{6,22},{7,23},{8,24},{9,... | collective-permute-start | bytes 294920 | tf_op jit(solution)/shard_map/ppermute | solution.py:83
  70.5 6.5 %collective-permute-start.9 = (bf16[1,256,256]{2,1,0:T(8,128)(2,1)S(1)}, bf16[1,256,256]{2,1,0:T(8,128)(2,1)S(1)}, u32[]{:S(2)}, u32[]{:S(2)}) collective-permute-start(bf16[1,256,256]{2,1,0:T(8,128)(2,1)S(1)} %fusion.28), channel_id=1, source_target_pairs={{0,4},{1,5},{2,6},{3,7},{4,0},{5,1},{6,2},{7,3},{8,12},{9,13},{10,... | collective-permute-start | bytes 393224 | tf_op jit(solution)/shard_map/ppermute | solution.py:80
  73.6 4.2 %collective-permute-start.16 = (bf16[384,256]{1,0:T(8,128)(2,1)S(1)}, bf16[384,256]{1,0:T(8,128)(2,1)S(1)}, u32[]{:S(2)}, u32[]{:S(2)}) collective-permute-start(bf16[384,256]{1,0:T(8,128)(2,1)S(1)} %pad_maximum_fusion.2), channel_id=1, source_target_pairs={{0,8},{1,9},{2,10},{3,11},{4,12},{5,13},{6,14},{7,15},{8,0},{9,1},... | collective-permute-start | bytes 589832 | tf_op jit(solution)/shard_map/ppermute | solution.py:83
  73.7 7.2 %copy-start = (bf16[1,256,256]{2,1,0:T(8,128)(2,1)}, bf16[1,256,256]{2,1,0:T(8,128)(2,1)S(1)}, u32[]{:S(2)}) copy-start(bf16[1,256,256]{2,1,0:T(8,128)(2,1)S(1)} %fusion.32) | copy-start | bytes 393220

commit v2 on v1

--- a/solution.py
+++ b/solution.py
@@ -123,13 +123,11 @@
     piece_one, piece_two = (part_of(f, col % group * cols, cols) for f in (factor_one, factor_two))
     piece_one, piece_two = after(piece_one), after(piece_two)
     order_one, order_two = list(range(bits)), [1, 0, *range(2, bits)]
-    have_one, have_two = over_chips(piece_one, *marks), over_chips(piece_two)
+    have_one, have_two = over_chips(piece_one, *marks, flags_one, flags_two), over_chips(piece_two)
     all_one = products(marks[0], over_cores(have_one))
     left_one, keep_one, one = first_swap(all_one, order_one)
-    column = over_cores(after(have_two, all_one))
-    all_two = products(marks[1], column)
+    all_two = products(marks[1], over_cores(after(have_two, all_one)))
     left_two, keep_two, two = first_swap(all_two, order_two)
-    all_one = after(all_one, all_two)
     sums = contraction(first, all_one), contraction(all_one, second_in_one), contraction(second, all_two)
     for _ in range(1, bits):
         keep_one = next_swap(left_one, keep_one, one, order_one)
@@ -145,8 +143,8 @@
         part = lax.dynamic_slice_in_dim(part, mine * half, half, 0) + got.astype(F32)
     part = part.astype(BF16)
     gates = [one[0], two[0], *one[1:]]
-    for bit in range(bits):
-        got = swap(after(part, gates[bit]), bit)
+    for bit, gate in zip((*range(2, bits), 0, 1), gates):
+        got = swap(after(part, gate), bit)
         part = (part.astype(F32) + got.astype(F32)).astype(BF16)
     for bit in reversed(range(row_bits)):
         got = swap_rows(after(part, one[-1] if bit == 0 else two[-2]), bit)

time: 81.4 us -> 77.8 us (0.956)
  waiting for transfers between devices: 37.5 us -> 29.4 us
  starting transfers between devices: 21.3 us -> 25.9 us
  matrix products: 9.73 us -> 7.62 us
  local copies, waits for them, and re-layouts: 5.22 us -> 6.53 us
    ppermute x9, starting transfers between devices: 8.06 us -> 14.2 us  [swap(): lax.ppermute(array, BOTH, [(at(r, c), at(r, c ^ 1 << bit)) for r, c in ev...]
    ppermute x2, waiting for transfers between devices: 6.09 us -> 1.41 us  [over_chips(): got = after(lax.ppermute(piece, BOTH, perm), *earlier)]
    ppermute x9, waiting for transfers between devices: 25.5 us -> 23.1 us  [swap(): lax.ppermute(array, BOTH, [(at(r, c), at(r, c ^ 1 << bit)) for r, c in ev...]
    dot_general x2, matrix products: 6.99 us -> 4.9 us  [products(): jnp.einsum('ijab,jbc->iac', kept, column, preferred_element_type=F32)]
    ppermute x4, starting transfers between devices: 4.35 us -> 2.7 us  [swap_rows(): lax.ppermute(array, BOTH, [(at(r, c), at(r ^ 1 << bit, c)) for r, c in ev...]
    dynamic_slice x2, local copies, waits for them, and re-layouts: 1.17 us -> 2.48 us  [shards(): m[row * rows + col].astype(F32)]
    ppermute x4, waiting for transfers between devices: 5.89 us -> 4.96 us  [swap_rows(): lax.ppermute(array, BOTH, [(at(r, c), at(r ^ 1 << bit, c)) for r, c in ev...]
where the time goes in v2:
time: 77.8 us; the launch traced here: 77.4 us
  waiting for transfers between devices  29.4 us (38%)
  starting transfers between devices  25.9 us (33%)
  matrix products  7.62 us (10%)
  local copies, waits for them, and re-layouts  6.53 us (8%)
  other arithmetic  3.23 us (4%)
  between operations  2.39 us (3%)
  Pallas kernels  2.27 us (3%)
    ppermute x9, waiting for transfers between devices, swap(): lax.ppermute(array, BOTH, [(at(r, c), at(r, c ^ 1 << bit)) for r, c in ev...  23.1 us
    ppermute x9, starting transfers between devices, swap(): lax.ppermute(array, BOTH, [(at(r, c), at(r, c ^ 1 << bit)) for r, c in ev...  14.2 us
    ppermute x2, starting transfers between devices, over_chips(): got = after(lax.ppermute(piece, BOTH, perm), *earlier)  6.23 us
    ppermute x4, waiting for transfers between devices, swap_rows(): lax.ppermute(array, BOTH, [(at(r, c), at(r ^ 1 << bit, c)) for r, c in ev...  4.96 us
    dot_general x2, matrix products, products(): jnp.einsum('ijab,jbc->iac', kept, column, preferred_element_type=F32)  4.9 us
    dynamic_slice x4, local copies, waits for them, and re-layouts, part_of(): return lax.dynamic_slice_in_dim(array, start, size, 0)  3.62 us
    ppermute x2, starting transfers between devices, over_cores(): lax.ppermute(have, BOTH, perm)  2.78 us
    ppermute x4, starting transfers between devices, swap_rows(): lax.ppermute(array, BOTH, [(at(r, c), at(r ^ 1 << bit, c)) for r, c in ev...  2.7 us
  transfers between devices with their start and end apart: 17, of which 11 were waited for; matrix products, arithmetic and copies ran while one was open for 15% of the time, Pallas kernels for 0%

profile of v2, /device:TPU:0, one launch (start us, length us, event | category | flops | bytes accessed | tf_op | source)
XLA Modules:
  0.0 77.4 jit_solution(4127174912165646043)
XLA Ops:
  0.6 1.1 %constant_dynamic-slice_fusion.4 = bf16[4,256,256]{2,1,0:T(8,128)(2,1)S(1)} fusion(bf16[8,256,256]{2,1,0:T(8,128)(2,1)} %param.13, s32[]{:T(128)S(6)} %select_n.157), kind=kLoop, calls=%fused_computation.71 | loop fusion | bytes 1048580 | tf_op jit(solution)/shard_map/dynamic_slice | solution.py:106
  1.7 4.9 %collective-permute-start = (bf16[4,256,256]{2,1,0:T(8,128)(2,1)S(1)}, bf16[4,256,256]{2,1,0:T(8,128)(2,1)S(1)}, u32[]{:S(2)}, u32[]{:S(2)}) collective-permute-start(bf16[4,256,256]{2,1,0:T(8,128)(2,1)S(1)} %constant_dynamic-slice_fusion.4), channel_id=1, source_target_pairs={{0,16},{1,17},{10,26},{11,27},{20,4},{21,5},{30,14},{31,15}} | collective-permute-start | bytes 1572872 | tf_op jit(solution)/shard_map/ppermute | solution.py:67
  6.6 1.1 %constant_dynamic-slice_fusion.2 = bf16[4,256,256]{2,1,0:T(8,128)(2,1)S(1)} fusion(bf16[8,256,256]{2,1,0:T(8,128)(2,1)} %param.14, s32[]{:T(128)S(6)} %select_n.157), kind=kLoop, calls=%fused_computation.69 | loop fusion | bytes 1048580 | tf_op jit(solution)/shard_map/dynamic_slice | solution.py:106
  7.7 1.3 %collective-permute-start.5 = (bf16[4,256,256]{2,1,0:T(8,128)(2,1)S(1)}, bf16[4,256,256]{2,1,0:T(8,128)(2,1)S(1)}, u32[]{:S(2)}, u32[]{:S(2)}) collective-permute-start(bf16[4,256,256]{2,1,0:T(8,128)(2,1)S(1)} %constant_dynamic-slice_fusion.2), channel_id=1, source_target_pairs={{0,16},{1,17},{10,26},{11,27},{20,4},{21,5},{30,14},{31,15}} | collective-permute-start | bytes 1572872 | tf_op jit(solution)/shard_map/ppermute | solution.py:67
  9.1 0.7 dynamic_slice.105
  10.6 0.7 broadcast_compare_fusion.2
  11.3 0.8 broadcast_compare_fusion
  12.1 1.2 %collective-permute-done = bf16[4,256,256]{2,1,0:T(8,128)(2,1)S(1)} collective-permute-done((bf16[4,256,256]{2,1,0:T(8,128)(2,1)S(1)}, bf16[4,256,256]{2,1,0:T(8,128)(2,1)S(1)}, u32[]{:S(2)}, u32[]{:S(2)}) %collective-permute-start) | collective-permute-done | bytes 524320 | tf_op jit(solution)/shard_map/ppermute | solution.py:67
  13.4 1.3 %collective-permute-start.1 = (bf16[4,256,256]{2,1,0:T(8,128)(2,1)S(1)}, bf16[4,256,256]{2,1,0:T(8,128)(2,1)S(1)}, u32[]{:S(2)}, u32[]{:S(2)}) collective-permute-start(bf16[4,256,256]{2,1,0:T(8,128)(2,1)S(1)} %broadcast_select_fusion.2), channel_id=1, source_target_pairs={{0,8},{1,9},{10,2},{11,3},{4,12},{5,13},{14,6},{15,7},{16,24},{17,... | collective-permute-start | bytes 1572872 | tf_op jit(solution)/shard_map/ppermute | solution.py:77
  14.7 1.2 %dynamic_slice.104 = s32[1]{0:T(128)} dynamic-slice(s32[32]{0:T(128)} %param.11, s32[]{:T(128)S(6)} %select_n.148), dynamic_slice_sizes={1} | dynamic-slice | bytes 12 | tf_op jit(solution)/shard_map/dynamic_slice | solution.py:154
  16.0 1.2 %dynamic_slice.122 = s32[1]{0:T(128)} dynamic-slice(s32[32]{0:T(128)} %param.12, s32[]{:T(128)S(6)} %select_n.148), dynamic_slice_sizes={1} | dynamic-slice | bytes 12 | tf_op jit(solution)/shard_map/dynamic_slice | solution.py:154
  19.0 3.6 %bitcast_convert_fusion.1 = bf16[8,256,256]{2,1,0:T(8,128)(2,1)S(1)} fusion(bf16[8,4,256,256]{3,2,1,0:T(8,128)(2,1)} %param.9, pred[8,4]{1,0:T(8,128)(4,1)S(1)} %copy.19, bf16[4,256,256]{2,1,0:T(8,128)(2,1)S(1)} %broadcast_select_fusion.2, bf16[4,256,256]{2,1,0:T(8,128)(2,1)S(1)} %collective-permute-done.1, pred[]{:T(512)S(6)} %eq.21), kind=kOutput, calls=%fused_computation.7 | convolution fusion | flops 1076625408 | bytes 6291489 | tf_op jit(solution)/shard_map/ijab,jbc->iac/dot_general | solution.py:113
  22.6 1.5 %collective-permute-start.6 = (bf16[4,256,256]{2,1,0:T(8,128)(2,1)S(1)}, bf16[4,256,256]{2,1,0:T(8,128)(2,1)S(1)}, u32[]{:S(2)}, u32[]{:S(2)}) collective-permute-start(bf16[4,256,256]{2,1,0:T(8,128)(2,1)S(1)} %broadcast_select_fusion.1), channel_id=1, source_target_pairs={{0,8},{1,9},{10,2},{11,3},{4,12},{5,13},{14,6},{15,7},{16,24},{17,... | collective-permute-start | bytes 1572872 | tf_op jit(solution)/shard_map/ppermute | solution.py:77
  24.1 1.6 %collective-permute-start.2 = (bf16[4,256,256]{2,1,0:T(8,128)(2,1)S(1)}, bf16[4,256,256]{2,1,0:T(8,128)(2,1)S(1)}, u32[]{:S(2)}, u32[]{:S(2)}) collective-permute-start(bf16[4,256,256]{2,1,0:T(8,128)(2,1)S(1)} %get-tuple-element.39), channel_id=1, source_target_pairs={{0,1},{1,0},{2,3},{3,2},{4,5},{5,4},{6,7},{7,6},{8,9},{9,8},{10,11... | collective-permute-start | bytes 1572872 | tf_op jit(solution)/shard_map/ppermute | solution.py:80
  26.9 1.3 %bitcast_convert_fusion = bf16[8,256,256]{2,1,0:T(8,128)(2,1)S(1)} fusion(bf16[8,4,256,256]{3,2,1,0:T(8,128)(2,1)S(1)} %copy-done.4, pred[8,4]{1,0:T(8,128)(4,1)S(1)} %copy.21, bf16[4,256,256]{2,1,0:T(8,128)(2,1)S(1)} %broadcast_select_fusion.1, bf16[4,256,256]{2,1,0:T(8,128)(2,1)S(1)} %collective-permute-done.6, pred[]{:T(512)S(6)} %eq.21), kind=kOutput, calls=%fused_computation.6 | convolution fusion | flops 1076625408 | bytes 6291489 | tf_op jit(solution)/shard_map/ijab,jbc->iac/dot_general | solution.py:113
  29.6 0.9 %collective-permute-done.10 = bf16[384,256]{1,0:T(8,128)(2,1)S(1)} collective-permute-done((bf16[384,256]{1,0:T(8,128)(2,1)S(1)}, bf16[384,256]{1,0:T(8,128)(2,1)S(1)}, u32[]{:S(2)}, u32[]{:S(2)}) %collective-permute-start.10) | collective-permute-done | bytes 196640 | tf_op jit(solution)/shard_map/ppermute | solution.py:83
  30.6 2.6 %collective-permute-start.11 = (bf16[192,256]{1,0:T(8,128)(2,1)S(1)}, bf16[192,256]{1,0:T(8,128)(2,1)S(1)}, u32[]{:S(2)}, u32[]{:S(2)}) collective-permute-start(bf16[192,256]{1,0:T(8,128)(2,1)S(1)} %dynamic-slice_convert_fusion.1), channel_id=1, source_target_pairs={{0,16},{1,17},{2,18},{3,19},{4,20},{5,21},{6,22},{7,23},{8,24},{9,... | collective-permute-start | bytes 294920 | tf_op jit(solution)/shard_map/ppermute | solution.py:83
  33.2 2.3 %collective-permute-done.2 = bf16[4,256,256]{2,1,0:T(8,128)(2,1)S(1)} collective-permute-done((bf16[4,256,256]{2,1,0:T(8,128)(2,1)S(1)}, bf16[4,256,256]{2,1,0:T(8,128)(2,1)S(1)}, u32[]{:S(2)}, u32[]{:S(2)}) %collective-permute-start.2) | collective-permute-done | bytes 524320 | tf_op jit(solution)/shard_map/ppermute | solution.py:80
  36.3 3.1 %collective-permute-start.12 = (bf16[192,256]{1,0:T(8,128)(2,1)S(1)}, bf16[192,256]{1,0:T(8,128)(2,1)S(1)}, u32[]{:S(2)}, u32[]{:S(2)}) collective-permute-start(bf16[192,256]{1,0:T(8,128)(2,1)S(1)} %add_convert_fusion.5), channel_id=1, source_target_pairs={{0,4},{1,5},{2,6},{3,7},{4,0},{5,1},{6,2},{7,3},{8,12},{9,13},{10,... | collective-permute-start | bytes 294920 | tf_op jit(solution)/shard_map/ppermute | solution.py:80
  39.4 9.8 %collective-permute-done.12 = bf16[192,256]{1,0:T(8,128)(2,1)S(1)} collective-permute-done((bf16[192,256]{1,0:T(8,128)(2,1)S(1)}, bf16[192,256]{1,0:T(8,128)(2,1)S(1)}, u32[]{:S(2)}, u32[]{:S(2)}) %collective-permute-start.12) | collective-permute-done | bytes 98336 | tf_op jit(solution)/shard_map/ppermute | solution.py:80
  49.3 0.8 %collective-permute-start.13 = (bf16[192,256]{1,0:T(8,128)(2,1)S(1)}, bf16[192,256]{1,0:T(8,128)(2,1)S(1)}, u32[]{:S(2)}, u32[]{:S(2)}) collective-permute-start(bf16[192,256]{1,0:T(8,128)(2,1)S(1)} %add_convert_fusion.4), channel_id=1, source_target_pairs={{0,1},{1,0},{2,3},{3,2},{4,5},{5,4},{6,7},{7,6},{8,9},{9,8},{10,11... | collective-permute-start | bytes 294920 | tf_op jit(solution)/shard_map/ppermute | solution.py:80
  50.2 1.3 %collective-permute-start.8 = (bf16[2,256,256]{2,1,0:T(8,128)(2,1)S(1)}, bf16[2,256,256]{2,1,0:T(8,128)(2,1)S(1)}, u32[]{:S(2)}, u32[]{:S(2)}) collective-permute-start(bf16[2,256,256]{2,1,0:T(8,128)(2,1)S(1)} %get-tuple-element.33), channel_id=1, source_target_pairs={{0,1},{1,0},{2,3},{3,2},{4,5},{5,4},{6,7},{7,6},{8,9},{9,8},{10,11... | collective-permute-start | bytes 786440 | tf_op jit(solution)/shard_map/ppermute | solution.py:80
  51.5 3.5 %collective-permute-done.13 = bf16[192,256]{1,0:T(8,128)(2,1)S(1)} collective-permute-done((bf16[192,256]{1,0:T(8,128)(2,1)S(1)}, bf16[192,256]{1,0:T(8,128)(2,1)S(1)}, u32[]{:S(2)}, u32[]{:S(2)}) %collective-permute-start.13) | collective-permute-done | bytes 98336 | tf_op jit(solution)/shard_map/ppermute | solution.py:80
  55.1 5.8 %collective-permute-start.14 = (bf16[192,256]{1,0:T(8,128)(2,1)S(1)}, bf16[192,256]{1,0:T(8,128)(2,1)S(1)}, u32[]{:S(2)}, u32[]{:S(2)}) collective-permute-start(bf16[192,256]{1,0:T(8,128)(2,1)S(1)} %add_convert_fusion.3), channel_id=1, source_target_pairs={{0,2},{1,3},{2,0},{3,1},{4,6},{5,7},{6,4},{7,5},{8,10},{9,11},{10,... | collective-permute-start | bytes 294920 | tf_op jit(solution)/shard_map/ppermute | solution.py:80
  61.0 3.5 %collective-permute-done.14 = bf16[192,256]{1,0:T(8,128)(2,1)S(1)} collective-permute-done((bf16[192,256]{1,0:T(8,128)(2,1)S(1)}, bf16[192,256]{1,0:T(8,128)(2,1)S(1)}, u32[]{:S(2)}, u32[]{:S(2)}) %collective-permute-start.14) | collective-permute-done | bytes 98336 | tf_op jit(solution)/shard_map/ppermute | solution.py:80
  64.7 1.1 %collective-permute-start.9 = (bf16[1,256,256]{2,1,0:T(8,128)(2,1)S(1)}, bf16[1,256,256]{2,1,0:T(8,128)(2,1)S(1)}, u32[]{:S(2)}, u32[]{:S(2)}) collective-permute-start(bf16[1,256,256]{2,1,0:T(8,128)(2,1)S(1)} %fusion.28), channel_id=1, source_target_pairs={{0,4},{1,5},{2,6},{3,7},{4,0},{5,1},{6,2},{7,3},{8,12},{9,13},{10,... | collective-permute-start | bytes 393224 | tf_op jit(solution)/shard_map/ppermute | solution.py:80
  65.8 3.5 %collective-permute-done.15 = bf16[192,256]{1,0:T(8,128)(2,1)S(1)} collective-permute-done((bf16[192,256]{1,0:T(8,128)(2,1)S(1)}, bf16[192,256]{1,0:T(8,128)(2,1)S(1)}, u32[]{:S(2)}, u32[]{:S(2)}) %collective-permute-start.15) | collective-permute-done | bytes 98336 | tf_op jit(solution)/shard_map/ppermute | solution.py:83
  69.3 2.7 %collective-permute-done.4 = bf16[1,256,256]{2,1,0:T(8,128)(2,1)S(1)} collective-permute-done((bf16[1,256,256]{2,1,0:T(8,128)(2,1)S(1)}, bf16[1,256,256]{2,1,0:T(8,128)(2,1)S(1)}, u32[]{:S(2)}, u32[]{:S(2)}) %collective-permute-start.4) | collective-permute-done | bytes 131104 | tf_op jit(solution)/shard_map/ppermute | solution.py:80
  72.0 1.3 %collective-permute-done.9 = bf16[1,256,256]{2,1,0:T(8,128)(2,1)S(1)} collective-permute-done((bf16[1,256,256]{2,1,0:T(8,128)(2,1)S(1)}, bf16[1,256,256]{2,1,0:T(8,128)(2,1)S(1)}, u32[]{:S(2)}, u32[]{:S(2)}) %collective-permute-start.9) | collective-permute-done | bytes 131104 | tf_op jit(solution)/shard_map/ppermute | solution.py:80
  73.4 0.9 %fusion.33 = bf16[1,256,256]{2,1,0:T(8,128)(2,1)} fusion(f32[2,1,1,256,256]{4,3,0,2,1:T(8,128)S(1)} %get-tuple-element.34, s32[]{:T(128)S(6)} %select_n.164, bf16[1,256,256]{2,1,0:T(8,128)(2,1)S(1)} %collective-permute-done.9, bf16[256,256]{1,0:T(8,128)(2,1)S(1)} %copy-done.1, bf16[1,256,256]{2,1,0:T(8,128)(2,1)S(1)} %fusion.32, ...), kind=kOutput, calls=%fused_computation.62 | convolution fusion | flops 34013184 | bytes 917512 | tf_op jit(solution)/shard_map/dot_general | solution.py:156
  74.3 0.8 %pad_maximum_fusion.1 = bf16[768,256]{1,0:T(8,128)(2,1)} fusion(bf16[384,256]{1,0:T(8,128)(2,1)S(1)} %get-tuple-element.42, bf16[384,256]{1,0:T(8,128)(2,1)S(1)} %get-tuple-element.41), kind=kLoop, calls=%fused_computation.36 | loop fusion | flops 786432 | bytes 786432 | tf_op jit(solution)/shard_map/concatenate | solution.py:152
  75.1 2.3 %shard_map.128 = (bf16[256,256]{1,0:T(8,128)(2,1)}, bf16[256,256]{1,0:T(8,128)(2,1)}, bf16[256,256]{1,0:T(8,128)(2,1)}) custom-call(bf16[3,256,256]{2,1,0:T(8,128)(2,1)} %bitcast.91, bf16[256,256]{1,0:T(8,128)(2,1)} %link.1, f32[256,256]{1,0:T(8,128)} %inverse_one.1, f32[256,256]{1,0:T(8,128)} %inverse_two.1), custom_call_target="tpu_custom_call" | custom-call | flops 100663296 | bytes 1048576 | tf_op jit(solution)/shard_map/pallas_call | solution.py:26
  (52 shorter events, 5.3 us)
Async XLA Ops:
  1.7 11.6 %collective-permute-start = (bf16[4,256,256]{2,1,0:T(8,128)(2,1)S(1)}, bf16[4,256,256]{2,1,0:T(8,128)(2,1)S(1)}, u32[]{:S(2)}, u32[]{:S(2)}) collective-permute-start(bf16[4,256,256]{2,1,0:T(8,128)(2,1)S(1)} %constant_dynamic-slice_fusion.4), channel_id=1, source_target_pairs={{0,16},{1,17},{10,26},{11,27},{20,4},{21,5},{30,14},{31,15}} | collective-permute-start | bytes 1572872 | tf_op jit(solution)/shard_map/ppermute | solution.py:67
  7.7 11.2 %collective-permute-start.5 = (bf16[4,256,256]{2,1,0:T(8,128)(2,1)S(1)}, bf16[4,256,256]{2,1,0:T(8,128)(2,1)S(1)}, u32[]{:S(2)}, u32[]{:S(2)}) collective-permute-start(bf16[4,256,256]{2,1,0:T(8,128)(2,1)S(1)} %constant_dynamic-slice_fusion.2), channel_id=1, source_target_pairs={{0,16},{1,17},{10,26},{11,27},{20,4},{21,5},{30,14},{31,15}} | collective-permute-start | bytes 1572872 | tf_op jit(solution)/shard_map/ppermute | solution.py:67
  13.4 5.6 %collective-permute-start.1 = (bf16[4,256,256]{2,1,0:T(8,128)(2,1)S(1)}, bf16[4,256,256]{2,1,0:T(8,128)(2,1)S(1)}, u32[]{:S(2)}, u32[]{:S(2)}) collective-permute-start(bf16[4,256,256]{2,1,0:T(8,128)(2,1)S(1)} %broadcast_select_fusion.2), channel_id=1, source_target_pairs={{0,8},{1,9},{10,2},{11,3},{4,12},{5,13},{14,6},{15,7},{16,24},{17,... | collective-permute-start | bytes 1572872 | tf_op jit(solution)/shard_map/ppermute | solution.py:77
  19.0 6.7 %copy-start.2 = (bf16[8,256,256]{2,1,0:T(8,128)(2,1)S(1)}, bf16[8,256,256]{2,1,0:T(8,128)(2,1)}, u32[]{:S(2)}) copy-start(bf16[8,256,256]{2,1,0:T(8,128)(2,1)} %param.13) | copy-start | bytes 3145732
  22.6 3.8 %copy-start.3 = (bf16[8,256,256]{2,1,0:T(8,128)(2,1)S(1)}, bf16[8,256,256]{2,1,0:T(8,128)(2,1)}, u32[]{:S(2)}) copy-start(bf16[8,256,256]{2,1,0:T(8,128)(2,1)} %param.14) | copy-start | bytes 3145732
  22.6 4.3 %collective-permute-start.6 = (bf16[4,256,256]{2,1,0:T(8,128)(2,1)S(1)}, bf16[4,256,256]{2,1,0:T(8,128)(2,1)S(1)}, u32[]{:S(2)}, u32[]{:S(2)}) collective-permute-start(bf16[4,256,256]{2,1,0:T(8,128)(2,1)S(1)} %broadcast_select_fusion.1), channel_id=1, source_target_pairs={{0,8},{1,9},{10,2},{11,3},{4,12},{5,13},{14,6},{15,7},{16,24},{17,... | collective-permute-start | bytes 1572872 | tf_op jit(solution)/shard_map/ppermute | solution.py:77
  24.0 2.9 %copy-start.4 = (bf16[8,4,256,256]{3,2,1,0:T(8,128)(2,1)S(1)}, bf16[8,4,256,256]{3,2,1,0:T(8,128)(2,1)}, u32[]{:S(2)}) copy-start(bf16[8,4,256,256]{3,2,1,0:T(8,128)(2,1)} %param.9) | copy-start | bytes 12582916
  24.1 11.3 %collective-permute-start.2 = (bf16[4,256,256]{2,1,0:T(8,128)(2,1)S(1)}, bf16[4,256,256]{2,1,0:T(8,128)(2,1)S(1)}, u32[]{:S(2)}, u32[]{:S(2)}) collective-permute-start(bf16[4,256,256]{2,1,0:T(8,128)(2,1)S(1)} %get-tuple-element.39), channel_id=1, source_target_pairs={{0,1},{1,0},{2,3},{3,2},{4,5},{5,4},{6,7},{7,6},{8,9},{9,8},{10,11... | collective-permute-start | bytes 1572872 | tf_op jit(solution)/shard_map/ppermute | solution.py:80
  29.1 1.5 %collective-permute-start.10 = (bf16[384,256]{1,0:T(8,128)(2,1)S(1)}, bf16[384,256]{1,0:T(8,128)(2,1)S(1)}, u32[]{:S(2)}, u32[]{:S(2)}) collective-permute-start(bf16[384,256]{1,0:T(8,128)(2,1)S(1)} %dynamic-slice_convert_fusion), channel_id=1, source_target_pairs={{0,8},{1,9},{2,10},{3,11},{4,12},{5,13},{6,14},{7,15},{8,0},{9,1},... | collective-permute-start | bytes 589832 | tf_op jit(solution)/shard_map/ppermute | solution.py:83
  29.3 20.0 %collective-permute-start.7 = (bf16[4,256,256]{2,1,0:T(8,128)(2,1)S(1)}, bf16[4,256,256]{2,1,0:T(8,128)(2,1)S(1)}, u32[]{:S(2)}, u32[]{:S(2)}) collective-permute-start(bf16[4,256,256]{2,1,0:T(8,128)(2,1)S(1)} %bitcast.96), channel_id=1, source_target_pairs={{0,2},{1,3},{2,0},{3,1},{4,6},{5,7},{6,4},{7,5},{8,10},{9,11},{10,... | collective-permute-start | bytes 1572872 | tf_op jit(solution)/shard_map/ppermute | solution.py:80
  30.6 5.6 %collective-permute-start.11 = (bf16[192,256]{1,0:T(8,128)(2,1)S(1)}, bf16[192,256]{1,0:T(8,128)(2,1)S(1)}, u32[]{:S(2)}, u32[]{:S(2)}) collective-permute-start(bf16[192,256]{1,0:T(8,128)(2,1)S(1)} %dynamic-slice_convert_fusion.1), channel_id=1, source_target_pairs={{0,16},{1,17},{2,18},{3,19},{4,20},{5,21},{6,22},{7,23},{8,24},{9,... | collective-permute-start | bytes 294920 | tf_op jit(solution)/shard_map/ppermute | solution.py:83
  35.6 37.8 %copy-start.1 = (bf16[256,256]{1,0:T(8,128)(2,1)S(1)}, bf16[256,256]{1,0:T(8,128)(2,1)}, u32[]{:S(2)}) copy-start(bf16[256,256]{1,0:T(8,128)(2,1)} %link.1) | copy-start | bytes 393220
  35.6 19.4 %collective-permute-start.3 = (bf16[2,256,256]{2,1,0:T(8,128)(2,1)S(1)}, bf16[2,256,256]{2,1,0:T(8,128)(2,1)S(1)}, u32[]{:S(2)}, u32[]{:S(2)}) collective-permute-start(bf16[2,256,256]{2,1,0:T(8,128)(2,1)S(1)} %get-tuple-element.35), channel_id=1, source_target_pairs={{0,2},{1,3},{2,0},{3,1},{4,6},{5,7},{6,4},{7,5},{8,10},{9,11},{10,... | collective-permute-start | bytes 786440 | tf_op jit(solution)/shard_map/ppermute | solution.py:80
  36.3 12.9 %collective-permute-start.12 = (bf16[192,256]{1,0:T(8,128)(2,1)S(1)}, bf16[192,256]{1,0:T(8,128)(2,1)S(1)}, u32[]{:S(2)}, u32[]{:S(2)}) collective-permute-start(bf16[192,256]{1,0:T(8,128)(2,1)S(1)} %add_convert_fusion.5), channel_id=1, source_target_pairs={{0,4},{1,5},{2,6},{3,7},{4,0},{5,1},{6,2},{7,3},{8,12},{9,13},{10,... | collective-permute-start | bytes 294920 | tf_op jit(solution)/shard_map/ppermute | solution.py:80
  49.3 5.8 %collective-permute-start.13 = (bf16[192,256]{1,0:T(8,128)(2,1)S(1)}, bf16[192,256]{1,0:T(8,128)(2,1)S(1)}, u32[]{:S(2)}, u32[]{:S(2)}) collective-permute-start(bf16[192,256]{1,0:T(8,128)(2,1)S(1)} %add_convert_fusion.4), channel_id=1, source_target_pairs={{0,1},{1,0},{2,3},{3,2},{4,5},{5,4},{6,7},{7,6},{8,9},{9,8},{10,11... | collective-permute-start | bytes 294920 | tf_op jit(solution)/shard_map/ppermute | solution.py:80
  50.2 14.3 %collective-permute-start.8 = (bf16[2,256,256]{2,1,0:T(8,128)(2,1)S(1)}, bf16[2,256,256]{2,1,0:T(8,128)(2,1)S(1)}, u32[]{:S(2)}, u32[]{:S(2)}) collective-permute-start(bf16[2,256,256]{2,1,0:T(8,128)(2,1)S(1)} %get-tuple-element.33), channel_id=1, source_target_pairs={{0,1},{1,0},{2,3},{3,2},{4,5},{5,4},{6,7},{7,6},{8,9},{9,8},{10,11... | collective-permute-start | bytes 786440 | tf_op jit(solution)/shard_map/ppermute | solution.py:80
  55.1 9.5 %collective-permute-start.14 = (bf16[192,256]{1,0:T(8,128)(2,1)S(1)}, bf16[192,256]{1,0:T(8,128)(2,1)S(1)}, u32[]{:S(2)}, u32[]{:S(2)}) collective-permute-start(bf16[192,256]{1,0:T(8,128)(2,1)S(1)} %add_convert_fusion.3), channel_id=1, source_target_pairs={{0,2},{1,3},{2,0},{3,1},{4,6},{5,7},{6,4},{7,5},{8,10},{9,11},{10,... | collective-permute-start | bytes 294920 | tf_op jit(solution)/shard_map/ppermute | solution.py:80
  61.0 11.0 %collective-permute-start.4 = (bf16[1,256,256]{2,1,0:T(8,128)(2,1)S(1)}, bf16[1,256,256]{2,1,0:T(8,128)(2,1)S(1)}, u32[]{:S(2)}, u32[]{:S(2)}) collective-permute-start(bf16[1,256,256]{2,1,0:T(8,128)(2,1)S(1)} %fusion.29), channel_id=1, source_target_pairs={{0,4},{1,5},{2,6},{3,7},{4,0},{5,1},{6,2},{7,3},{8,12},{9,13},{10,... | collective-permute-start | bytes 393224 | tf_op jit(solution)/shard_map/ppermute | solution.py:80
  64.6 4.7 %collective-permute-start.15 = (bf16[192,256]{1,0:T(8,128)(2,1)S(1)}, bf16[192,256]{1,0:T(8,128)(2,1)S(1)}, u32[]{:S(2)}, u32[]{:S(2)}) collective-permute-start(bf16[192,256]{1,0:T(8,128)(2,1)S(1)} %add_convert_fusion.2), channel_id=1, source_target_pairs={{0,16},{1,17},{2,18},{3,19},{4,20},{5,21},{6,22},{7,23},{8,24},{9,... | collective-permute-start | bytes 294920 | tf_op jit(solution)/shard_map/ppermute | solution.py:83
  64.7 8.7 %collective-permute-start.9 = (bf16[1,256,256]{2,1,0:T(8,128)(2,1)S(1)}, bf16[1,256,256]{2,1,0:T(8,128)(2,1)S(1)}, u32[]{:S(2)}, u32[]{:S(2)}) collective-permute-start(bf16[1,256,256]{2,1,0:T(8,128)(2,1)S(1)} %fusion.28), channel_id=1, source_target_pairs={{0,4},{1,5},{2,6},{3,7},{4,0},{5,1},{6,2},{7,3},{8,12},{9,13},{10,... | collective-permute-start | bytes 393224 | tf_op jit(solution)/shard_map/ppermute | solution.py:80
  72.0 2.3 %collective-permute-start.16 = (bf16[384,256]{1,0:T(8,128)(2,1)S(1)}, bf16[384,256]{1,0:T(8,128)(2,1)S(1)}, u32[]{:S(2)}, u32[]{:S(2)}) collective-permute-start(bf16[384,256]{1,0:T(8,128)(2,1)S(1)} %pad_maximum_fusion.2), channel_id=1, source_target_pairs={{0,8},{1,9},{2,10},{3,11},{4,12},{5,13},{6,14},{7,15},{8,0},{9,1},... | collective-permute-start | bytes 589832 | tf_op jit(solution)/shard_map/ppermute | solution.py:83
  72.0 5.3 %copy-start = (bf16[1,256,256]{2,1,0:T(8,128)(2,1)}, bf16[1,256,256]{2,1,0:T(8,128)(2,1)S(1)}, u32[]{:S(2)}) copy-start(bf16[1,256,256]{2,1,0:T(8,128)(2,1)S(1)} %fusion.32) | copy-start | bytes 393220

commit v3 on v2

--- a/solution.py
+++ b/solution.py
@@ -13,7 +13,10 @@
     return lax.dot_general(a, b, (((0,), (0,)), ((), ())), preferred_element_type=F32)
 
 
-def diagonal_kernel(sums, link, inverse_one, inverse_two, diag_one, cross, diag_two):
+def diagonal_kernel(place, mine, other, link, inverse_one, inverse_two, diag_one, cross, diag_two):
+    low = place[0] == 0
+    low, high = jnp.where(low, mine[...], other[...]), jnp.where(low, other[...], mine[...])
+    sums = jnp.concatenate([low, high]).reshape(3, *link.shape)
     diag_one[...] = (inverse_one[...] + sums[0].astype(F32)).astype(BF16)
     step = jnp.dot(diag_one[...], link[...], preferred_element_type=F32)
     cross[...] = (sums[1].astype(F32) - step).astype(BF16)
@@ -82,23 +85,17 @@
     def swap_rows(array, bit):
         return lax.ppermute(array, BOTH, [(at(r, c), at(r ^ (1 << bit), c)) for r, c in everyone])
 
-    def pick(array, bits_left, bit, other):
-        lower = 1 << bits_left.index(bit)
-        split = array.reshape(-1, 2, lower, tile, tile)
-        return lax.dynamic_slice_in_dim(split, (col >> bit & 1) ^ other, 1, 1).reshape(-1, tile, tile).astype(F32)
+    def pick(array, bit, other):
+        split = array.reshape(-1, 2, tile, tile)
+        return lax.dynamic_slice_in_dim(split, (col >> bit & 1) ^ other, 1, 1)[:, 0].astype(F32)
 
-    def first_swap(array, order):
-        left = list(range(bits))
-        away, keep = (pick(array, left, order[0], other) for other in (1, 0))
-        left.remove(order[0])
-        return left, keep, [swap(away.astype(BF16), order[0])]
+    def first_swap(array, *earlier):
+        away, keep = (pick(array, 0, other) for other in (1, 0))
+        return keep, [swap(after(away.astype(BF16), *earlier), 0)]
 
-    def next_swap(left, keep, arrived, order):
-        bit = order[len(arrived)]
-        away, keep = (
-            pick(keep, left, bit, other) + pick(arrived[-1], left, bit, other) for other in (1, 0)
-        )
-        left.remove(bit)
+    def next_swap(keep, arrived):
+        bit = len(arrived)
+        away, keep = (pick(keep, bit, other) + pick(arrived[-1], bit, other) for other in (1, 0))
         arrived.append(swap(away.astype(BF16), bit))
         return keep
 
@@ -122,19 +119,17 @@
 
     piece_one, piece_two = (part_of(f, col % group * cols, cols) for f in (factor_one, factor_two))
     piece_one, piece_two = after(piece_one), after(piece_two)
-    order_one, order_two = list(range(bits)), [1, 0, *range(2, bits)]
     have_one, have_two = over_chips(piece_one, *marks, flags_one, flags_two), over_chips(piece_two)
     all_one = products(marks[0], over_cores(have_one))
-    left_one, keep_one, one = first_swap(all_one, order_one)
+    keep_one, one = first_swap(all_one)
     all_two = products(marks[1], over_cores(after(have_two, all_one)))
-    left_two, keep_two, two = first_swap(all_two, order_two)
+    keep_two, two = first_swap(all_two, one[0])
     sums = contraction(first, all_one), contraction(all_one, second_in_one), contraction(second, all_two)
     for _ in range(1, bits):
-        keep_one = next_swap(left_one, keep_one, one, order_one)
-        keep_two = next_swap(left_two, keep_two, two, order_two)
+        keep_one = next_swap(keep_one, one)
+        keep_two = next_swap(keep_two, two)
 
     sums = jnp.stack(sums)
-    shape = sums.shape
     part = sums.reshape(-1, tile)
     for bit in range(row_bits):
         half = part.shape[0] // 2
@@ -142,21 +137,27 @@
         got = swap_rows(lax.dynamic_slice_in_dim(part, (1 - mine) * half, half, 0).astype(BF16), bit)
         part = lax.dynamic_slice_in_dim(part, mine * half, half, 0) + got.astype(F32)
     part = part.astype(BF16)
-    gates = [one[0], two[0], *one[1:]]
-    for bit, gate in zip((*range(2, bits), 0, 1), gates):
+    gates = [one[0], *one[1:-1], two[0]]
+    for bit, gate in zip(reversed(range(bits)), gates):
         got = swap(after(part, gate), bit)
         part = (part.astype(F32) + got.astype(F32)).astype(BF16)
     for bit in reversed(range(row_bits)):
-        got = swap_rows(after(part, one[-1] if bit == 0 else two[-2]), bit)
-        low = (row >> bit & 1) == 0
-        part = jnp.concatenate([jnp.where(low, part, got), jnp.where(low, got, part)])
+        got = swap_rows(after(part, *((one[-1], two[-2]) if bit == 0 else ())), bit)
+        if bit:
+            low = (row >> bit & 1) == 0
+            part = jnp.concatenate([jnp.where(low, part, got), jnp.where(low, got, part)])
 
     member_one, member_two = (m[row * rows + col].astype(F32) for m in (member_one, member_two))
     column_one = (-member_one * (keep_one[0] + one[-1][0].astype(F32))).astype(BF16)
     linked = jnp.dot(column_one, link_block, preferred_element_type=F32) + keep_two[0]
     column_two = (-member_two * (linked + two[-1][0].astype(F32))).astype(BF16)
     diag_one, cross_block, diag_two = small_kernel(
-        diagonal_kernel, 3, 3, tile, (part.reshape(shape), link_block, inverse_one, inverse_two)
+        diagonal_kernel,
+        3,
+        3,
+        tile,
+        ((row & 1)[None], part, got, link_block, inverse_one, inverse_two),
+        1,
     )
     return (column_one[None], column_two[None], diag_one, cross_block, diag_two)
 

time: 77.8 us -> 77.6 us (level)
  starting transfers between devices: 25.9 us -> 27.8 us
  waiting for transfers between devices: 29.4 us -> 27.5 us
  other arithmetic: 3.23 us -> 2.37 us
    ppermute x9, waiting for transfers between devices: 23.1 us -> 20.6 us  [swap(): lax.ppermute(array, BOTH, [(at(r, c), at(r, c ^ 1 << bit)) for r, c in ev...]
    ppermute x9, starting transfers between devices: 14.2 us -> 15.3 us  [swap(): lax.ppermute(array, BOTH, [(at(r, c), at(r, c ^ 1 << bit)) for r, c in ev...]
    concatenate x2 -> x1, other arithmetic: 0.8 us -> 0.02 us  [shards(): jnp.concatenate([jnp.where(low, part, got), jnp.where(low, got, part)])]
  transfers between devices with their start and end apart: 17 -> 17, of which waited for: 11 -> 9; matrix products, arithmetic and copies ran while one was open for 15% -> 15% of each run, Pallas kernels for 0% -> 0%
where the time goes in v3:
time: 77.6 us; the launch traced here: 77.2 us
  starting transfers between devices  27.8 us (36%)
  waiting for transfers between devices  27.5 us (35%)
  matrix products  7.62 us (10%)
  local copies, waits for them, and re-layouts  7.2 us (9%)
  between operations  2.41 us (3%)
  other arithmetic  2.37 us (3%)
  Pallas kernels  2.33 us (3%)
    ppermute x9, waiting for transfers between devices, swap(): lax.ppermute(array, BOTH, [(at(r, c), at(r, c ^ 1 << bit)) for r, c in ev...  20.6 us
    ppermute x9, starting transfers between devices, swap(): lax.ppermute(array, BOTH, [(at(r, c), at(r, c ^ 1 << bit)) for r, c in ev...  15.3 us
    ppermute x2, starting transfers between devices, over_chips(): got = after(lax.ppermute(piece, BOTH, perm), *earlier)  6.23 us
    ppermute x4, waiting for transfers between devices, swap_rows(): lax.ppermute(array, BOTH, [(at(r, c), at(r ^ 1 << bit, c)) for r, c in ev...  5.41 us
    dot_general x2, matrix products, products(): jnp.einsum('ijab,jbc->iac', kept, column, preferred_element_type=F32)  4.9 us
    dynamic_slice x4, local copies, waits for them, and re-layouts, part_of(): return lax.dynamic_slice_in_dim(array, start, size, 0)  3.62 us
    ppermute x4, starting transfers between devices, swap_rows(): lax.ppermute(array, BOTH, [(at(r, c), at(r ^ 1 << bit, c)) for r, c in ev...  3.46 us
    ppermute x2, starting transfers between devices, over_cores(): lax.ppermute(have, BOTH, perm)  2.78 us
  transfers between devices with their start and end apart: 17, of which 9 were waited for; matrix products, arithmetic and copies ran while one was open for 15% of the time, Pallas kernels for 0%

profile of v3, /device:TPU:0, one launch (start us, length us, event | category | flops | bytes accessed | tf_op | source)
XLA Modules:
  0.0 77.2 jit_solution(3348875912060197780)
XLA Ops:
  0.6 1.1 %constant_dynamic-slice_fusion.3 = bf16[4,256,256]{2,1,0:T(8,128)(2,1)S(1)} fusion(bf16[8,256,256]{2,1,0:T(8,128)(2,1)} %param.13, s32[]{:T(128)S(6)} %select_n.145), kind=kLoop, calls=%fused_computation.69 | loop fusion | bytes 1048580 | tf_op jit(solution)/shard_map/dynamic_slice | solution.py:103
  1.7 4.9 %collective-permute-start = (bf16[4,256,256]{2,1,0:T(8,128)(2,1)S(1)}, bf16[4,256,256]{2,1,0:T(8,128)(2,1)S(1)}, u32[]{:S(2)}, u32[]{:S(2)}) collective-permute-start(bf16[4,256,256]{2,1,0:T(8,128)(2,1)S(1)} %constant_dynamic-slice_fusion.3), channel_id=1, source_target_pairs={{0,16},{1,17},{10,26},{11,27},{20,4},{21,5},{30,14},{31,15}} | collective-permute-start | bytes 1572872 | tf_op jit(solution)/shard_map/ppermute | solution.py:70
  6.6 1.1 %constant_dynamic-slice_fusion.1 = bf16[4,256,256]{2,1,0:T(8,128)(2,1)S(1)} fusion(bf16[8,256,256]{2,1,0:T(8,128)(2,1)} %param.14, s32[]{:T(128)S(6)} %select_n.145), kind=kLoop, calls=%fused_computation.67 | loop fusion | bytes 1048580 | tf_op jit(solution)/shard_map/dynamic_slice | solution.py:103
  7.7 1.3 %collective-permute-start.5 = (bf16[4,256,256]{2,1,0:T(8,128)(2,1)S(1)}, bf16[4,256,256]{2,1,0:T(8,128)(2,1)S(1)}, u32[]{:S(2)}, u32[]{:S(2)}) collective-permute-start(bf16[4,256,256]{2,1,0:T(8,128)(2,1)S(1)} %constant_dynamic-slice_fusion.1), channel_id=1, source_target_pairs={{0,16},{1,17},{10,26},{11,27},{20,4},{21,5},{30,14},{31,15}} | collective-permute-start | bytes 1572872 | tf_op jit(solution)/shard_map/ppermute | solution.py:70
  9.1 0.7 dynamic_slice.81
  9.8 0.7 dynamic_slice.83
  10.6 0.7 broadcast_compare_fusion.2
  11.3 0.8 broadcast_compare_fusion
  12.1 1.2 %collective-permute-done = bf16[4,256,256]{2,1,0:T(8,128)(2,1)S(1)} collective-permute-done((bf16[4,256,256]{2,1,0:T(8,128)(2,1)S(1)}, bf16[4,256,256]{2,1,0:T(8,128)(2,1)S(1)}, u32[]{:S(2)}, u32[]{:S(2)}) %collective-permute-start) | collective-permute-done | bytes 524320 | tf_op jit(solution)/shard_map/ppermute | solution.py:70
  13.4 1.3 %collective-permute-start.1 = (bf16[4,256,256]{2,1,0:T(8,128)(2,1)S(1)}, bf16[4,256,256]{2,1,0:T(8,128)(2,1)S(1)}, u32[]{:S(2)}, u32[]{:S(2)}) collective-permute-start(bf16[4,256,256]{2,1,0:T(8,128)(2,1)S(1)} %broadcast_select_fusion.2), channel_id=1, source_target_pairs={{0,8},{1,9},{10,2},{11,3},{4,12},{5,13},{14,6},{15,7},{16,24},{17,... | collective-permute-start | bytes 1572872 | tf_op jit(solution)/shard_map/ppermute | solution.py:80
  14.7 1.2 %dynamic_slice.80 = s32[1]{0:T(128)} dynamic-slice(s32[32]{0:T(128)} %param.11, s32[]{:T(128)S(6)} %select_n.136), dynamic_slice_sizes={1} | dynamic-slice | bytes 12 | tf_op jit(solution)/shard_map/dynamic_slice | solution.py:150
  16.0 1.2 %dynamic_slice.92 = s32[1]{0:T(128)} dynamic-slice(s32[32]{0:T(128)} %param.12, s32[]{:T(128)S(6)} %select_n.136), dynamic_slice_sizes={1} | dynamic-slice | bytes 12 | tf_op jit(solution)/shard_map/dynamic_slice | solution.py:150
  19.0 3.6 %bitcast_convert_fusion.1 = bf16[8,256,256]{2,1,0:T(8,128)(2,1)S(1)} fusion(bf16[8,4,256,256]{3,2,1,0:T(8,128)(2,1)} %param.9, pred[8,4]{1,0:T(8,128)(4,1)S(1)} %copy.19, bf16[4,256,256]{2,1,0:T(8,128)(2,1)S(1)} %broadcast_select_fusion.2, bf16[4,256,256]{2,1,0:T(8,128)(2,1)S(1)} %collective-permute-done.1, pred[]{:T(512)S(6)} %eq.18), kind=kOutput, calls=%fused_computation.7 | convolution fusion | flops 1076625408 | bytes 6291489 | tf_op jit(solution)/shard_map/ijab,jbc->iac/dot_general | solution.py:110
  22.6 1.5 %collective-permute-start.6 = (bf16[4,256,256]{2,1,0:T(8,128)(2,1)S(1)}, bf16[4,256,256]{2,1,0:T(8,128)(2,1)S(1)}, u32[]{:S(2)}, u32[]{:S(2)}) collective-permute-start(bf16[4,256,256]{2,1,0:T(8,128)(2,1)S(1)} %broadcast_select_fusion.1), channel_id=1, source_target_pairs={{0,8},{1,9},{10,2},{11,3},{4,12},{5,13},{14,6},{15,7},{16,24},{17,... | collective-permute-start | bytes 1572872 | tf_op jit(solution)/shard_map/ppermute | solution.py:80
  24.1 1.6 %collective-permute-start.2 = (bf16[4,256,256]{2,1,0:T(8,128)(2,1)S(1)}, bf16[4,256,256]{2,1,0:T(8,128)(2,1)S(1)}, u32[]{:S(2)}, u32[]{:S(2)}) collective-permute-start(bf16[4,256,256]{2,1,0:T(8,128)(2,1)S(1)} %get-tuple-element.37), channel_id=1, source_target_pairs={{0,1},{1,0},{2,3},{3,2},{4,5},{5,4},{6,7},{7,6},{8,9},{9,8},{10,11... | collective-permute-start | bytes 1572872 | tf_op jit(solution)/shard_map/ppermute | solution.py:83
  26.9 1.3 %bitcast_convert_fusion = bf16[8,256,256]{2,1,0:T(8,128)(2,1)S(1)} fusion(bf16[8,4,256,256]{3,2,1,0:T(8,128)(2,1)S(1)} %copy-done.6, pred[8,4]{1,0:T(8,128)(4,1)S(1)} %copy.21, bf16[4,256,256]{2,1,0:T(8,128)(2,1)S(1)} %broadcast_select_fusion.1, bf16[4,256,256]{2,1,0:T(8,128)(2,1)S(1)} %collective-permute-done.6, pred[]{:T(512)S(6)} %eq.18), kind=kOutput, calls=%fused_computation.6 | convolution fusion | flops 1076625408 | bytes 6291489 | tf_op jit(solution)/shard_map/ijab,jbc->iac/dot_general | solution.py:110
  29.2 6.2 %collective-permute-done.2 = bf16[4,256,256]{2,1,0:T(8,128)(2,1)S(1)} collective-permute-done((bf16[4,256,256]{2,1,0:T(8,128)(2,1)S(1)}, bf16[4,256,256]{2,1,0:T(8,128)(2,1)S(1)}, u32[]{:S(2)}, u32[]{:S(2)}) %collective-permute-start.2) | collective-permute-done | bytes 524320 | tf_op jit(solution)/shard_map/ppermute | solution.py:83
  35.8 2.5 %collective-permute-start.11 = (bf16[192,256]{1,0:T(8,128)(2,1)S(1)}, bf16[192,256]{1,0:T(8,128)(2,1)S(1)}, u32[]{:S(2)}, u32[]{:S(2)}) collective-permute-start(bf16[192,256]{1,0:T(8,128)(2,1)S(1)} %dynamic-slice_convert_fusion.1), channel_id=1, source_target_pairs={{0,16},{1,17},{2,18},{3,19},{4,20},{5,21},{6,22},{7,23},{8,24},{9,... | collective-permute-start | bytes 294920 | tf_op jit(solution)/shard_map/ppermute | solution.py:86
  38.4 1.6 %collective-permute-start.7 = (bf16[4,256,256]{2,1,0:T(8,128)(2,1)S(1)}, bf16[4,256,256]{2,1,0:T(8,128)(2,1)S(1)}, u32[]{:S(2)}, u32[]{:S(2)}) collective-permute-start(bf16[4,256,256]{2,1,0:T(8,128)(2,1)S(1)} %get-tuple-element.17), channel_id=1, source_target_pairs={{0,1},{1,0},{2,3},{3,2},{4,5},{5,4},{6,7},{7,6},{8,9},{9,8},{10,11... | collective-permute-start | bytes 1572872 | tf_op jit(solution)/shard_map/ppermute | solution.py:83
  40.0 1.6 %collective-permute-done.11 = bf16[192,256]{1,0:T(8,128)(2,1)S(1)} collective-permute-done((bf16[192,256]{1,0:T(8,128)(2,1)S(1)}, bf16[192,256]{1,0:T(8,128)(2,1)S(1)}, u32[]{:S(2)}, u32[]{:S(2)}) %collective-permute-start.11) | collective-permute-done | bytes 98336 | tf_op jit(solution)/shard_map/ppermute | solution.py:86
  41.5 2.9 %collective-permute-start.12 = (bf16[192,256]{1,0:T(8,128)(2,1)S(1)}, bf16[192,256]{1,0:T(8,128)(2,1)S(1)}, u32[]{:S(2)}, u32[]{:S(2)}) collective-permute-start(bf16[192,256]{1,0:T(8,128)(2,1)S(1)} %add_convert_fusion.4), channel_id=1, source_target_pairs={{0,4},{1,5},{2,6},{3,7},{4,0},{5,1},{6,2},{7,3},{8,12},{9,13},{10,... | collective-permute-start | bytes 294920 | tf_op jit(solution)/shard_map/ppermute | solution.py:83
  44.5 4.2 %collective-permute-done.12 = bf16[192,256]{1,0:T(8,128)(2,1)S(1)} collective-permute-done((bf16[192,256]{1,0:T(8,128)(2,1)S(1)}, bf16[192,256]{1,0:T(8,128)(2,1)S(1)}, u32[]{:S(2)}, u32[]{:S(2)}) %collective-permute-start.12) | collective-permute-done | bytes 98336 | tf_op jit(solution)/shard_map/ppermute | solution.py:83
  49.2 3.6 %collective-permute-start.4 = (bf16[1,256,256]{2,1,0:T(8,128)(2,1)S(1)}, bf16[1,256,256]{2,1,0:T(8,128)(2,1)S(1)}, u32[]{:S(2)}, u32[]{:S(2)}) collective-permute-start(bf16[1,256,256]{2,1,0:T(8,128)(2,1)S(1)} %fusion.30), channel_id=1, source_target_pairs={{0,4},{1,5},{2,6},{3,7},{4,0},{5,1},{6,2},{7,3},{8,12},{9,13},{10,... | collective-permute-start | bytes 393224 | tf_op jit(solution)/shard_map/ppermute | solution.py:83
  53.5 1.6 %collective-permute-start.14 = (bf16[192,256]{1,0:T(8,128)(2,1)S(1)}, bf16[192,256]{1,0:T(8,128)(2,1)S(1)}, u32[]{:S(2)}, u32[]{:S(2)}) collective-permute-start(bf16[192,256]{1,0:T(8,128)(2,1)S(1)} %add_convert_fusion.2), channel_id=1, source_target_pairs={{0,1},{1,0},{2,3},{3,2},{4,5},{5,4},{6,7},{7,6},{8,9},{9,8},{10,11... | collective-permute-start | bytes 294920 | tf_op jit(solution)/shard_map/ppermute | solution.py:83
  55.5 2.6 %collective-permute-done.14 = bf16[192,256]{1,0:T(8,128)(2,1)S(1)} collective-permute-done((bf16[192,256]{1,0:T(8,128)(2,1)S(1)}, bf16[192,256]{1,0:T(8,128)(2,1)S(1)}, u32[]{:S(2)}, u32[]{:S(2)}) %collective-permute-start.14) | collective-permute-done | bytes 98336 | tf_op jit(solution)/shard_map/ppermute | solution.py:83
  58.2 0.8 %collective-permute-start.15 = (bf16[192,256]{1,0:T(8,128)(2,1)S(1)}, bf16[192,256]{1,0:T(8,128)(2,1)S(1)}, u32[]{:S(2)}, u32[]{:S(2)}) collective-permute-start(bf16[192,256]{1,0:T(8,128)(2,1)S(1)} %add_convert_fusion.1), channel_id=1, source_target_pairs={{0,16},{1,17},{2,18},{3,19},{4,20},{5,21},{6,22},{7,23},{8,24},{9,... | collective-permute-start | bytes 294920 | tf_op jit(solution)/shard_map/ppermute | solution.py:86
  59.0 3.9 %collective-permute-done.15 = bf16[192,256]{1,0:T(8,128)(2,1)S(1)} collective-permute-done((bf16[192,256]{1,0:T(8,128)(2,1)S(1)}, bf16[192,256]{1,0:T(8,128)(2,1)S(1)}, u32[]{:S(2)}, u32[]{:S(2)}) %collective-permute-start.15) | collective-permute-done | bytes 98336 | tf_op jit(solution)/shard_map/ppermute | solution.py:86
  63.1 3.3 %collective-permute-start.9 = (bf16[1,256,256]{2,1,0:T(8,128)(2,1)S(1)}, bf16[1,256,256]{2,1,0:T(8,128)(2,1)S(1)}, u32[]{:S(2)}, u32[]{:S(2)}) collective-permute-start(bf16[1,256,256]{2,1,0:T(8,128)(2,1)S(1)} %fusion.29), channel_id=1, source_target_pairs={{0,4},{1,5},{2,6},{3,7},{4,0},{5,1},{6,2},{7,3},{8,12},{9,13},{10,... | collective-permute-start | bytes 393224 | tf_op jit(solution)/shard_map/ppermute | solution.py:83
  66.4 6.9 %collective-permute-done.9 = bf16[1,256,256]{2,1,0:T(8,128)(2,1)S(1)} collective-permute-done((bf16[1,256,256]{2,1,0:T(8,128)(2,1)S(1)}, bf16[1,256,256]{2,1,0:T(8,128)(2,1)S(1)}, u32[]{:S(2)}, u32[]{:S(2)}) %collective-permute-start.9) | collective-permute-done | bytes 131104 | tf_op jit(solution)/shard_map/ppermute | solution.py:83
  73.3 0.9 %fusion.34 = bf16[1,256,256]{2,1,0:T(8,128)(2,1)} fusion(f32[2,1,256,256]{3,2,1,0:T(8,128)S(1)} %convert_add_fusion, s32[]{:T(128)S(6)} %select_n.152, bf16[1,256,256]{2,1,0:T(8,128)(2,1)S(1)} %collective-permute-done.9, bf16[256,256]{1,0:T(8,128)(2,1)S(1)} %copy-done.2, bf16[1,256,256]{2,1,0:T(8,128)(2,1)S(1)} %fusion.33, ...), kind=kOutput, calls=%fused_computation.61 | convolution fusion | flops 34013184 | bytes 917512 | tf_op jit(solution)/shard_map/dot_general | solution.py:152
  74.2 0.7 copy-done.5
  74.9 2.3 %shard_map.128 = (bf16[256,256]{1,0:T(8,128)(2,1)}, bf16[256,256]{1,0:T(8,128)(2,1)}, bf16[256,256]{1,0:T(8,128)(2,1)}) custom-call(s32[1]{0:T(128)} %bitcast.28.place, bf16[384,256]{1,0:T(8,128)(2,1)} %copy-done, bf16[384,256]{1,0:T(8,128)(2,1)} %copy-done.5, bf16[256,256]{1,0:T(8,128)(2,1)} %link.1, f32[256,256]{1,0:T(8,128)} %inverse_one.1, ...), custom_call_target="tpu_custom_call" | custom-call | flops 100663296 | bytes 1572864 | tf_op jit(solution)/shard_map/pallas_call | solution.py:29
  (55 shorter events, 5.1 us)
Async XLA Ops:
  1.7 11.6 %collective-permute-start = (bf16[4,256,256]{2,1,0:T(8,128)(2,1)S(1)}, bf16[4,256,256]{2,1,0:T(8,128)(2,1)S(1)}, u32[]{:S(2)}, u32[]{:S(2)}) collective-permute-start(bf16[4,256,256]{2,1,0:T(8,128)(2,1)S(1)} %constant_dynamic-slice_fusion.3), channel_id=1, source_target_pairs={{0,16},{1,17},{10,26},{11,27},{20,4},{21,5},{30,14},{31,15}} | collective-permute-start | bytes 1572872 | tf_op jit(solution)/shard_map/ppermute | solution.py:70
  7.7 11.2 %collective-permute-start.5 = (bf16[4,256,256]{2,1,0:T(8,128)(2,1)S(1)}, bf16[4,256,256]{2,1,0:T(8,128)(2,1)S(1)}, u32[]{:S(2)}, u32[]{:S(2)}) collective-permute-start(bf16[4,256,256]{2,1,0:T(8,128)(2,1)S(1)} %constant_dynamic-slice_fusion.1), channel_id=1, source_target_pairs={{0,16},{1,17},{10,26},{11,27},{20,4},{21,5},{30,14},{31,15}} | collective-permute-start | bytes 1572872 | tf_op jit(solution)/shard_map/ppermute | solution.py:70
  13.4 5.6 %collective-permute-start.1 = (bf16[4,256,256]{2,1,0:T(8,128)(2,1)S(1)}, bf16[4,256,256]{2,1,0:T(8,128)(2,1)S(1)}, u32[]{:S(2)}, u32[]{:S(2)}) collective-permute-start(bf16[4,256,256]{2,1,0:T(8,128)(2,1)S(1)} %broadcast_select_fusion.2), channel_id=1, source_target_pairs={{0,8},{1,9},{10,2},{11,3},{4,12},{5,13},{14,6},{15,7},{16,24},{17,... | collective-permute-start | bytes 1572872 | tf_op jit(solution)/shard_map/ppermute | solution.py:80
  19.0 6.7 %copy-start.3 = (bf16[8,256,256]{2,1,0:T(8,128)(2,1)S(1)}, bf16[8,256,256]{2,1,0:T(8,128)(2,1)}, u32[]{:S(2)}) copy-start(bf16[8,256,256]{2,1,0:T(8,128)(2,1)} %param.13) | copy-start | bytes 3145732
  22.6 3.8 %copy-start.4 = (bf16[8,256,256]{2,1,0:T(8,128)(2,1)S(1)}, bf16[8,256,256]{2,1,0:T(8,128)(2,1)}, u32[]{:S(2)}) copy-start(bf16[8,256,256]{2,1,0:T(8,128)(2,1)} %param.14) | copy-start | bytes 3145732
  22.6 4.3 %collective-permute-start.6 = (bf16[4,256,256]{2,1,0:T(8,128)(2,1)S(1)}, bf16[4,256,256]{2,1,0:T(8,128)(2,1)S(1)}, u32[]{:S(2)}, u32[]{:S(2)}) collective-permute-start(bf16[4,256,256]{2,1,0:T(8,128)(2,1)S(1)} %broadcast_select_fusion.1), channel_id=1, source_target_pairs={{0,8},{1,9},{10,2},{11,3},{4,12},{5,13},{14,6},{15,7},{16,24},{17,... | collective-permute-start | bytes 1572872 | tf_op jit(solution)/shard_map/ppermute | solution.py:80
  24.0 2.9 %copy-start.6 = (bf16[8,4,256,256]{3,2,1,0:T(8,128)(2,1)S(1)}, bf16[8,4,256,256]{3,2,1,0:T(8,128)(2,1)}, u32[]{:S(2)}) copy-start(bf16[8,4,256,256]{3,2,1,0:T(8,128)(2,1)} %param.9) | copy-start | bytes 12582916
  24.1 11.3 %collective-permute-start.2 = (bf16[4,256,256]{2,1,0:T(8,128)(2,1)S(1)}, bf16[4,256,256]{2,1,0:T(8,128)(2,1)S(1)}, u32[]{:S(2)}, u32[]{:S(2)}) collective-permute-start(bf16[4,256,256]{2,1,0:T(8,128)(2,1)S(1)} %get-tuple-element.37), channel_id=1, source_target_pairs={{0,1},{1,0},{2,3},{3,2},{4,5},{5,4},{6,7},{7,6},{8,9},{9,8},{10,11... | collective-permute-start | bytes 1572872 | tf_op jit(solution)/shard_map/ppermute | solution.py:83
  29.1 6.6 %collective-permute-start.10 = (bf16[384,256]{1,0:T(8,128)(2,1)S(1)}, bf16[384,256]{1,0:T(8,128)(2,1)S(1)}, u32[]{:S(2)}, u32[]{:S(2)}) collective-permute-start(bf16[384,256]{1,0:T(8,128)(2,1)S(1)} %dynamic-slice_convert_fusion), channel_id=1, source_target_pairs={{0,8},{1,9},{2,10},{3,11},{4,12},{5,13},{6,14},{7,15},{8,0},{9,1},... | collective-permute-start | bytes 589832 | tf_op jit(solution)/shard_map/ppermute | solution.py:86
  35.6 13.1 %collective-permute-start.3 = (bf16[2,256,256]{2,1,0:T(8,128)(2,1)S(1)}, bf16[2,256,256]{2,1,0:T(8,128)(2,1)S(1)}, u32[]{:S(2)}, u32[]{:S(2)}) collective-permute-start(bf16[2,256,256]{2,1,0:T(8,128)(2,1)S(1)} %get-tuple-element.33), channel_id=1, source_target_pairs={{0,2},{1,3},{2,0},{3,1},{4,6},{5,7},{6,4},{7,5},{8,10},{9,11},{10,... | collective-permute-start | bytes 786440 | tf_op jit(solution)/shard_map/ppermute | solution.py:83
  35.8 5.7 %collective-permute-start.11 = (bf16[192,256]{1,0:T(8,128)(2,1)S(1)}, bf16[192,256]{1,0:T(8,128)(2,1)S(1)}, u32[]{:S(2)}, u32[]{:S(2)}) collective-permute-start(bf16[192,256]{1,0:T(8,128)(2,1)S(1)} %dynamic-slice_convert_fusion.1), channel_id=1, source_target_pairs={{0,16},{1,17},{2,18},{3,19},{4,20},{5,21},{6,22},{7,23},{8,24},{9,... | collective-permute-start | bytes 294920 | tf_op jit(solution)/shard_map/ppermute | solution.py:86
  38.4 34.9 %copy-start.2 = (bf16[256,256]{1,0:T(8,128)(2,1)S(1)}, bf16[256,256]{1,0:T(8,128)(2,1)}, u32[]{:S(2)}) copy-start(bf16[256,256]{1,0:T(8,128)(2,1)} %link.1) | copy-start | bytes 393220
  38.4 15.1 %collective-permute-start.7 = (bf16[4,256,256]{2,1,0:T(8,128)(2,1)S(1)}, bf16[4,256,256]{2,1,0:T(8,128)(2,1)S(1)}, u32[]{:S(2)}, u32[]{:S(2)}) collective-permute-start(bf16[4,256,256]{2,1,0:T(8,128)(2,1)S(1)} %get-tuple-element.17), channel_id=1, source_target_pairs={{0,1},{1,0},{2,3},{3,2},{4,5},{5,4},{6,7},{7,6},{8,9},{9,8},{10,11... | collective-permute-start | bytes 1572872 | tf_op jit(solution)/shard_map/ppermute | solution.py:83
  41.5 7.2 %collective-permute-start.12 = (bf16[192,256]{1,0:T(8,128)(2,1)S(1)}, bf16[192,256]{1,0:T(8,128)(2,1)S(1)}, u32[]{:S(2)}, u32[]{:S(2)}) collective-permute-start(bf16[192,256]{1,0:T(8,128)(2,1)S(1)} %add_convert_fusion.4), channel_id=1, source_target_pairs={{0,4},{1,5},{2,6},{3,7},{4,0},{5,1},{6,2},{7,3},{8,12},{9,13},{10,... | collective-permute-start | bytes 294920 | tf_op jit(solution)/shard_map/ppermute | solution.py:83
  48.7 4.7 %collective-permute-start.13 = (bf16[192,256]{1,0:T(8,128)(2,1)S(1)}, bf16[192,256]{1,0:T(8,128)(2,1)S(1)}, u32[]{:S(2)}, u32[]{:S(2)}) collective-permute-start(bf16[192,256]{1,0:T(8,128)(2,1)S(1)} %add_convert_fusion.3), channel_id=1, source_target_pairs={{0,2},{1,3},{2,0},{3,1},{4,6},{5,7},{6,4},{7,5},{8,10},{9,11},{10,... | collective-permute-start | bytes 294920 | tf_op jit(solution)/shard_map/ppermute | solution.py:83
  49.2 13.7 %collective-permute-start.4 = (bf16[1,256,256]{2,1,0:T(8,128)(2,1)S(1)}, bf16[1,256,256]{2,1,0:T(8,128)(2,1)S(1)}, u32[]{:S(2)}, u32[]{:S(2)}) collective-permute-start(bf16[1,256,256]{2,1,0:T(8,128)(2,1)S(1)} %fusion.30), channel_id=1, source_target_pairs={{0,4},{1,5},{2,6},{3,7},{4,0},{5,1},{6,2},{7,3},{8,12},{9,13},{10,... | collective-permute-start | bytes 393224 | tf_op jit(solution)/shard_map/ppermute | solution.py:83
  53.5 4.7 %collective-permute-start.14 = (bf16[192,256]{1,0:T(8,128)(2,1)S(1)}, bf16[192,256]{1,0:T(8,128)(2,1)S(1)}, u32[]{:S(2)}, u32[]{:S(2)}) collective-permute-start(bf16[192,256]{1,0:T(8,128)(2,1)S(1)} %add_convert_fusion.2), channel_id=1, source_target_pairs={{0,1},{1,0},{2,3},{3,2},{4,5},{5,4},{6,7},{7,6},{8,9},{9,8},{10,11... | collective-permute-start | bytes 294920 | tf_op jit(solution)/shard_map/ppermute | solution.py:83
  55.1 7.8 %collective-permute-start.8 = (bf16[2,256,256]{2,1,0:T(8,128)(2,1)S(1)}, bf16[2,256,256]{2,1,0:T(8,128)(2,1)S(1)}, u32[]{:S(2)}, u32[]{:S(2)}) collective-permute-start(bf16[2,256,256]{2,1,0:T(8,128)(2,1)S(1)} %fusion.26), channel_id=1, source_target_pairs={{0,2},{1,3},{2,0},{3,1},{4,6},{5,7},{6,4},{7,5},{8,10},{9,11},{10,... | collective-permute-start | bytes 786440 | tf_op jit(solution)/shard_map/ppermute | solution.py:83
  58.2 4.7 %collective-permute-start.15 = (bf16[192,256]{1,0:T(8,128)(2,1)S(1)}, bf16[192,256]{1,0:T(8,128)(2,1)S(1)}, u32[]{:S(2)}, u32[]{:S(2)}) collective-permute-start(bf16[192,256]{1,0:T(8,128)(2,1)S(1)} %add_convert_fusion.1), channel_id=1, source_target_pairs={{0,16},{1,17},{2,18},{3,19},{4,20},{5,21},{6,22},{7,23},{8,24},{9,... | collective-permute-start | bytes 294920 | tf_op jit(solution)/shard_map/ppermute | solution.py:86
  62.9 11.3 %copy-start = (bf16[384,256]{1,0:T(8,128)(2,1)}, bf16[384,256]{1,0:T(8,128)(2,1)S(1)}, u32[]{:S(2)}) copy-start(bf16[384,256]{1,0:T(8,128)(2,1)S(1)} %pad_maximum_fusion.1.mine) | copy-start | bytes 589828
  62.9 11.2 %collective-permute-start.16 = (bf16[384,256]{1,0:T(8,128)(2,1)S(1)}, bf16[384,256]{1,0:T(8,128)(2,1)S(1)}, u32[]{:S(2)}, u32[]{:S(2)}) collective-permute-start(bf16[384,256]{1,0:T(8,128)(2,1)S(1)} %pad_maximum_fusion.1.mine), channel_id=1, source_target_pairs={{0,8},{1,9},{2,10},{3,11},{4,12},{5,13},{6,14},{7,15},{8,0},{9,1},... | collective-permute-start | bytes 589832 | tf_op jit(solution)/shard_map/ppermute | solution.py:86
  63.1 10.3 %collective-permute-start.9 = (bf16[1,256,256]{2,1,0:T(8,128)(2,1)S(1)}, bf16[1,256,256]{2,1,0:T(8,128)(2,1)S(1)}, u32[]{:S(2)}, u32[]{:S(2)}) collective-permute-start(bf16[1,256,256]{2,1,0:T(8,128)(2,1)S(1)} %fusion.29), channel_id=1, source_target_pairs={{0,4},{1,5},{2,6},{3,7},{4,0},{5,1},{6,2},{7,3},{8,12},{9,13},{10,... | collective-permute-start | bytes 393224 | tf_op jit(solution)/shard_map/ppermute | solution.py:83
  66.4 10.8 %copy-start.1 = (bf16[1,256,256]{2,1,0:T(8,128)(2,1)}, bf16[1,256,256]{2,1,0:T(8,128)(2,1)S(1)}, u32[]{:S(2)}) copy-start(bf16[1,256,256]{2,1,0:T(8,128)(2,1)S(1)} %fusion.33) | copy-start | bytes 393220
  74.2 0.7 copy-start.5

commit v4 on v3

--- a/solution.py
+++ b/solution.py
@@ -137,20 +137,16 @@
         got = swap_rows(lax.dynamic_slice_in_dim(part, (1 - mine) * half, half, 0).astype(BF16), bit)
         part = lax.dynamic_slice_in_dim(part, mine * half, half, 0) + got.astype(F32)
     part = part.astype(BF16)
-    gates = [one[0], *one[1:-1], two[0]]
+    gates = [one[0], two[0], *one[1:]]
     for bit, gate in zip(reversed(range(bits)), gates):
         got = swap(after(part, gate), bit)
         part = (part.astype(F32) + got.astype(F32)).astype(BF16)
     for bit in reversed(range(row_bits)):
-        got = swap_rows(after(part, *((one[-1], two[-2]) if bit == 0 else ())), bit)
+        got = swap_rows(after(part, one[-1] if bit == 0 else two[-2]), bit)
         if bit:
             low = (row >> bit & 1) == 0
             part = jnp.concatenate([jnp.where(low, part, got), jnp.where(low, got, part)])
 
-    member_one, member_two = (m[row * rows + col].astype(F32) for m in (member_one, member_two))
-    column_one = (-member_one * (keep_one[0] + one[-1][0].astype(F32))).astype(BF16)
-    linked = jnp.dot(column_one, link_block, preferred_element_type=F32) + keep_two[0]
-    column_two = (-member_two * (linked + two[-1][0].astype(F32))).astype(BF16)
     diag_one, cross_block, diag_two = small_kernel(
         diagonal_kernel,
         3,
@@ -159,6 +155,10 @@
         ((row & 1)[None], part, got, link_block, inverse_one, inverse_two),
         1,
     )
+    member_one, member_two = (m[row * rows + col].astype(F32) for m in (member_one, member_two))
+    column_one = (-member_one * (keep_one[0] + one[-1][0].astype(F32))).astype(BF16)
+    linked = jnp.dot(column_one, link_block, preferred_element_type=F32) + keep_two[0]
+    column_two = (-member_two * (linked + after(two[-1], diag_two)[0].astype(F32))).astype(BF16)
     return (column_one[None], column_two[None], diag_one, cross_block, diag_two)
 
 

time: 77.6 us -> 74.2 us (0.956)
  waiting for transfers between devices: 27.5 us -> 25.2 us
  starting transfers between devices: 27.8 us -> 26.6 us
    ppermute x9, waiting for transfers between devices: 20.6 us -> 18.2 us  [swap(): lax.ppermute(array, BOTH, [(at(r, c), at(r, c ^ 1 << bit)) for r, c in ev...]
    ppermute x9, starting transfers between devices: 15.3 us -> 13 us  [swap(): lax.ppermute(array, BOTH, [(at(r, c), at(r, c ^ 1 << bit)) for r, c in ev...]
    ppermute x4, starting transfers between devices: 3.46 us -> 4.67 us  [swap_rows(): lax.ppermute(array, BOTH, [(at(r, c), at(r ^ 1 << bit, c)) for r, c in ev...]
  transfers between devices with their start and end apart: 17 -> 17, of which waited for: 9 -> 9; matrix products, arithmetic and copies ran while one was open for 15% -> 15% of each run, Pallas kernels for 0% -> 3%
where the time goes in v4:
time: 74.2 us; the launch traced here: 73.8 us
  starting transfers between devices  26.6 us (36%)
  waiting for transfers between devices  25.2 us (34%)
  matrix products  7.62 us (10%)
  local copies, waits for them, and re-layouts  7.21 us (10%)
  between operations  2.41 us (3%)
  other arithmetic  2.38 us (3%)
  Pallas kernels  2.32 us (3%)
    ppermute x9, waiting for transfers between devices, swap(): lax.ppermute(array, BOTH, [(at(r, c), at(r, c ^ 1 << bit)) for r, c in ev...  18.2 us
    ppermute x9, starting transfers between devices, swap(): lax.ppermute(array, BOTH, [(at(r, c), at(r, c ^ 1 << bit)) for r, c in ev...  13 us
    ppermute x2, starting transfers between devices, over_chips(): got = after(lax.ppermute(piece, BOTH, perm), *earlier)  6.23 us
    ppermute x4, waiting for transfers between devices, swap_rows(): lax.ppermute(array, BOTH, [(at(r, c), at(r ^ 1 << bit, c)) for r, c in ev...  5.59 us
    dot_general x2, matrix products, products(): jnp.einsum('ijab,jbc->iac', kept, column, preferred_element_type=F32)  4.9 us
    ppermute x4, starting transfers between devices, swap_rows(): lax.ppermute(array, BOTH, [(at(r, c), at(r ^ 1 << bit, c)) for r, c in ev...  4.67 us
    dynamic_slice x4, local copies, waits for them, and re-layouts, part_of(): return lax.dynamic_slice_in_dim(array, start, size, 0)  3.62 us
    ppermute x2, starting transfers between devices, over_cores(): lax.ppermute(have, BOTH, perm)  2.78 us
  transfers between devices with their start and end apart: 17, of which 9 were waited for; matrix products, arithmetic and copies ran while one was open for 15% of the time, Pallas kernels for 3%

profile of v4, /device:TPU:0, one launch (start us, length us, event | category | flops | bytes accessed | tf_op | source)
XLA Modules:
  0.0 73.8 jit_solution(16141260249412606889)
XLA Ops:
  0.6 1.1 %constant_dynamic-slice_fusion.3 = bf16[4,256,256]{2,1,0:T(8,128)(2,1)S(1)} fusion(bf16[8,256,256]{2,1,0:T(8,128)(2,1)} %param.13, s32[]{:T(128)S(6)} %select_n.145), kind=kLoop, calls=%fused_computation.69 | loop fusion | bytes 1048580 | tf_op jit(solution)/shard_map/dynamic_slice | solution.py:103
  1.7 4.9 %collective-permute-start = (bf16[4,256,256]{2,1,0:T(8,128)(2,1)S(1)}, bf16[4,256,256]{2,1,0:T(8,128)(2,1)S(1)}, u32[]{:S(2)}, u32[]{:S(2)}) collective-permute-start(bf16[4,256,256]{2,1,0:T(8,128)(2,1)S(1)} %constant_dynamic-slice_fusion.3), channel_id=1, source_target_pairs={{0,16},{1,17},{10,26},{11,27},{20,4},{21,5},{30,14},{31,15}} | collective-permute-start | bytes 1572872 | tf_op jit(solution)/shard_map/ppermute | solution.py:70
  6.6 1.1 %constant_dynamic-slice_fusion.1 = bf16[4,256,256]{2,1,0:T(8,128)(2,1)S(1)} fusion(bf16[8,256,256]{2,1,0:T(8,128)(2,1)} %param.14, s32[]{:T(128)S(6)} %select_n.145), kind=kLoop, calls=%fused_computation.67 | loop fusion | bytes 1048580 | tf_op jit(solution)/shard_map/dynamic_slice | solution.py:103
  7.7 1.3 %collective-permute-start.5 = (bf16[4,256,256]{2,1,0:T(8,128)(2,1)S(1)}, bf16[4,256,256]{2,1,0:T(8,128)(2,1)S(1)}, u32[]{:S(2)}, u32[]{:S(2)}) collective-permute-start(bf16[4,256,256]{2,1,0:T(8,128)(2,1)S(1)} %constant_dynamic-slice_fusion.1), channel_id=1, source_target_pairs={{0,16},{1,17},{10,26},{11,27},{20,4},{21,5},{30,14},{31,15}} | collective-permute-start | bytes 1572872 | tf_op jit(solution)/shard_map/ppermute | solution.py:70
  9.1 0.7 dynamic_slice.81
  10.6 0.7 %broadcast_compare_fusion.2 = (pred[8]{0:T(512)(128)(4,1)S(1)}, pred[8]{0:T(512)(128)(4,1)S(1)}) fusion(s32[32]{0:T(128)} %param.12, s32[]{:T(128)S(6)} %select_n.146, s32[32]{0:T(128)} %param.11), kind=kLoop, calls=%fused_computation.74 | loop fusion | flops 16 | bytes 84 | tf_op jit(solution)/shard_map/gt | solution.py:106
  11.3 0.8 %broadcast_compare_fusion = (pred[8,4]{0,1:T(4,128)(4,1)S(1)}, pred[8,4]{0,1:T(4,128)(4,1)S(1)}) fusion(s32[8,4]{0,1:T(4,128)} %param.10, s32[4]{0:T(128)S(1)} %dynamic_slice.83, s32[4]{0:T(128)S(1)} %dynamic_slice.81), kind=kLoop, calls=%fused_computation.71 | loop fusion | flops 128 | bytes 224 | tf_op jit(solution)/shard_map/gt | solution.py:106
  12.1 1.2 %collective-permute-done = bf16[4,256,256]{2,1,0:T(8,128)(2,1)S(1)} collective-permute-done((bf16[4,256,256]{2,1,0:T(8,128)(2,1)S(1)}, bf16[4,256,256]{2,1,0:T(8,128)(2,1)S(1)}, u32[]{:S(2)}, u32[]{:S(2)}) %collective-permute-start) | collective-permute-done | bytes 524320 | tf_op jit(solution)/shard_map/ppermute | solution.py:70
  13.4 1.3 %collective-permute-start.1 = (bf16[4,256,256]{2,1,0:T(8,128)(2,1)S(1)}, bf16[4,256,256]{2,1,0:T(8,128)(2,1)S(1)}, u32[]{:S(2)}, u32[]{:S(2)}) collective-permute-start(bf16[4,256,256]{2,1,0:T(8,128)(2,1)S(1)} %broadcast_select_fusion.2), channel_id=1, source_target_pairs={{0,8},{1,9},{10,2},{11,3},{4,12},{5,13},{14,6},{15,7},{16,24},{17,... | collective-permute-start | bytes 1572872 | tf_op jit(solution)/shard_map/ppermute | solution.py:80
  14.7 1.2 %dynamic_slice.80 = s32[1]{0:T(128)} dynamic-slice(s32[32]{0:T(128)} %param.11, s32[]{:T(128)S(6)} %select_n.136), dynamic_slice_sizes={1} | dynamic-slice | bytes 12 | tf_op jit(solution)/shard_map/dynamic_slice | solution.py:158
  16.0 1.2 %dynamic_slice.92 = s32[1]{0:T(128)} dynamic-slice(s32[32]{0:T(128)} %param.12, s32[]{:T(128)S(6)} %select_n.136), dynamic_slice_sizes={1} | dynamic-slice | bytes 12 | tf_op jit(solution)/shard_map/dynamic_slice | solution.py:158
  19.0 3.6 %bitcast_convert_fusion.1 = bf16[8,256,256]{2,1,0:T(8,128)(2,1)S(1)} fusion(bf16[8,4,256,256]{3,2,1,0:T(8,128)(2,1)} %param.9, pred[8,4]{1,0:T(8,128)(4,1)S(1)} %copy.19, bf16[4,256,256]{2,1,0:T(8,128)(2,1)S(1)} %broadcast_select_fusion.2, bf16[4,256,256]{2,1,0:T(8,128)(2,1)S(1)} %collective-permute-done.1, pred[]{:T(512)S(6)} %eq.18), kind=kOutput, calls=%fused_computation.7 | convolution fusion | flops 1076625408 | bytes 6291489 | tf_op jit(solution)/shard_map/ijab,jbc->iac/dot_general | solution.py:110
  22.6 1.5 %collective-permute-start.6 = (bf16[4,256,256]{2,1,0:T(8,128)(2,1)S(1)}, bf16[4,256,256]{2,1,0:T(8,128)(2,1)S(1)}, u32[]{:S(2)}, u32[]{:S(2)}) collective-permute-start(bf16[4,256,256]{2,1,0:T(8,128)(2,1)S(1)} %broadcast_select_fusion.1), channel_id=1, source_target_pairs={{0,8},{1,9},{10,2},{11,3},{4,12},{5,13},{14,6},{15,7},{16,24},{17,... | collective-permute-start | bytes 1572872 | tf_op jit(solution)/shard_map/ppermute | solution.py:80
  24.8 1.6 %collective-permute-start.2 = (bf16[4,256,256]{2,1,0:T(8,128)(2,1)S(1)}, bf16[4,256,256]{2,1,0:T(8,128)(2,1)S(1)}, u32[]{:S(2)}, u32[]{:S(2)}) collective-permute-start(bf16[4,256,256]{2,1,0:T(8,128)(2,1)S(1)} %get-tuple-element.41), channel_id=1, source_target_pairs={{0,1},{1,0},{2,3},{3,2},{4,5},{5,4},{6,7},{7,6},{8,9},{9,8},{10,11... | collective-permute-start | bytes 1572872 | tf_op jit(solution)/shard_map/ppermute | solution.py:83
  27.0 1.3 %bitcast_convert_fusion = bf16[8,256,256]{2,1,0:T(8,128)(2,1)S(1)} fusion(bf16[8,4,256,256]{3,2,1,0:T(8,128)(2,1)S(1)} %copy-done.6, pred[8,4]{1,0:T(8,128)(4,1)S(1)} %copy.21, bf16[4,256,256]{2,1,0:T(8,128)(2,1)S(1)} %broadcast_select_fusion.1, bf16[4,256,256]{2,1,0:T(8,128)(2,1)S(1)} %collective-permute-done.6, pred[]{:T(512)S(6)} %eq.18), kind=kOutput, calls=%fused_computation.6 | convolution fusion | flops 1076625408 | bytes 6291489 | tf_op jit(solution)/shard_map/ijab,jbc->iac/dot_general | solution.py:110
  29.3 7.7 %collective-permute-done.2 = bf16[4,256,256]{2,1,0:T(8,128)(2,1)S(1)} collective-permute-done((bf16[4,256,256]{2,1,0:T(8,128)(2,1)S(1)}, bf16[4,256,256]{2,1,0:T(8,128)(2,1)S(1)}, u32[]{:S(2)}, u32[]{:S(2)}) %collective-permute-start.2) | collective-permute-done | bytes 524320 | tf_op jit(solution)/shard_map/ppermute | solution.py:83
  37.0 1.5 %collective-permute-start.7 = (bf16[4,256,256]{2,1,0:T(8,128)(2,1)S(1)}, bf16[4,256,256]{2,1,0:T(8,128)(2,1)S(1)}, u32[]{:S(2)}, u32[]{:S(2)}) collective-permute-start(bf16[4,256,256]{2,1,0:T(8,128)(2,1)S(1)} %get-tuple-element.19), channel_id=1, source_target_pairs={{0,1},{1,0},{2,3},{3,2},{4,5},{5,4},{6,7},{7,6},{8,9},{9,8},{10,11... | collective-permute-start | bytes 1572872 | tf_op jit(solution)/shard_map/ppermute | solution.py:83
  38.7 2.5 %collective-permute-start.11 = (bf16[192,256]{1,0:T(8,128)(2,1)S(1)}, bf16[192,256]{1,0:T(8,128)(2,1)S(1)}, u32[]{:S(2)}, u32[]{:S(2)}) collective-permute-start(bf16[192,256]{1,0:T(8,128)(2,1)S(1)} %dynamic-slice_convert_fusion.1), channel_id=1, source_target_pairs={{0,16},{1,17},{2,18},{3,19},{4,20},{5,21},{6,22},{7,23},{8,24},{9,... | collective-permute-start | bytes 294920 | tf_op jit(solution)/shard_map/ppermute | solution.py:86
  41.4 2.5 %collective-permute-done.11 = bf16[192,256]{1,0:T(8,128)(2,1)S(1)} collective-permute-done((bf16[192,256]{1,0:T(8,128)(2,1)S(1)}, bf16[192,256]{1,0:T(8,128)(2,1)S(1)}, u32[]{:S(2)}, u32[]{:S(2)}) %collective-permute-start.11) | collective-permute-done | bytes 98336 | tf_op jit(solution)/shard_map/ppermute | solution.py:86
  43.9 3.2 %collective-permute-start.12 = (bf16[192,256]{1,0:T(8,128)(2,1)S(1)}, bf16[192,256]{1,0:T(8,128)(2,1)S(1)}, u32[]{:S(2)}, u32[]{:S(2)}) collective-permute-start(bf16[192,256]{1,0:T(8,128)(2,1)S(1)} %add_convert_fusion.4), channel_id=1, source_target_pairs={{0,4},{1,5},{2,6},{3,7},{4,0},{5,1},{6,2},{7,3},{8,12},{9,13},{10,... | collective-permute-start | bytes 294920 | tf_op jit(solution)/shard_map/ppermute | solution.py:83
  47.1 2.9 %collective-permute-start.4 = (bf16[1,256,256]{2,1,0:T(8,128)(2,1)S(1)}, bf16[1,256,256]{2,1,0:T(8,128)(2,1)S(1)}, u32[]{:S(2)}, u32[]{:S(2)}) collective-permute-start(bf16[1,256,256]{2,1,0:T(8,128)(2,1)S(1)} %fusion.30), channel_id=1, source_target_pairs={{0,4},{1,5},{2,6},{3,7},{4,0},{5,1},{6,2},{7,3},{8,12},{9,13},{10,... | collective-permute-start | bytes 393224 | tf_op jit(solution)/shard_map/ppermute | solution.py:83
  50.0 3.3 %collective-permute-done.12 = bf16[192,256]{1,0:T(8,128)(2,1)S(1)} collective-permute-done((bf16[192,256]{1,0:T(8,128)(2,1)S(1)}, bf16[192,256]{1,0:T(8,128)(2,1)S(1)}, u32[]{:S(2)}, u32[]{:S(2)}) %collective-permute-start.12) | collective-permute-done | bytes 98336 | tf_op jit(solution)/shard_map/ppermute | solution.py:83
  53.4 2.1 %collective-permute-start.8 = (bf16[2,256,256]{2,1,0:T(8,128)(2,1)S(1)}, bf16[2,256,256]{2,1,0:T(8,128)(2,1)S(1)}, u32[]{:S(2)}, u32[]{:S(2)}) collective-permute-start(bf16[2,256,256]{2,1,0:T(8,128)(2,1)S(1)} %fusion.26), channel_id=1, source_target_pairs={{0,2},{1,3},{2,0},{3,1},{4,6},{5,7},{6,4},{7,5},{8,10},{9,11},{10,... | collective-permute-start | bytes 786440 | tf_op jit(solution)/shard_map/ppermute | solution.py:83
  55.5 3.4 %collective-permute-done.13 = bf16[192,256]{1,0:T(8,128)(2,1)S(1)} collective-permute-done((bf16[192,256]{1,0:T(8,128)(2,1)S(1)}, bf16[192,256]{1,0:T(8,128)(2,1)S(1)}, u32[]{:S(2)}, u32[]{:S(2)}) %collective-permute-start.13) | collective-permute-done | bytes 98336 | tf_op jit(solution)/shard_map/ppermute | solution.py:83
  58.9 0.8 %collective-permute-start.14 = (bf16[192,256]{1,0:T(8,128)(2,1)S(1)}, bf16[192,256]{1,0:T(8,128)(2,1)S(1)}, u32[]{:S(2)}, u32[]{:S(2)}) collective-permute-start(bf16[192,256]{1,0:T(8,128)(2,1)S(1)} %add_convert_fusion.2), channel_id=1, source_target_pairs={{0,1},{1,0},{2,3},{3,2},{4,5},{5,4},{6,7},{7,6},{8,9},{9,8},{10,11... | collective-permute-start | bytes 294920 | tf_op jit(solution)/shard_map/ppermute | solution.py:83
  59.8 3.9 %collective-permute-done.14 = bf16[192,256]{1,0:T(8,128)(2,1)S(1)} collective-permute-done((bf16[192,256]{1,0:T(8,128)(2,1)S(1)}, bf16[192,256]{1,0:T(8,128)(2,1)S(1)}, u32[]{:S(2)}, u32[]{:S(2)}) %collective-permute-start.14) | collective-permute-done | bytes 98336 | tf_op jit(solution)/shard_map/ppermute | solution.py:83
  63.7 2.0 %collective-permute-start.15 = (bf16[192,256]{1,0:T(8,128)(2,1)S(1)}, bf16[192,256]{1,0:T(8,128)(2,1)S(1)}, u32[]{:S(2)}, u32[]{:S(2)}) collective-permute-start(bf16[192,256]{1,0:T(8,128)(2,1)S(1)} %add_convert_fusion.1), channel_id=1, source_target_pairs={{0,16},{1,17},{2,18},{3,19},{4,20},{5,21},{6,22},{7,23},{8,24},{9,... | collective-permute-start | bytes 294920 | tf_op jit(solution)/shard_map/ppermute | solution.py:86
  65.7 0.9 %collective-permute-start.9 = (bf16[1,256,256]{2,1,0:T(8,128)(2,1)S(1)}, bf16[1,256,256]{2,1,0:T(8,128)(2,1)S(1)}, u32[]{:S(2)}, u32[]{:S(2)}) collective-permute-start(bf16[1,256,256]{2,1,0:T(8,128)(2,1)S(1)} %fusion.29), channel_id=1, source_target_pairs={{0,4},{1,5},{2,6},{3,7},{4,0},{5,1},{6,2},{7,3},{8,12},{9,13},{10,... | collective-permute-start | bytes 393224 | tf_op jit(solution)/shard_map/ppermute | solution.py:83
  66.6 1.7 %collective-permute-done.15 = bf16[192,256]{1,0:T(8,128)(2,1)S(1)} collective-permute-done((bf16[192,256]{1,0:T(8,128)(2,1)S(1)}, bf16[192,256]{1,0:T(8,128)(2,1)S(1)}, u32[]{:S(2)}, u32[]{:S(2)}) %collective-permute-start.15) | collective-permute-done | bytes 98336 | tf_op jit(solution)/shard_map/ppermute | solution.py:86
  68.6 1.3 %collective-permute-done.16.other = bf16[384,256]{1,0:T(8,128)(2,1)S(1)} collective-permute-done((bf16[384,256]{1,0:T(8,128)(2,1)S(1)}, bf16[384,256]{1,0:T(8,128)(2,1)S(1)}, u32[]{:S(2)}, u32[]{:S(2)}) %collective-permute-start.16) | collective-permute-done | bytes 196640 | tf_op jit(solution)/shard_map/ppermute | solution.py:86
  70.6 2.3 %shard_map.128 = (bf16[256,256]{1,0:T(8,128)(2,1)}, bf16[256,256]{1,0:T(8,128)(2,1)}, bf16[256,256]{1,0:T(8,128)(2,1)}) custom-call(s32[1]{0:T(128)} %bitcast.26.place, bf16[384,256]{1,0:T(8,128)(2,1)} %copy-done, bf16[384,256]{1,0:T(8,128)(2,1)} %copy-done.5, bf16[256,256]{1,0:T(8,128)(2,1)} %link.1, f32[256,256]{1,0:T(8,128)} %inverse_one.1, ...), custom_call_target="tpu_custom_call" | custom-call | flops 100663296 | bytes 1572864 | tf_op jit(solution)/shard_map/pallas_call | solution.py:29
  72.9 0.9 %fusion.34 = bf16[1,256,256]{2,1,0:T(8,128)(2,1)} fusion(f32[2,1,256,256]{3,2,1,0:T(8,128)S(1)} %convert_add_fusion, s32[]{:T(128)S(6)} %select_n.152, bf16[1,256,256]{2,1,0:T(8,128)(2,1)S(1)} %collective-permute-done.9, bf16[256,256]{1,0:T(8,128)(2,1)S(1)} %copy-done.2, bf16[1,256,256]{2,1,0:T(8,128)(2,1)S(1)} %fusion.33, ...), kind=kOutput, calls=%fused_computation.61 | convolution fusion | flops 34013184 | bytes 917512 | tf_op jit(solution)/shard_map/dot_general | solution.py:160
  (55 shorter events, 5.1 us)
Async XLA Ops:
  1.7 11.6 %collective-permute-start = (bf16[4,256,256]{2,1,0:T(8,128)(2,1)S(1)}, bf16[4,256,256]{2,1,0:T(8,128)(2,1)S(1)}, u32[]{:S(2)}, u32[]{:S(2)}) collective-permute-start(bf16[4,256,256]{2,1,0:T(8,128)(2,1)S(1)} %constant_dynamic-slice_fusion.3), channel_id=1, source_target_pairs={{0,16},{1,17},{10,26},{11,27},{20,4},{21,5},{30,14},{31,15}} | collective-permute-start | bytes 1572872 | tf_op jit(solution)/shard_map/ppermute | solution.py:70
  7.7 11.2 %collective-permute-start.5 = (bf16[4,256,256]{2,1,0:T(8,128)(2,1)S(1)}, bf16[4,256,256]{2,1,0:T(8,128)(2,1)S(1)}, u32[]{:S(2)}, u32[]{:S(2)}) collective-permute-start(bf16[4,256,256]{2,1,0:T(8,128)(2,1)S(1)} %constant_dynamic-slice_fusion.1), channel_id=1, source_target_pairs={{0,16},{1,17},{10,26},{11,27},{20,4},{21,5},{30,14},{31,15}} | collective-permute-start | bytes 1572872 | tf_op jit(solution)/shard_map/ppermute | solution.py:70
  13.4 5.6 %collective-permute-start.1 = (bf16[4,256,256]{2,1,0:T(8,128)(2,1)S(1)}, bf16[4,256,256]{2,1,0:T(8,128)(2,1)S(1)}, u32[]{:S(2)}, u32[]{:S(2)}) collective-permute-start(bf16[4,256,256]{2,1,0:T(8,128)(2,1)S(1)} %broadcast_select_fusion.2), channel_id=1, source_target_pairs={{0,8},{1,9},{10,2},{11,3},{4,12},{5,13},{14,6},{15,7},{16,24},{17,... | collective-permute-start | bytes 1572872 | tf_op jit(solution)/shard_map/ppermute | solution.py:80
  19.0 5.1 %copy-start.3 = (bf16[8,256,256]{2,1,0:T(8,128)(2,1)S(1)}, bf16[8,256,256]{2,1,0:T(8,128)(2,1)}, u32[]{:S(2)}) copy-start(bf16[8,256,256]{2,1,0:T(8,128)(2,1)} %param.13) | copy-start | bytes 3145732
  22.6 3.9 %copy-start.4 = (bf16[8,256,256]{2,1,0:T(8,128)(2,1)S(1)}, bf16[8,256,256]{2,1,0:T(8,128)(2,1)}, u32[]{:S(2)}) copy-start(bf16[8,256,256]{2,1,0:T(8,128)(2,1)} %param.14) | copy-start | bytes 3145732
  22.6 4.4 %collective-permute-start.6 = (bf16[4,256,256]{2,1,0:T(8,128)(2,1)S(1)}, bf16[4,256,256]{2,1,0:T(8,128)(2,1)S(1)}, u32[]{:S(2)}, u32[]{:S(2)}) collective-permute-start(bf16[4,256,256]{2,1,0:T(8,128)(2,1)S(1)} %broadcast_select_fusion.1), channel_id=1, source_target_pairs={{0,8},{1,9},{10,2},{11,3},{4,12},{5,13},{14,6},{15,7},{16,24},{17,... | collective-permute-start | bytes 1572872 | tf_op jit(solution)/shard_map/ppermute | solution.py:80
  24.7 2.3 %copy-start.6 = (bf16[8,4,256,256]{3,2,1,0:T(8,128)(2,1)S(1)}, bf16[8,4,256,256]{3,2,1,0:T(8,128)(2,1)}, u32[]{:S(2)}) copy-start(bf16[8,4,256,256]{3,2,1,0:T(8,128)(2,1)} %param.9) | copy-start | bytes 12582916
  24.8 12.2 %collective-permute-start.2 = (bf16[4,256,256]{2,1,0:T(8,128)(2,1)S(1)}, bf16[4,256,256]{2,1,0:T(8,128)(2,1)S(1)}, u32[]{:S(2)}, u32[]{:S(2)}) collective-permute-start(bf16[4,256,256]{2,1,0:T(8,128)(2,1)S(1)} %get-tuple-element.41), channel_id=1, source_target_pairs={{0,1},{1,0},{2,3},{3,2},{4,5},{5,4},{6,7},{7,6},{8,9},{9,8},{10,11... | collective-permute-start | bytes 1572872 | tf_op jit(solution)/shard_map/ppermute | solution.py:83
  29.2 9.5 %collective-permute-start.10 = (bf16[384,256]{1,0:T(8,128)(2,1)S(1)}, bf16[384,256]{1,0:T(8,128)(2,1)S(1)}, u32[]{:S(2)}, u32[]{:S(2)}) collective-permute-start(bf16[384,256]{1,0:T(8,128)(2,1)S(1)} %dynamic-slice_convert_fusion), channel_id=1, source_target_pairs={{0,8},{1,9},{2,10},{3,11},{4,12},{5,13},{6,14},{7,15},{8,0},{9,1},... | collective-permute-start | bytes 589832 | tf_op jit(solution)/shard_map/ppermute | solution.py:86
  37.0 16.3 %collective-permute-start.7 = (bf16[4,256,256]{2,1,0:T(8,128)(2,1)S(1)}, bf16[4,256,256]{2,1,0:T(8,128)(2,1)S(1)}, u32[]{:S(2)}, u32[]{:S(2)}) collective-permute-start(bf16[4,256,256]{2,1,0:T(8,128)(2,1)S(1)} %get-tuple-element.19), channel_id=1, source_target_pairs={{0,1},{1,0},{2,3},{3,2},{4,5},{5,4},{6,7},{7,6},{8,9},{9,8},{10,11... | collective-permute-start | bytes 1572872 | tf_op jit(solution)/shard_map/ppermute | solution.py:83
  38.6 8.5 %collective-permute-start.3 = (bf16[2,256,256]{2,1,0:T(8,128)(2,1)S(1)}, bf16[2,256,256]{2,1,0:T(8,128)(2,1)S(1)}, u32[]{:S(2)}, u32[]{:S(2)}) collective-permute-start(bf16[2,256,256]{2,1,0:T(8,128)(2,1)S(1)} %get-tuple-element.37), channel_id=1, source_target_pairs={{0,2},{1,3},{2,0},{3,1},{4,6},{5,7},{6,4},{7,5},{8,10},{9,11},{10,... | collective-permute-start | bytes 786440 | tf_op jit(solution)/shard_map/ppermute | solution.py:83
  38.7 5.1 %collective-permute-start.11 = (bf16[192,256]{1,0:T(8,128)(2,1)S(1)}, bf16[192,256]{1,0:T(8,128)(2,1)S(1)}, u32[]{:S(2)}, u32[]{:S(2)}) collective-permute-start(bf16[192,256]{1,0:T(8,128)(2,1)S(1)} %dynamic-slice_convert_fusion.1), channel_id=1, source_target_pairs={{0,16},{1,17},{2,18},{3,19},{4,20},{5,21},{6,22},{7,23},{8,24},{9,... | collective-permute-start | bytes 294920 | tf_op jit(solution)/shard_map/ppermute | solution.py:86
  41.3 31.6 %copy-start.2 = (bf16[256,256]{1,0:T(8,128)(2,1)S(1)}, bf16[256,256]{1,0:T(8,128)(2,1)}, u32[]{:S(2)}) copy-start(bf16[256,256]{1,0:T(8,128)(2,1)} %link.1) | copy-start | bytes 393220
  43.9 9.3 %collective-permute-start.12 = (bf16[192,256]{1,0:T(8,128)(2,1)S(1)}, bf16[192,256]{1,0:T(8,128)(2,1)S(1)}, u32[]{:S(2)}, u32[]{:S(2)}) collective-permute-start(bf16[192,256]{1,0:T(8,128)(2,1)S(1)} %add_convert_fusion.4), channel_id=1, source_target_pairs={{0,4},{1,5},{2,6},{3,7},{4,0},{5,1},{6,2},{7,3},{8,12},{9,13},{10,... | collective-permute-start | bytes 294920 | tf_op jit(solution)/shard_map/ppermute | solution.py:83
  47.1 21.3 %collective-permute-start.4 = (bf16[1,256,256]{2,1,0:T(8,128)(2,1)S(1)}, bf16[1,256,256]{2,1,0:T(8,128)(2,1)S(1)}, u32[]{:S(2)}, u32[]{:S(2)}) collective-permute-start(bf16[1,256,256]{2,1,0:T(8,128)(2,1)S(1)} %fusion.30), channel_id=1, source_target_pairs={{0,4},{1,5},{2,6},{3,7},{4,0},{5,1},{6,2},{7,3},{8,12},{9,13},{10,... | collective-permute-start | bytes 393224 | tf_op jit(solution)/shard_map/ppermute | solution.py:83
  53.3 5.6 %collective-permute-start.13 = (bf16[192,256]{1,0:T(8,128)(2,1)S(1)}, bf16[192,256]{1,0:T(8,128)(2,1)S(1)}, u32[]{:S(2)}, u32[]{:S(2)}) collective-permute-start(bf16[192,256]{1,0:T(8,128)(2,1)S(1)} %add_convert_fusion.3), channel_id=1, source_target_pairs={{0,2},{1,3},{2,0},{3,1},{4,6},{5,7},{6,4},{7,5},{8,10},{9,11},{10,... | collective-permute-start | bytes 294920 | tf_op jit(solution)/shard_map/ppermute | solution.py:83
  53.4 10.2 %collective-permute-start.8 = (bf16[2,256,256]{2,1,0:T(8,128)(2,1)S(1)}, bf16[2,256,256]{2,1,0:T(8,128)(2,1)S(1)}, u32[]{:S(2)}, u32[]{:S(2)}) collective-permute-start(bf16[2,256,256]{2,1,0:T(8,128)(2,1)S(1)} %fusion.26), channel_id=1, source_target_pairs={{0,2},{1,3},{2,0},{3,1},{4,6},{5,7},{6,4},{7,5},{8,10},{9,11},{10,... | collective-permute-start | bytes 786440 | tf_op jit(solution)/shard_map/ppermute | solution.py:83
  58.9 4.7 %collective-permute-start.14 = (bf16[192,256]{1,0:T(8,128)(2,1)S(1)}, bf16[192,256]{1,0:T(8,128)(2,1)S(1)}, u32[]{:S(2)}, u32[]{:S(2)}) collective-permute-start(bf16[192,256]{1,0:T(8,128)(2,1)S(1)} %add_convert_fusion.2), channel_id=1, source_target_pairs={{0,1},{1,0},{2,3},{3,2},{4,5},{5,4},{6,7},{7,6},{8,9},{9,8},{10,11... | collective-permute-start | bytes 294920 | tf_op jit(solution)/shard_map/ppermute | solution.py:83
  63.7 4.7 %collective-permute-start.15 = (bf16[192,256]{1,0:T(8,128)(2,1)S(1)}, bf16[192,256]{1,0:T(8,128)(2,1)S(1)}, u32[]{:S(2)}, u32[]{:S(2)}) collective-permute-start(bf16[192,256]{1,0:T(8,128)(2,1)S(1)} %add_convert_fusion.1), channel_id=1, source_target_pairs={{0,16},{1,17},{2,18},{3,19},{4,20},{5,21},{6,22},{7,23},{8,24},{9,... | collective-permute-start | bytes 294920 | tf_op jit(solution)/shard_map/ppermute | solution.py:86
  65.7 7.2 %collective-permute-start.9 = (bf16[1,256,256]{2,1,0:T(8,128)(2,1)S(1)}, bf16[1,256,256]{2,1,0:T(8,128)(2,1)S(1)}, u32[]{:S(2)}, u32[]{:S(2)}) collective-permute-start(bf16[1,256,256]{2,1,0:T(8,128)(2,1)S(1)} %fusion.29), channel_id=1, source_target_pairs={{0,4},{1,5},{2,6},{3,7},{4,0},{5,1},{6,2},{7,3},{8,12},{9,13},{10,... | collective-permute-start | bytes 393224 | tf_op jit(solution)/shard_map/ppermute | solution.py:83
  68.4 1.5 %copy-start = (bf16[384,256]{1,0:T(8,128)(2,1)}, bf16[384,256]{1,0:T(8,128)(2,1)S(1)}, u32[]{:S(2)}) copy-start(bf16[384,256]{1,0:T(8,128)(2,1)S(1)} %pad_maximum_fusion.1.mine) | copy-start | bytes 589828
  68.4 1.5 %collective-permute-start.16 = (bf16[384,256]{1,0:T(8,128)(2,1)S(1)}, bf16[384,256]{1,0:T(8,128)(2,1)S(1)}, u32[]{:S(2)}, u32[]{:S(2)}) collective-permute-start(bf16[384,256]{1,0:T(8,128)(2,1)S(1)} %pad_maximum_fusion.1.mine), channel_id=1, source_target_pairs={{0,8},{1,9},{2,10},{3,11},{4,12},{5,13},{6,14},{7,15},{8,0},{9,1},... | collective-permute-start | bytes 589832 | tf_op jit(solution)/shard_map/ppermute | solution.py:86
  68.6 5.2 %copy-start.1 = (bf16[1,256,256]{2,1,0:T(8,128)(2,1)}, bf16[1,256,256]{2,1,0:T(8,128)(2,1)S(1)}, u32[]{:S(2)}) copy-start(bf16[1,256,256]{2,1,0:T(8,128)(2,1)S(1)} %fusion.33) | copy-start | bytes 393220
  69.9 0.7 copy-start.5

commit v5 on v4

--- a/solution.py
+++ b/solution.py
@@ -123,7 +123,7 @@
     all_one = products(marks[0], over_cores(have_one))
     keep_one, one = first_swap(all_one)
     all_two = products(marks[1], over_cores(after(have_two, all_one)))
-    keep_two, two = first_swap(all_two, one[0])
+    keep_two, two = first_swap(all_two)
     sums = contraction(first, all_one), contraction(all_one, second_in_one), contraction(second, all_two)
     for _ in range(1, bits):
         keep_one = next_swap(keep_one, one)
@@ -137,9 +137,9 @@
         got = swap_rows(lax.dynamic_slice_in_dim(part, (1 - mine) * half, half, 0).astype(BF16), bit)
         part = lax.dynamic_slice_in_dim(part, mine * half, half, 0) + got.astype(F32)
     part = part.astype(BF16)
-    gates = [one[0], two[0], *one[1:]]
-    for bit, gate in zip(reversed(range(bits)), gates):
-        got = swap(after(part, gate), bit)
+    gates = {bits - 1: one[:1], 0: [two[0], *one[1:-1]]}
+    for bit in reversed(range(bits)):
+        got = swap(after(part, *gates.get(bit, ())), bit)
         part = (part.astype(F32) + got.astype(F32)).astype(BF16)
     for bit in reversed(range(row_bits)):
         got = swap_rows(after(part, one[-1] if bit == 0 else two[-2]), bit)

time: 74.2 us -> 74.3 us (level)
  waiting for transfers between devices: 25.2 us -> 19.1 us
  starting transfers between devices: 26.6 us -> 32.1 us
    ppermute x9, starting transfers between devices: 13 us -> 20.2 us  [swap(): lax.ppermute(array, BOTH, [(at(r, c), at(r, c ^ 1 << bit)) for r, c in ev...]
    ppermute x4, waiting for transfers between devices: 5.59 us -> 1.76 us  [swap_rows(): lax.ppermute(array, BOTH, [(at(r, c), at(r ^ 1 << bit, c)) for r, c in ev...]
    ppermute x9, waiting for transfers between devices: 18.2 us -> 16 us  [swap(): lax.ppermute(array, BOTH, [(at(r, c), at(r, c ^ 1 << bit)) for r, c in ev...]
    ppermute x4, starting transfers between devices: 4.67 us -> 2.91 us  [swap_rows(): lax.ppermute(array, BOTH, [(at(r, c), at(r ^ 1 << bit, c)) for r, c in ev...]
where the time goes in v5:
time: 74.3 us; the launch traced here: 73.1 us
  starting transfers between devices  32.1 us (43%)
  waiting for transfers between devices  19.1 us (26%)
  matrix products  7.62 us (10%)
  local copies, waits for them, and re-layouts  7.21 us (10%)
  other arithmetic  2.39 us (3%)
  between operations  2.39 us (3%)
  Pallas kernels  2.32 us (3%)
    ppermute x9, starting transfers between devices, swap(): lax.ppermute(array, BOTH, [(at(r, c), at(r, c ^ 1 << bit)) for r, c in ev...  20.2 us
    ppermute x9, waiting for transfers between devices, swap(): lax.ppermute(array, BOTH, [(at(r, c), at(r, c ^ 1 << bit)) for r, c in ev...  16 us
    ppermute x2, starting transfers between devices, over_chips(): got = after(lax.ppermute(piece, BOTH, perm), *earlier)  6.23 us
    dot_general x2, matrix products, products(): jnp.einsum('ijab,jbc->iac', kept, column, preferred_element_type=F32)  4.9 us
    dynamic_slice x4, local copies, waits for them, and re-layouts, part_of(): return lax.dynamic_slice_in_dim(array, start, size, 0)  3.62 us
    ppermute x4, starting transfers between devices, swap_rows(): lax.ppermute(array, BOTH, [(at(r, c), at(r ^ 1 << bit, c)) for r, c in ev...  2.91 us
    ppermute x2, starting transfers between devices, over_cores(): lax.ppermute(have, BOTH, perm)  2.78 us
    dynamic_slice x2, local copies, waits for them, and re-layouts, shards(): m[row * rows + col].astype(F32)  2.48 us
  transfers between devices with their start and end apart: 17, of which 9 were waited for; matrix products, arithmetic and copies ran while one was open for 15% of the time, Pallas kernels for 3%

profile of v5, /device:TPU:0, one launch (start us, length us, event | category | flops | bytes accessed | tf_op | source)
XLA Modules:
  0.0 73.1 jit_solution(16977266886316205742)
XLA Ops:
  0.6 1.1 %constant_dynamic-slice_fusion.3 = bf16[4,256,256]{2,1,0:T(8,128)(2,1)S(1)} fusion(bf16[8,256,256]{2,1,0:T(8,128)(2,1)} %param.13, s32[]{:T(128)S(6)} %select_n.145), kind=kLoop, calls=%fused_computation.69 | loop fusion | bytes 1048580 | tf_op jit(solution)/shard_map/dynamic_slice | solution.py:103
  1.7 4.9 %collective-permute-start = (bf16[4,256,256]{2,1,0:T(8,128)(2,1)S(1)}, bf16[4,256,256]{2,1,0:T(8,128)(2,1)S(1)}, u32[]{:S(2)}, u32[]{:S(2)}) collective-permute-start(bf16[4,256,256]{2,1,0:T(8,128)(2,1)S(1)} %constant_dynamic-slice_fusion.3), channel_id=1, source_target_pairs={{0,16},{1,17},{10,26},{11,27},{20,4},{21,5},{30,14},{31,15}} | collective-permute-start | bytes 1572872 | tf_op jit(solution)/shard_map/ppermute | solution.py:70
  6.6 1.1 %constant_dynamic-slice_fusion.1 = bf16[4,256,256]{2,1,0:T(8,128)(2,1)S(1)} fusion(bf16[8,256,256]{2,1,0:T(8,128)(2,1)} %param.14, s32[]{:T(128)S(6)} %select_n.145), kind=kLoop, calls=%fused_computation.67 | loop fusion | bytes 1048580 | tf_op jit(solution)/shard_map/dynamic_slice | solution.py:103
  7.7 1.3 %collective-permute-start.5 = (bf16[4,256,256]{2,1,0:T(8,128)(2,1)S(1)}, bf16[4,256,256]{2,1,0:T(8,128)(2,1)S(1)}, u32[]{:S(2)}, u32[]{:S(2)}) collective-permute-start(bf16[4,256,256]{2,1,0:T(8,128)(2,1)S(1)} %constant_dynamic-slice_fusion.1), channel_id=1, source_target_pairs={{0,16},{1,17},{10,26},{11,27},{20,4},{21,5},{30,14},{31,15}} | collective-permute-start | bytes 1572872 | tf_op jit(solution)/shard_map/ppermute | solution.py:70
  9.1 0.7 %dynamic_slice.81 = s32[4]{0:T(128)S(1)} dynamic-slice(s32[32]{0:T(128)} %param.11, s32[]{:T(128)S(6)} %select_n.137), dynamic_slice_sizes={4} | dynamic-slice | bytes 36 | tf_op jit(solution)/shard_map/dynamic_slice | solution.py:103
  9.8 0.7 dynamic_slice.83
  10.6 0.7 %broadcast_compare_fusion.2 = (pred[8]{0:T(512)(128)(4,1)S(1)}, pred[8]{0:T(512)(128)(4,1)S(1)}) fusion(s32[32]{0:T(128)} %param.12, s32[]{:T(128)S(6)} %select_n.146, s32[32]{0:T(128)} %param.11), kind=kLoop, calls=%fused_computation.74 | loop fusion | flops 16 | bytes 84 | tf_op jit(solution)/shard_map/gt | solution.py:106
  11.3 0.8 %broadcast_compare_fusion = (pred[8,4]{0,1:T(4,128)(4,1)S(1)}, pred[8,4]{0,1:T(4,128)(4,1)S(1)}) fusion(s32[8,4]{0,1:T(4,128)} %param.10, s32[4]{0:T(128)S(1)} %dynamic_slice.83, s32[4]{0:T(128)S(1)} %dynamic_slice.81), kind=kLoop, calls=%fused_computation.71 | loop fusion | flops 128 | bytes 224 | tf_op jit(solution)/shard_map/gt | solution.py:106
  12.1 1.2 %collective-permute-done = bf16[4,256,256]{2,1,0:T(8,128)(2,1)S(1)} collective-permute-done((bf16[4,256,256]{2,1,0:T(8,128)(2,1)S(1)}, bf16[4,256,256]{2,1,0:T(8,128)(2,1)S(1)}, u32[]{:S(2)}, u32[]{:S(2)}) %collective-permute-start) | collective-permute-done | bytes 524320 | tf_op jit(solution)/shard_map/ppermute | solution.py:70
  13.4 1.3 %collective-permute-start.1 = (bf16[4,256,256]{2,1,0:T(8,128)(2,1)S(1)}, bf16[4,256,256]{2,1,0:T(8,128)(2,1)S(1)}, u32[]{:S(2)}, u32[]{:S(2)}) collective-permute-start(bf16[4,256,256]{2,1,0:T(8,128)(2,1)S(1)} %broadcast_select_fusion.2), channel_id=1, source_target_pairs={{0,8},{1,9},{10,2},{11,3},{4,12},{5,13},{14,6},{15,7},{16,24},{17,... | collective-permute-start | bytes 1572872 | tf_op jit(solution)/shard_map/ppermute | solution.py:80
  14.7 1.2 %dynamic_slice.80 = s32[1]{0:T(128)} dynamic-slice(s32[32]{0:T(128)} %param.11, s32[]{:T(128)S(6)} %select_n.136), dynamic_slice_sizes={1} | dynamic-slice | bytes 12 | tf_op jit(solution)/shard_map/dynamic_slice | solution.py:158
  16.0 1.2 %dynamic_slice.92 = s32[1]{0:T(128)} dynamic-slice(s32[32]{0:T(128)} %param.12, s32[]{:T(128)S(6)} %select_n.136), dynamic_slice_sizes={1} | dynamic-slice | bytes 12 | tf_op jit(solution)/shard_map/dynamic_slice | solution.py:158
  19.0 3.6 %bitcast_convert_fusion.1 = bf16[8,256,256]{2,1,0:T(8,128)(2,1)S(1)} fusion(bf16[8,4,256,256]{3,2,1,0:T(8,128)(2,1)} %param.9, pred[8,4]{1,0:T(8,128)(4,1)S(1)} %copy.19, bf16[4,256,256]{2,1,0:T(8,128)(2,1)S(1)} %broadcast_select_fusion.2, bf16[4,256,256]{2,1,0:T(8,128)(2,1)S(1)} %collective-permute-done.1, pred[]{:T(512)S(6)} %eq.18), kind=kOutput, calls=%fused_computation.7 | convolution fusion | flops 1076625408 | bytes 6291489 | tf_op jit(solution)/shard_map/ijab,jbc->iac/dot_general | solution.py:110
  22.6 1.5 %collective-permute-start.6 = (bf16[4,256,256]{2,1,0:T(8,128)(2,1)S(1)}, bf16[4,256,256]{2,1,0:T(8,128)(2,1)S(1)}, u32[]{:S(2)}, u32[]{:S(2)}) collective-permute-start(bf16[4,256,256]{2,1,0:T(8,128)(2,1)S(1)} %broadcast_select_fusion.1), channel_id=1, source_target_pairs={{0,8},{1,9},{10,2},{11,3},{4,12},{5,13},{14,6},{15,7},{16,24},{17,... | collective-permute-start | bytes 1572872 | tf_op jit(solution)/shard_map/ppermute | solution.py:80
  24.1 1.6 %collective-permute-start.2 = (bf16[4,256,256]{2,1,0:T(8,128)(2,1)S(1)}, bf16[4,256,256]{2,1,0:T(8,128)(2,1)S(1)}, u32[]{:S(2)}, u32[]{:S(2)}) collective-permute-start(bf16[4,256,256]{2,1,0:T(8,128)(2,1)S(1)} %get-tuple-element.37), channel_id=1, source_target_pairs={{0,1},{1,0},{2,3},{3,2},{4,5},{5,4},{6,7},{7,6},{8,9},{9,8},{10,11... | collective-permute-start | bytes 1572872 | tf_op jit(solution)/shard_map/ppermute | solution.py:83
  26.9 1.3 %bitcast_convert_fusion = bf16[8,256,256]{2,1,0:T(8,128)(2,1)S(1)} fusion(bf16[8,4,256,256]{3,2,1,0:T(8,128)(2,1)S(1)} %copy-done.6, pred[8,4]{1,0:T(8,128)(4,1)S(1)} %copy.21, bf16[4,256,256]{2,1,0:T(8,128)(2,1)S(1)} %broadcast_select_fusion.1, bf16[4,256,256]{2,1,0:T(8,128)(2,1)S(1)} %collective-permute-done.6, pred[]{:T(512)S(6)} %eq.18), kind=kOutput, calls=%fused_computation.6 | convolution fusion | flops 1076625408 | bytes 6291489 | tf_op jit(solution)/shard_map/ijab,jbc->iac/dot_general | solution.py:110
  29.3 0.8 %collective-permute-start.7 = (bf16[4,256,256]{2,1,0:T(8,128)(2,1)S(1)}, bf16[4,256,256]{2,1,0:T(8,128)(2,1)S(1)}, u32[]{:S(2)}, u32[]{:S(2)}) collective-permute-start(bf16[4,256,256]{2,1,0:T(8,128)(2,1)S(1)} %get-tuple-element.35), channel_id=1, source_target_pairs={{0,1},{1,0},{2,3},{3,2},{4,5},{5,4},{6,7},{7,6},{8,9},{9,8},{10,11... | collective-permute-start | bytes 1572872 | tf_op jit(solution)/shard_map/ppermute | solution.py:83
  30.6 2.6 %collective-permute-start.11 = (bf16[192,256]{1,0:T(8,128)(2,1)S(1)}, bf16[192,256]{1,0:T(8,128)(2,1)S(1)}, u32[]{:S(2)}, u32[]{:S(2)}) collective-permute-start(bf16[192,256]{1,0:T(8,128)(2,1)S(1)} %dynamic-slice_convert_fusion.1), channel_id=1, source_target_pairs={{0,16},{1,17},{2,18},{3,19},{4,20},{5,21},{6,22},{7,23},{8,24},{9,... | collective-permute-start | bytes 294920 | tf_op jit(solution)/shard_map/ppermute | solution.py:86
  33.2 5.2 %collective-permute-done.2 = bf16[4,256,256]{2,1,0:T(8,128)(2,1)S(1)} collective-permute-done((bf16[4,256,256]{2,1,0:T(8,128)(2,1)S(1)}, bf16[4,256,256]{2,1,0:T(8,128)(2,1)S(1)}, u32[]{:S(2)}, u32[]{:S(2)}) %collective-permute-start.2) | collective-permute-done | bytes 524320 | tf_op jit(solution)/shard_map/ppermute | solution.py:83
  38.7 3.6 %collective-permute-start.12 = (bf16[192,256]{1,0:T(8,128)(2,1)S(1)}, bf16[192,256]{1,0:T(8,128)(2,1)S(1)}, u32[]{:S(2)}, u32[]{:S(2)}) collective-permute-start(bf16[192,256]{1,0:T(8,128)(2,1)S(1)} %add_convert_fusion.4), channel_id=1, source_target_pairs={{0,4},{1,5},{2,6},{3,7},{4,0},{5,1},{6,2},{7,3},{8,12},{9,13},{10,... | collective-permute-start | bytes 294920 | tf_op jit(solution)/shard_map/ppermute | solution.py:83
  42.4 4.5 %collective-permute-done.12 = bf16[192,256]{1,0:T(8,128)(2,1)S(1)} collective-permute-done((bf16[192,256]{1,0:T(8,128)(2,1)S(1)}, bf16[192,256]{1,0:T(8,128)(2,1)S(1)}, u32[]{:S(2)}, u32[]{:S(2)}) %collective-permute-start.12) | collective-permute-done | bytes 98336 | tf_op jit(solution)/shard_map/ppermute | solution.py:83
  46.9 4.0 %collective-permute-start.13 = (bf16[192,256]{1,0:T(8,128)(2,1)S(1)}, bf16[192,256]{1,0:T(8,128)(2,1)S(1)}, u32[]{:S(2)}, u32[]{:S(2)}) collective-permute-start(bf16[192,256]{1,0:T(8,128)(2,1)S(1)} %add_convert_fusion.3), channel_id=1, source_target_pairs={{0,2},{1,3},{2,0},{3,1},{4,6},{5,7},{6,4},{7,5},{8,10},{9,11},{10,... | collective-permute-start | bytes 294920 | tf_op jit(solution)/shard_map/ppermute | solution.py:83
  50.9 1.3 %collective-permute-start.4 = (bf16[1,256,256]{2,1,0:T(8,128)(2,1)S(1)}, bf16[1,256,256]{2,1,0:T(8,128)(2,1)S(1)}, u32[]{:S(2)}, u32[]{:S(2)}) collective-permute-start(bf16[1,256,256]{2,1,0:T(8,128)(2,1)S(1)} %fusion.30), channel_id=1, source_target_pairs={{0,4},{1,5},{2,6},{3,7},{4,0},{5,1},{6,2},{7,3},{8,12},{9,13},{10,... | collective-permute-start | bytes 393224 | tf_op jit(solution)/shard_map/ppermute | solution.py:83
  52.2 2.0 %collective-permute-done.13 = bf16[192,256]{1,0:T(8,128)(2,1)S(1)} collective-permute-done((bf16[192,256]{1,0:T(8,128)(2,1)S(1)}, bf16[192,256]{1,0:T(8,128)(2,1)S(1)}, u32[]{:S(2)}, u32[]{:S(2)}) %collective-permute-start.13) | collective-permute-done | bytes 98336 | tf_op jit(solution)/shard_map/ppermute | solution.py:83
  54.3 1.5 %collective-permute-start.14 = (bf16[192,256]{1,0:T(8,128)(2,1)S(1)}, bf16[192,256]{1,0:T(8,128)(2,1)S(1)}, u32[]{:S(2)}, u32[]{:S(2)}) collective-permute-start(bf16[192,256]{1,0:T(8,128)(2,1)S(1)} %add_convert_fusion.2), channel_id=1, source_target_pairs={{0,1},{1,0},{2,3},{3,2},{4,5},{5,4},{6,7},{7,6},{8,9},{9,8},{10,11... | collective-permute-start | bytes 294920 | tf_op jit(solution)/shard_map/ppermute | solution.py:83
  55.8 2.4 %collective-permute-start.8 = (bf16[2,256,256]{2,1,0:T(8,128)(2,1)S(1)}, bf16[2,256,256]{2,1,0:T(8,128)(2,1)S(1)}, u32[]{:S(2)}, u32[]{:S(2)}) collective-permute-start(bf16[2,256,256]{2,1,0:T(8,128)(2,1)S(1)} %fusion.26), channel_id=1, source_target_pairs={{0,2},{1,3},{2,0},{3,1},{4,6},{5,7},{6,4},{7,5},{8,10},{9,11},{10,... | collective-permute-start | bytes 786440 | tf_op jit(solution)/shard_map/ppermute | solution.py:83
  58.3 0.7 collective-permute-done.14
  59.0 3.6 %collective-permute-done.8 = bf16[2,256,256]{2,1,0:T(8,128)(2,1)S(1)} collective-permute-done((bf16[2,256,256]{2,1,0:T(8,128)(2,1)S(1)}, bf16[2,256,256]{2,1,0:T(8,128)(2,1)S(1)}, u32[]{:S(2)}, u32[]{:S(2)}) %collective-permute-start.8) | collective-permute-done | bytes 262176 | tf_op jit(solution)/shard_map/ppermute | solution.py:83
  62.8 4.9 %collective-permute-start.9 = (bf16[1,256,256]{2,1,0:T(8,128)(2,1)S(1)}, bf16[1,256,256]{2,1,0:T(8,128)(2,1)S(1)}, u32[]{:S(2)}, u32[]{:S(2)}) collective-permute-start(bf16[1,256,256]{2,1,0:T(8,128)(2,1)S(1)} %fusion.29), channel_id=1, source_target_pairs={{0,4},{1,5},{2,6},{3,7},{4,0},{5,1},{6,2},{7,3},{8,12},{9,13},{10,... | collective-permute-start | bytes 393224 | tf_op jit(solution)/shard_map/ppermute | solution.py:83
  67.9 1.3 %collective-permute-done.16.other = bf16[384,256]{1,0:T(8,128)(2,1)S(1)} collective-permute-done((bf16[384,256]{1,0:T(8,128)(2,1)S(1)}, bf16[384,256]{1,0:T(8,128)(2,1)S(1)}, u32[]{:S(2)}, u32[]{:S(2)}) %collective-permute-start.16) | collective-permute-done | bytes 196640 | tf_op jit(solution)/shard_map/ppermute | solution.py:86
  70.0 2.3 %shard_map.128 = (bf16[256,256]{1,0:T(8,128)(2,1)}, bf16[256,256]{1,0:T(8,128)(2,1)}, bf16[256,256]{1,0:T(8,128)(2,1)}) custom-call(s32[1]{0:T(128)} %bitcast.26.place, bf16[384,256]{1,0:T(8,128)(2,1)} %copy-done, bf16[384,256]{1,0:T(8,128)(2,1)} %copy-done.5, bf16[256,256]{1,0:T(8,128)(2,1)} %link.1, f32[256,256]{1,0:T(8,128)} %inverse_one.1, ...), custom_call_target="tpu_custom_call" | custom-call | flops 100663296 | bytes 1572864 | tf_op jit(solution)/shard_map/pallas_call | solution.py:29
  72.3 0.9 %fusion.34 = bf16[1,256,256]{2,1,0:T(8,128)(2,1)} fusion(f32[2,1,256,256]{3,2,1,0:T(8,128)S(1)} %convert_add_fusion, s32[]{:T(128)S(6)} %select_n.152, bf16[1,256,256]{2,1,0:T(8,128)(2,1)S(1)} %collective-permute-done.9, bf16[256,256]{1,0:T(8,128)(2,1)S(1)} %copy-done.2, bf16[1,256,256]{2,1,0:T(8,128)(2,1)S(1)} %fusion.33, ...), kind=kOutput, calls=%fused_computation.61 | convolution fusion | flops 34013184 | bytes 917512 | tf_op jit(solution)/shard_map/dot_general | solution.py:160
  (55 shorter events, 4.9 us)
Async XLA Ops:
  1.7 11.6 %collective-permute-start = (bf16[4,256,256]{2,1,0:T(8,128)(2,1)S(1)}, bf16[4,256,256]{2,1,0:T(8,128)(2,1)S(1)}, u32[]{:S(2)}, u32[]{:S(2)}) collective-permute-start(bf16[4,256,256]{2,1,0:T(8,128)(2,1)S(1)} %constant_dynamic-slice_fusion.3), channel_id=1, source_target_pairs={{0,16},{1,17},{10,26},{11,27},{20,4},{21,5},{30,14},{31,15}} | collective-permute-start | bytes 1572872 | tf_op jit(solution)/shard_map/ppermute | solution.py:70
  7.7 11.2 %collective-permute-start.5 = (bf16[4,256,256]{2,1,0:T(8,128)(2,1)S(1)}, bf16[4,256,256]{2,1,0:T(8,128)(2,1)S(1)}, u32[]{:S(2)}, u32[]{:S(2)}) collective-permute-start(bf16[4,256,256]{2,1,0:T(8,128)(2,1)S(1)} %constant_dynamic-slice_fusion.1), channel_id=1, source_target_pairs={{0,16},{1,17},{10,26},{11,27},{20,4},{21,5},{30,14},{31,15}} | collective-permute-start | bytes 1572872 | tf_op jit(solution)/shard_map/ppermute | solution.py:70
  13.4 5.6 %collective-permute-start.1 = (bf16[4,256,256]{2,1,0:T(8,128)(2,1)S(1)}, bf16[4,256,256]{2,1,0:T(8,128)(2,1)S(1)}, u32[]{:S(2)}, u32[]{:S(2)}) collective-permute-start(bf16[4,256,256]{2,1,0:T(8,128)(2,1)S(1)} %broadcast_select_fusion.2), channel_id=1, source_target_pairs={{0,8},{1,9},{10,2},{11,3},{4,12},{5,13},{14,6},{15,7},{16,24},{17,... | collective-permute-start | bytes 1572872 | tf_op jit(solution)/shard_map/ppermute | solution.py:80
  19.0 6.7 %copy-start.3 = (bf16[8,256,256]{2,1,0:T(8,128)(2,1)S(1)}, bf16[8,256,256]{2,1,0:T(8,128)(2,1)}, u32[]{:S(2)}) copy-start(bf16[8,256,256]{2,1,0:T(8,128)(2,1)} %param.13) | copy-start | bytes 3145732
  22.6 3.8 %copy-start.4 = (bf16[8,256,256]{2,1,0:T(8,128)(2,1)S(1)}, bf16[8,256,256]{2,1,0:T(8,128)(2,1)}, u32[]{:S(2)}) copy-start(bf16[8,256,256]{2,1,0:T(8,128)(2,1)} %param.14) | copy-start | bytes 3145732
  22.6 4.3 %collective-permute-start.6 = (bf16[4,256,256]{2,1,0:T(8,128)(2,1)S(1)}, bf16[4,256,256]{2,1,0:T(8,128)(2,1)S(1)}, u32[]{:S(2)}, u32[]{:S(2)}) collective-permute-start(bf16[4,256,256]{2,1,0:T(8,128)(2,1)S(1)} %broadcast_select_fusion.1), channel_id=1, source_target_pairs={{0,8},{1,9},{10,2},{11,3},{4,12},{5,13},{14,6},{15,7},{16,24},{17,... | collective-permute-start | bytes 1572872 | tf_op jit(solution)/shard_map/ppermute | solution.py:80
  24.0 2.9 %copy-start.6 = (bf16[8,4,256,256]{3,2,1,0:T(8,128)(2,1)S(1)}, bf16[8,4,256,256]{3,2,1,0:T(8,128)(2,1)}, u32[]{:S(2)}) copy-start(bf16[8,4,256,256]{3,2,1,0:T(8,128)(2,1)} %param.9) | copy-start | bytes 12582916
  24.1 14.3 %collective-permute-start.2 = (bf16[4,256,256]{2,1,0:T(8,128)(2,1)S(1)}, bf16[4,256,256]{2,1,0:T(8,128)(2,1)S(1)}, u32[]{:S(2)}, u32[]{:S(2)}) collective-permute-start(bf16[4,256,256]{2,1,0:T(8,128)(2,1)S(1)} %get-tuple-element.37), channel_id=1, source_target_pairs={{0,1},{1,0},{2,3},{3,2},{4,5},{5,4},{6,7},{7,6},{8,9},{9,8},{10,11... | collective-permute-start | bytes 1572872 | tf_op jit(solution)/shard_map/ppermute | solution.py:83
  29.1 1.5 %collective-permute-start.10 = (bf16[384,256]{1,0:T(8,128)(2,1)S(1)}, bf16[384,256]{1,0:T(8,128)(2,1)S(1)}, u32[]{:S(2)}, u32[]{:S(2)}) collective-permute-start(bf16[384,256]{1,0:T(8,128)(2,1)S(1)} %dynamic-slice_convert_fusion), channel_id=1, source_target_pairs={{0,8},{1,9},{2,10},{3,11},{4,12},{5,13},{6,14},{7,15},{8,0},{9,1},... | collective-permute-start | bytes 589832 | tf_op jit(solution)/shard_map/ppermute | solution.py:86
  29.3 25.0 %collective-permute-start.7 = (bf16[4,256,256]{2,1,0:T(8,128)(2,1)S(1)}, bf16[4,256,256]{2,1,0:T(8,128)(2,1)S(1)}, u32[]{:S(2)}, u32[]{:S(2)}) collective-permute-start(bf16[4,256,256]{2,1,0:T(8,128)(2,1)S(1)} %get-tuple-element.35), channel_id=1, source_target_pairs={{0,1},{1,0},{2,3},{3,2},{4,5},{5,4},{6,7},{7,6},{8,9},{9,8},{10,11... | collective-permute-start | bytes 1572872 | tf_op jit(solution)/shard_map/ppermute | solution.py:83
  30.6 8.0 %collective-permute-start.11 = (bf16[192,256]{1,0:T(8,128)(2,1)S(1)}, bf16[192,256]{1,0:T(8,128)(2,1)S(1)}, u32[]{:S(2)}, u32[]{:S(2)}) collective-permute-start(bf16[192,256]{1,0:T(8,128)(2,1)S(1)} %dynamic-slice_convert_fusion.1), channel_id=1, source_target_pairs={{0,16},{1,17},{2,18},{3,19},{4,20},{5,21},{6,22},{7,23},{8,24},{9,... | collective-permute-start | bytes 294920 | tf_op jit(solution)/shard_map/ppermute | solution.py:86
  38.5 12.4 %collective-permute-start.3 = (bf16[2,256,256]{2,1,0:T(8,128)(2,1)S(1)}, bf16[2,256,256]{2,1,0:T(8,128)(2,1)S(1)}, u32[]{:S(2)}, u32[]{:S(2)}) collective-permute-start(bf16[2,256,256]{2,1,0:T(8,128)(2,1)S(1)} %get-tuple-element.33), channel_id=1, source_target_pairs={{0,2},{1,3},{2,0},{3,1},{4,6},{5,7},{6,4},{7,5},{8,10},{9,11},{10,... | collective-permute-start | bytes 786440 | tf_op jit(solution)/shard_map/ppermute | solution.py:83
  38.7 33.6 %copy-start.2 = (bf16[256,256]{1,0:T(8,128)(2,1)S(1)}, bf16[256,256]{1,0:T(8,128)(2,1)}, u32[]{:S(2)}) copy-start(bf16[256,256]{1,0:T(8,128)(2,1)} %link.1) | copy-start | bytes 393220
  38.7 8.2 %collective-permute-start.12 = (bf16[192,256]{1,0:T(8,128)(2,1)S(1)}, bf16[192,256]{1,0:T(8,128)(2,1)S(1)}, u32[]{:S(2)}, u32[]{:S(2)}) collective-permute-start(bf16[192,256]{1,0:T(8,128)(2,1)S(1)} %add_convert_fusion.4), channel_id=1, source_target_pairs={{0,4},{1,5},{2,6},{3,7},{4,0},{5,1},{6,2},{7,3},{8,12},{9,13},{10,... | collective-permute-start | bytes 294920 | tf_op jit(solution)/shard_map/ppermute | solution.py:83
  46.9 7.3 %collective-permute-start.13 = (bf16[192,256]{1,0:T(8,128)(2,1)S(1)}, bf16[192,256]{1,0:T(8,128)(2,1)S(1)}, u32[]{:S(2)}, u32[]{:S(2)}) collective-permute-start(bf16[192,256]{1,0:T(8,128)(2,1)S(1)} %add_convert_fusion.3), channel_id=1, source_target_pairs={{0,2},{1,3},{2,0},{3,1},{4,6},{5,7},{6,4},{7,5},{8,10},{9,11},{10,... | collective-permute-start | bytes 294920 | tf_op jit(solution)/shard_map/ppermute | solution.py:83
  50.9 16.8 %collective-permute-start.4 = (bf16[1,256,256]{2,1,0:T(8,128)(2,1)S(1)}, bf16[1,256,256]{2,1,0:T(8,128)(2,1)S(1)}, u32[]{:S(2)}, u32[]{:S(2)}) collective-permute-start(bf16[1,256,256]{2,1,0:T(8,128)(2,1)S(1)} %fusion.30), channel_id=1, source_target_pairs={{0,4},{1,5},{2,6},{3,7},{4,0},{5,1},{6,2},{7,3},{8,12},{9,13},{10,... | collective-permute-start | bytes 393224 | tf_op jit(solution)/shard_map/ppermute | solution.py:83
  54.3 4.7 %collective-permute-start.14 = (bf16[192,256]{1,0:T(8,128)(2,1)S(1)}, bf16[192,256]{1,0:T(8,128)(2,1)S(1)}, u32[]{:S(2)}, u32[]{:S(2)}) collective-permute-start(bf16[192,256]{1,0:T(8,128)(2,1)S(1)} %add_convert_fusion.2), channel_id=1, source_target_pairs={{0,1},{1,0},{2,3},{3,2},{4,5},{5,4},{6,7},{7,6},{8,9},{9,8},{10,11... | collective-permute-start | bytes 294920 | tf_op jit(solution)/shard_map/ppermute | solution.py:83
  55.8 6.8 %collective-permute-start.8 = (bf16[2,256,256]{2,1,0:T(8,128)(2,1)S(1)}, bf16[2,256,256]{2,1,0:T(8,128)(2,1)S(1)}, u32[]{:S(2)}, u32[]{:S(2)}) collective-permute-start(bf16[2,256,256]{2,1,0:T(8,128)(2,1)S(1)} %fusion.26), channel_id=1, source_target_pairs={{0,2},{1,3},{2,0},{3,1},{4,6},{5,7},{6,4},{7,5},{8,10},{9,11},{10,... | collective-permute-start | bytes 786440 | tf_op jit(solution)/shard_map/ppermute | solution.py:83
  62.6 5.1 %collective-permute-start.15 = (bf16[192,256]{1,0:T(8,128)(2,1)S(1)}, bf16[192,256]{1,0:T(8,128)(2,1)S(1)}, u32[]{:S(2)}, u32[]{:S(2)}) collective-permute-start(bf16[192,256]{1,0:T(8,128)(2,1)S(1)} %add_convert_fusion.1), channel_id=1, source_target_pairs={{0,16},{1,17},{2,18},{3,19},{4,20},{5,21},{6,22},{7,23},{8,24},{9,... | collective-permute-start | bytes 294920 | tf_op jit(solution)/shard_map/ppermute | solution.py:86
  62.8 9.5 %collective-permute-start.9 = (bf16[1,256,256]{2,1,0:T(8,128)(2,1)S(1)}, bf16[1,256,256]{2,1,0:T(8,128)(2,1)S(1)}, u32[]{:S(2)}, u32[]{:S(2)}) collective-permute-start(bf16[1,256,256]{2,1,0:T(8,128)(2,1)S(1)} %fusion.29), channel_id=1, source_target_pairs={{0,4},{1,5},{2,6},{3,7},{4,0},{5,1},{6,2},{7,3},{8,12},{9,13},{10,... | collective-permute-start | bytes 393224 | tf_op jit(solution)/shard_map/ppermute | solution.py:83
  67.8 1.5 %copy-start = (bf16[384,256]{1,0:T(8,128)(2,1)}, bf16[384,256]{1,0:T(8,128)(2,1)S(1)}, u32[]{:S(2)}) copy-start(bf16[384,256]{1,0:T(8,128)(2,1)S(1)} %pad_maximum_fusion.1.mine) | copy-start | bytes 589828
  67.8 1.5 %collective-permute-start.16 = (bf16[384,256]{1,0:T(8,128)(2,1)S(1)}, bf16[384,256]{1,0:T(8,128)(2,1)S(1)}, u32[]{:S(2)}, u32[]{:S(2)}) collective-permute-start(bf16[384,256]{1,0:T(8,128)(2,1)S(1)} %pad_maximum_fusion.1.mine), channel_id=1, source_target_pairs={{0,8},{1,9},{2,10},{3,11},{4,12},{5,13},{6,14},{7,15},{8,0},{9,1},... | collective-permute-start | bytes 589832 | tf_op jit(solution)/shard_map/ppermute | solution.py:86
  67.9 5.2 %copy-start.1 = (bf16[1,256,256]{2,1,0:T(8,128)(2,1)}, bf16[1,256,256]{2,1,0:T(8,128)(2,1)S(1)}, u32[]{:S(2)}) copy-start(bf16[1,256,256]{2,1,0:T(8,128)(2,1)S(1)} %fusion.33) | copy-start | bytes 393220
  69.3 0.7 copy-start.5

commit v6 on v5

--- a/solution.py
+++ b/solution.py
@@ -96,8 +96,9 @@
     def next_swap(keep, arrived):
         bit = len(arrived)
         away, keep = (pick(keep, bit, other) + pick(arrived[-1], bit, other) for other in (1, 0))
-        arrived.append(swap(away.astype(BF16), bit))
-        return keep
+        away = away.astype(BF16)
+        arrived.append(swap(away, bit))
+        return keep, away
 
     def part_of(array, start, size):
         return lax.dynamic_slice_in_dim(array, start, size, 0)
@@ -126,8 +127,8 @@
     keep_two, two = first_swap(all_two)
     sums = contraction(first, all_one), contraction(all_one, second_in_one), contraction(second, all_two)
     for _ in range(1, bits):
-        keep_one = next_swap(keep_one, one)
-        keep_two = next_swap(keep_two, two)
+        keep_one, _ = next_swap(keep_one, one)
+        keep_two, last = next_swap(keep_two, two)
 
     sums = jnp.stack(sums)
     part = sums.reshape(-1, tile)
@@ -141,24 +142,25 @@
     for bit in reversed(range(bits)):
         got = swap(after(part, *gates.get(bit, ())), bit)
         part = (part.astype(F32) + got.astype(F32)).astype(BF16)
+    one_last = after(one[-1], part)
     for bit in reversed(range(row_bits)):
-        got = swap_rows(after(part, one[-1] if bit == 0 else two[-2]), bit)
+        got = swap_rows(after(part, *((one_last, last) if bit == 0 else ())), bit)
         if bit:
             low = (row >> bit & 1) == 0
             part = jnp.concatenate([jnp.where(low, part, got), jnp.where(low, got, part)])
 
+    member_one, member_two = (m[row * rows + col].astype(F32) for m in (member_one, member_two))
+    column_one = (-member_one * (keep_one[0] + one_last[0].astype(F32))).astype(BF16)
+    linked = jnp.dot(column_one, link_block, preferred_element_type=F32) + keep_two[0]
+    column_two = (-member_two * (linked + two[-1][0].astype(F32))).astype(BF16)
     diag_one, cross_block, diag_two = small_kernel(
         diagonal_kernel,
         3,
         3,
         tile,
-        ((row & 1)[None], part, got, link_block, inverse_one, inverse_two),
+        ((row & 1)[None], part, after(got, column_two), link_block, inverse_one, inverse_two),
         1,
     )
-    member_one, member_two = (m[row * rows + col].astype(F32) for m in (member_one, member_two))
-    column_one = (-member_one * (keep_one[0] + one[-1][0].astype(F32))).astype(BF16)
-    linked = jnp.dot(column_one, link_block, preferred_element_type=F32) + keep_two[0]
-    column_two = (-member_two * (linked + after(two[-1], diag_two)[0].astype(F32))).astype(BF16)
     return (column_one[None], column_two[None], diag_one, cross_block, diag_two)
 
 

time: 74.3 us -> 75.1 us (1.011)
  waiting for transfers between devices: 19.1 us -> 21 us
    ppermute x9, waiting for transfers between devices: 16 us -> 19.1 us  [swap(): lax.ppermute(array, BOTH, [(at(r, c), at(r, c ^ 1 << bit)) for r, c in ev...]
    ppermute x4, waiting for transfers between devices: 1.76 us -> 0.41 us  [swap_rows(): lax.ppermute(array, BOTH, [(at(r, c), at(r ^ 1 << bit, c)) for r, c in ev...]
    ppermute x9, starting transfers between devices: 20.2 us -> 19 us  [swap(): lax.ppermute(array, BOTH, [(at(r, c), at(r, c ^ 1 << bit)) for r, c in ev...]
    ppermute x4, starting transfers between devices: 2.91 us -> 3.68 us  [swap_rows(): lax.ppermute(array, BOTH, [(at(r, c), at(r ^ 1 << bit, c)) for r, c in ev...]
  transfers between devices with their start and end apart: 17 -> 17, of which waited for: 9 -> 9; matrix products, arithmetic and copies ran while one was open for 15% -> 16% of each run, Pallas kernels for 3% -> 0%
where the time goes in v6:
time: 75.1 us; the launch traced here: 74.5 us
  starting transfers between devices  31.6 us (42%)
  waiting for transfers between devices  21 us (28%)
  matrix products  7.62 us (10%)
  local copies, waits for them, and re-layouts  7.21 us (10%)
  between operations  2.39 us (3%)
  other arithmetic  2.36 us (3%)
  Pallas kernels  2.32 us (3%)
    ppermute x9, waiting for transfers between devices, swap(): lax.ppermute(array, BOTH, [(at(r, c), at(r, c ^ 1 << bit)) for r, c in ev...  19.1 us
    ppermute x9, starting transfers between devices, swap(): lax.ppermute(array, BOTH, [(at(r, c), at(r, c ^ 1 << bit)) for r, c in ev...  19 us
    ppermute x2, starting transfers between devices, over_chips(): got = after(lax.ppermute(piece, BOTH, perm), *earlier)  6.23 us
    dot_general x2, matrix products, products(): jnp.einsum('ijab,jbc->iac', kept, column, preferred_element_type=F32)  4.9 us
    ppermute x4, starting transfers between devices, swap_rows(): lax.ppermute(array, BOTH, [(at(r, c), at(r ^ 1 << bit, c)) for r, c in ev...  3.68 us
    dynamic_slice x4, local copies, waits for them, and re-layouts, part_of(): return lax.dynamic_slice_in_dim(array, start, size, 0)  3.62 us
    ppermute x2, starting transfers between devices, over_cores(): lax.ppermute(have, BOTH, perm)  2.78 us
    dynamic_slice x2, local copies, waits for them, and re-layouts, shards(): m[row * rows + col].astype(F32)  2.48 us
  transfers between devices with their start and end apart: 17, of which 9 were waited for; matrix products, arithmetic and copies ran while one was open for 16% of the time, Pallas kernels for 0%

profile of v6, /device:TPU:0, one launch (start us, length us, event | category | flops | bytes accessed | tf_op | source)
XLA Modules:
  0.0 74.5 jit_solution(3899040552824377137)
XLA Ops:
  0.6 1.1 %constant_dynamic-slice_fusion.3 = bf16[4,256,256]{2,1,0:T(8,128)(2,1)S(1)} fusion(bf16[8,256,256]{2,1,0:T(8,128)(2,1)} %param.13, s32[]{:T(128)S(6)} %select_n.145), kind=kLoop, calls=%fused_computation.68 | loop fusion | bytes 1048580 | tf_op jit(solution)/shard_map/dynamic_slice | solution.py:104
  1.7 4.9 %collective-permute-start = (bf16[4,256,256]{2,1,0:T(8,128)(2,1)S(1)}, bf16[4,256,256]{2,1,0:T(8,128)(2,1)S(1)}, u32[]{:S(2)}, u32[]{:S(2)}) collective-permute-start(bf16[4,256,256]{2,1,0:T(8,128)(2,1)S(1)} %constant_dynamic-slice_fusion.3), channel_id=1, source_target_pairs={{0,16},{1,17},{10,26},{11,27},{20,4},{21,5},{30,14},{31,15}} | collective-permute-start | bytes 1572872 | tf_op jit(solution)/shard_map/ppermute | solution.py:70
  6.6 1.1 %constant_dynamic-slice_fusion.1 = bf16[4,256,256]{2,1,0:T(8,128)(2,1)S(1)} fusion(bf16[8,256,256]{2,1,0:T(8,128)(2,1)} %param.14, s32[]{:T(128)S(6)} %select_n.145), kind=kLoop, calls=%fused_computation.66 | loop fusion | bytes 1048580 | tf_op jit(solution)/shard_map/dynamic_slice | solution.py:104
  7.7 1.3 %collective-permute-start.5 = (bf16[4,256,256]{2,1,0:T(8,128)(2,1)S(1)}, bf16[4,256,256]{2,1,0:T(8,128)(2,1)S(1)}, u32[]{:S(2)}, u32[]{:S(2)}) collective-permute-start(bf16[4,256,256]{2,1,0:T(8,128)(2,1)S(1)} %constant_dynamic-slice_fusion.1), channel_id=1, source_target_pairs={{0,16},{1,17},{10,26},{11,27},{20,4},{21,5},{30,14},{31,15}} | collective-permute-start | bytes 1572872 | tf_op jit(solution)/shard_map/ppermute | solution.py:70
  9.1 0.7 dynamic_slice.81
  9.8 0.7 dynamic_slice.83
  10.6 0.7 %broadcast_compare_fusion.2 = (pred[8]{0:T(512)(128)(4,1)S(1)}, pred[8]{0:T(512)(128)(4,1)S(1)}) fusion(s32[32]{0:T(128)} %param.12, s32[]{:T(128)S(6)} %select_n.146, s32[32]{0:T(128)} %param.11), kind=kLoop, calls=%fused_computation.73 | loop fusion | flops 16 | bytes 84 | tf_op jit(solution)/shard_map/gt | solution.py:107
  11.3 0.8 %broadcast_compare_fusion = (pred[8,4]{0,1:T(4,128)(4,1)S(1)}, pred[8,4]{0,1:T(4,128)(4,1)S(1)}) fusion(s32[8,4]{0,1:T(4,128)} %param.10, s32[4]{0:T(128)S(1)} %dynamic_slice.83, s32[4]{0:T(128)S(1)} %dynamic_slice.81), kind=kLoop, calls=%fused_computation.70 | loop fusion | flops 128 | bytes 224 | tf_op jit(solution)/shard_map/gt | solution.py:107
  12.1 1.2 %collective-permute-done = bf16[4,256,256]{2,1,0:T(8,128)(2,1)S(1)} collective-permute-done((bf16[4,256,256]{2,1,0:T(8,128)(2,1)S(1)}, bf16[4,256,256]{2,1,0:T(8,128)(2,1)S(1)}, u32[]{:S(2)}, u32[]{:S(2)}) %collective-permute-start) | collective-permute-done | bytes 524320 | tf_op jit(solution)/shard_map/ppermute | solution.py:70
  13.4 1.3 %collective-permute-start.1 = (bf16[4,256,256]{2,1,0:T(8,128)(2,1)S(1)}, bf16[4,256,256]{2,1,0:T(8,128)(2,1)S(1)}, u32[]{:S(2)}, u32[]{:S(2)}) collective-permute-start(bf16[4,256,256]{2,1,0:T(8,128)(2,1)S(1)} %broadcast_select_fusion.2), channel_id=1, source_target_pairs={{0,8},{1,9},{10,2},{11,3},{4,12},{5,13},{14,6},{15,7},{16,24},{17,... | collective-permute-start | bytes 1572872 | tf_op jit(solution)/shard_map/ppermute | solution.py:80
  14.7 1.2 %dynamic_slice.80 = s32[1]{0:T(128)} dynamic-slice(s32[32]{0:T(128)} %param.11, s32[]{:T(128)S(6)} %select_n.136), dynamic_slice_sizes={1} | dynamic-slice | bytes 12 | tf_op jit(solution)/shard_map/dynamic_slice | solution.py:152
  16.0 1.2 %dynamic_slice.98 = s32[1]{0:T(128)} dynamic-slice(s32[32]{0:T(128)} %param.12, s32[]{:T(128)S(6)} %select_n.136), dynamic_slice_sizes={1} | dynamic-slice | bytes 12 | tf_op jit(solution)/shard_map/dynamic_slice | solution.py:152
  19.0 3.6 %bitcast_convert_fusion.1 = bf16[8,256,256]{2,1,0:T(8,128)(2,1)S(1)} fusion(bf16[8,4,256,256]{3,2,1,0:T(8,128)(2,1)} %param.9, pred[8,4]{1,0:T(8,128)(4,1)S(1)} %copy.19, bf16[4,256,256]{2,1,0:T(8,128)(2,1)S(1)} %broadcast_select_fusion.2, bf16[4,256,256]{2,1,0:T(8,128)(2,1)S(1)} %collective-permute-done.1, pred[]{:T(512)S(6)} %eq.18), kind=kOutput, calls=%fused_computation.7 | convolution fusion | flops 1076625408 | bytes 6291489 | tf_op jit(solution)/shard_map/ijab,jbc->iac/dot_general | solution.py:111
  22.6 1.5 %collective-permute-start.6 = (bf16[4,256,256]{2,1,0:T(8,128)(2,1)S(1)}, bf16[4,256,256]{2,1,0:T(8,128)(2,1)S(1)}, u32[]{:S(2)}, u32[]{:S(2)}) collective-permute-start(bf16[4,256,256]{2,1,0:T(8,128)(2,1)S(1)} %broadcast_select_fusion.1), channel_id=1, source_target_pairs={{0,8},{1,9},{10,2},{11,3},{4,12},{5,13},{14,6},{15,7},{16,24},{17,... | collective-permute-start | bytes 1572872 | tf_op jit(solution)/shard_map/ppermute | solution.py:80
  24.1 1.6 %collective-permute-start.2 = (bf16[4,256,256]{2,1,0:T(8,128)(2,1)S(1)}, bf16[4,256,256]{2,1,0:T(8,128)(2,1)S(1)}, u32[]{:S(2)}, u32[]{:S(2)}) collective-permute-start(bf16[4,256,256]{2,1,0:T(8,128)(2,1)S(1)} %get-tuple-element.37), channel_id=1, source_target_pairs={{0,1},{1,0},{2,3},{3,2},{4,5},{5,4},{6,7},{7,6},{8,9},{9,8},{10,11... | collective-permute-start | bytes 1572872 | tf_op jit(solution)/shard_map/ppermute | solution.py:83
  26.9 1.3 %bitcast_convert_fusion = bf16[8,256,256]{2,1,0:T(8,128)(2,1)S(1)} fusion(bf16[8,4,256,256]{3,2,1,0:T(8,128)(2,1)S(1)} %copy-done.6, pred[8,4]{1,0:T(8,128)(4,1)S(1)} %copy.23, bf16[4,256,256]{2,1,0:T(8,128)(2,1)S(1)} %broadcast_select_fusion.1, bf16[4,256,256]{2,1,0:T(8,128)(2,1)S(1)} %collective-permute-done.6, pred[]{:T(512)S(6)} %eq.18), kind=kOutput, calls=%fused_computation.6 | convolution fusion | flops 1076625408 | bytes 6291489 | tf_op jit(solution)/shard_map/ijab,jbc->iac/dot_general | solution.py:111
  29.3 0.8 %collective-permute-start.11 = (bf16[4,256,256]{2,1,0:T(8,128)(2,1)S(1)}, bf16[4,256,256]{2,1,0:T(8,128)(2,1)S(1)}, u32[]{:S(2)}, u32[]{:S(2)}) collective-permute-start(bf16[4,256,256]{2,1,0:T(8,128)(2,1)S(1)} %get-tuple-element.36), channel_id=1, source_target_pairs={{0,1},{1,0},{2,3},{3,2},{4,5},{5,4},{6,7},{7,6},{8,9},{9,8},{10,11... | collective-permute-start | bytes 1572872 | tf_op jit(solution)/shard_map/ppermute | solution.py:83
  30.6 2.6 %collective-permute-start.8 = (bf16[192,256]{1,0:T(8,128)(2,1)S(1)}, bf16[192,256]{1,0:T(8,128)(2,1)S(1)}, u32[]{:S(2)}, u32[]{:S(2)}) collective-permute-start(bf16[192,256]{1,0:T(8,128)(2,1)S(1)} %dynamic-slice_convert_fusion.1), channel_id=1, source_target_pairs={{0,16},{1,17},{2,18},{3,19},{4,20},{5,21},{6,22},{7,23},{8,24},{9,... | collective-permute-start | bytes 294920 | tf_op jit(solution)/shard_map/ppermute | solution.py:86
  33.2 5.2 %collective-permute-done.2 = bf16[4,256,256]{2,1,0:T(8,128)(2,1)S(1)} collective-permute-done((bf16[4,256,256]{2,1,0:T(8,128)(2,1)S(1)}, bf16[4,256,256]{2,1,0:T(8,128)(2,1)S(1)}, u32[]{:S(2)}, u32[]{:S(2)}) %collective-permute-start.2) | collective-permute-done | bytes 524320 | tf_op jit(solution)/shard_map/ppermute | solution.py:83
  38.7 3.6 %collective-permute-start.9 = (bf16[192,256]{1,0:T(8,128)(2,1)S(1)}, bf16[192,256]{1,0:T(8,128)(2,1)S(1)}, u32[]{:S(2)}, u32[]{:S(2)}) collective-permute-start(bf16[192,256]{1,0:T(8,128)(2,1)S(1)} %add_convert_fusion.4), channel_id=1, source_target_pairs={{0,4},{1,5},{2,6},{3,7},{4,0},{5,1},{6,2},{7,3},{8,12},{9,13},{10,... | collective-permute-start | bytes 294920 | tf_op jit(solution)/shard_map/ppermute | solution.py:83
  42.4 4.5 %collective-permute-done.9 = bf16[192,256]{1,0:T(8,128)(2,1)S(1)} collective-permute-done((bf16[192,256]{1,0:T(8,128)(2,1)S(1)}, bf16[192,256]{1,0:T(8,128)(2,1)S(1)}, u32[]{:S(2)}, u32[]{:S(2)}) %collective-permute-start.9) | collective-permute-done | bytes 98336 | tf_op jit(solution)/shard_map/ppermute | solution.py:83
  46.9 4.0 %collective-permute-start.10 = (bf16[192,256]{1,0:T(8,128)(2,1)S(1)}, bf16[192,256]{1,0:T(8,128)(2,1)S(1)}, u32[]{:S(2)}, u32[]{:S(2)}) collective-permute-start(bf16[192,256]{1,0:T(8,128)(2,1)S(1)} %add_convert_fusion.3), channel_id=1, source_target_pairs={{0,2},{1,3},{2,0},{3,1},{4,6},{5,7},{6,4},{7,5},{8,10},{9,11},{10,... | collective-permute-start | bytes 294920 | tf_op jit(solution)/shard_map/ppermute | solution.py:83
  51.0 1.3 %collective-permute-start.4 = (bf16[1,256,256]{2,1,0:T(8,128)(2,1)S(1)}, bf16[1,256,256]{2,1,0:T(8,128)(2,1)S(1)}, u32[]{:S(2)}, u32[]{:S(2)}) collective-permute-start(bf16[1,256,256]{2,1,0:T(8,128)(2,1)S(1)} %fusion.30), channel_id=1, source_target_pairs={{0,4},{1,5},{2,6},{3,7},{4,0},{5,1},{6,2},{7,3},{8,12},{9,13},{10,... | collective-permute-start | bytes 393224 | tf_op jit(solution)/shard_map/ppermute | solution.py:83
  52.2 2.0 %collective-permute-done.10 = bf16[192,256]{1,0:T(8,128)(2,1)S(1)} collective-permute-done((bf16[192,256]{1,0:T(8,128)(2,1)S(1)}, bf16[192,256]{1,0:T(8,128)(2,1)S(1)}, u32[]{:S(2)}, u32[]{:S(2)}) %collective-permute-start.10) | collective-permute-done | bytes 98336 | tf_op jit(solution)/shard_map/ppermute | solution.py:83
  54.3 1.5 %collective-permute-start.12 = (bf16[192,256]{1,0:T(8,128)(2,1)S(1)}, bf16[192,256]{1,0:T(8,128)(2,1)S(1)}, u32[]{:S(2)}, u32[]{:S(2)}) collective-permute-start(bf16[192,256]{1,0:T(8,128)(2,1)S(1)} %add_convert_fusion.2), channel_id=1, source_target_pairs={{0,1},{1,0},{2,3},{3,2},{4,5},{5,4},{6,7},{7,6},{8,9},{9,8},{10,11... | collective-permute-start | bytes 294920 | tf_op jit(solution)/shard_map/ppermute | solution.py:83
  55.8 2.4 %collective-permute-start.13 = (bf16[2,256,256]{2,1,0:T(8,128)(2,1)S(1)}, bf16[2,256,256]{2,1,0:T(8,128)(2,1)S(1)}, u32[]{:S(2)}, u32[]{:S(2)}) collective-permute-start(bf16[2,256,256]{2,1,0:T(8,128)(2,1)S(1)} %fusion.26), channel_id=1, source_target_pairs={{0,2},{1,3},{2,0},{3,1},{4,6},{5,7},{6,4},{7,5},{8,10},{9,11},{10,... | collective-permute-start | bytes 786440 | tf_op jit(solution)/shard_map/ppermute | solution.py:83
  59.0 1.0 %collective-permute-start.15 = (bf16[192,256]{1,0:T(8,128)(2,1)S(1)}, bf16[192,256]{1,0:T(8,128)(2,1)S(1)}, u32[]{:S(2)}, u32[]{:S(2)}) collective-permute-start(bf16[192,256]{1,0:T(8,128)(2,1)S(1)} %add_convert_fusion.1), channel_id=1, source_target_pairs={{0,16},{1,17},{2,18},{3,19},{4,20},{5,21},{6,22},{7,23},{8,24},{9,... | collective-permute-start | bytes 294920 | tf_op jit(solution)/shard_map/ppermute | solution.py:86
  60.1 3.9 %collective-permute-done.13 = bf16[2,256,256]{2,1,0:T(8,128)(2,1)S(1)} collective-permute-done((bf16[2,256,256]{2,1,0:T(8,128)(2,1)S(1)}, bf16[2,256,256]{2,1,0:T(8,128)(2,1)S(1)}, u32[]{:S(2)}, u32[]{:S(2)}) %collective-permute-start.13) | collective-permute-done | bytes 262176 | tf_op jit(solution)/shard_map/ppermute | solution.py:83
  64.0 3.7 %collective-permute-start.14 = (bf16[1,256,256]{2,1,0:T(8,128)(2,1)S(1)}, bf16[1,256,256]{2,1,0:T(8,128)(2,1)S(1)}, u32[]{:S(2)}, u32[]{:S(2)}) collective-permute-start(bf16[1,256,256]{2,1,0:T(8,128)(2,1)S(1)} %fusion.29), channel_id=1, source_target_pairs={{0,4},{1,5},{2,6},{3,7},{4,0},{5,1},{6,2},{7,3},{8,12},{9,13},{10,... | collective-permute-start | bytes 393224 | tf_op jit(solution)/shard_map/ppermute | solution.py:83
  67.8 2.8 %collective-permute-done.14 = bf16[1,256,256]{2,1,0:T(8,128)(2,1)S(1)} collective-permute-done((bf16[1,256,256]{2,1,0:T(8,128)(2,1)S(1)}, bf16[1,256,256]{2,1,0:T(8,128)(2,1)S(1)}, u32[]{:S(2)}, u32[]{:S(2)}) %collective-permute-start.14) | collective-permute-done | bytes 131104 | tf_op jit(solution)/shard_map/ppermute | solution.py:83
  70.7 0.9 %fusion.28 = bf16[256,256]{1,0:T(8,128)(2,1)} fusion(f32[2,1,256,256]{3,2,1,0:T(8,128)S(1)} %convert_add_fusion, s32[]{:T(128)S(6)} %select_n.152, bf16[1,256,256]{2,1,0:T(8,128)(2,1)S(1)} %collective-permute-done.14, bf16[256,256]{1,0:T(8,128)(2,1)S(1)} %copy-done.2, bf16[1,256,256]{2,1,0:T(8,128)(2,1)S(1)} %fusion.33, ...), kind=kOutput, calls=%fused_computation.44 | convolution fusion | flops 34013184 | bytes 917512 | tf_op jit(solution)/shard_map/dot_general | solution.py:154
  72.2 2.3 %shard_map.128 = (bf16[256,256]{1,0:T(8,128)(2,1)}, bf16[256,256]{1,0:T(8,128)(2,1)}, bf16[256,256]{1,0:T(8,128)(2,1)}) custom-call(s32[1]{0:T(128)} %bitcast.35.place, bf16[384,256]{1,0:T(8,128)(2,1)} %copy-done, bf16[384,256]{1,0:T(8,128)(2,1)} %copy-done.5, bf16[256,256]{1,0:T(8,128)(2,1)} %link.1, f32[256,256]{1,0:T(8,128)} %inverse_one.1, ...), custom_call_target="tpu_custom_call" | custom-call | flops 100663296 | bytes 1572864 | tf_op jit(solution)/shard_map/pallas_call | solution.py:29
  (55 shorter events, 5.3 us)
Async XLA Ops:
  1.7 11.6 %collective-permute-start = (bf16[4,256,256]{2,1,0:T(8,128)(2,1)S(1)}, bf16[4,256,256]{2,1,0:T(8,128)(2,1)S(1)}, u32[]{:S(2)}, u32[]{:S(2)}) collective-permute-start(bf16[4,256,256]{2,1,0:T(8,128)(2,1)S(1)} %constant_dynamic-slice_fusion.3), channel_id=1, source_target_pairs={{0,16},{1,17},{10,26},{11,27},{20,4},{21,5},{30,14},{31,15}} | collective-permute-start | bytes 1572872 | tf_op jit(solution)/shard_map/ppermute | solution.py:70
  7.7 11.2 %collective-permute-start.5 = (bf16[4,256,256]{2,1,0:T(8,128)(2,1)S(1)}, bf16[4,256,256]{2,1,0:T(8,128)(2,1)S(1)}, u32[]{:S(2)}, u32[]{:S(2)}) collective-permute-start(bf16[4,256,256]{2,1,0:T(8,128)(2,1)S(1)} %constant_dynamic-slice_fusion.1), channel_id=1, source_target_pairs={{0,16},{1,17},{10,26},{11,27},{20,4},{21,5},{30,14},{31,15}} | collective-permute-start | bytes 1572872 | tf_op jit(solution)/shard_map/ppermute | solution.py:70
  13.4 5.6 %collective-permute-start.1 = (bf16[4,256,256]{2,1,0:T(8,128)(2,1)S(1)}, bf16[4,256,256]{2,1,0:T(8,128)(2,1)S(1)}, u32[]{:S(2)}, u32[]{:S(2)}) collective-permute-start(bf16[4,256,256]{2,1,0:T(8,128)(2,1)S(1)} %broadcast_select_fusion.2), channel_id=1, source_target_pairs={{0,8},{1,9},{10,2},{11,3},{4,12},{5,13},{14,6},{15,7},{16,24},{17,... | collective-permute-start | bytes 1572872 | tf_op jit(solution)/shard_map/ppermute | solution.py:80
  19.0 6.7 %copy-start.3 = (bf16[8,256,256]{2,1,0:T(8,128)(2,1)S(1)}, bf16[8,256,256]{2,1,0:T(8,128)(2,1)}, u32[]{:S(2)}) copy-start(bf16[8,256,256]{2,1,0:T(8,128)(2,1)} %param.13) | copy-start | bytes 3145732
  22.6 3.8 %copy-start.4 = (bf16[8,256,256]{2,1,0:T(8,128)(2,1)S(1)}, bf16[8,256,256]{2,1,0:T(8,128)(2,1)}, u32[]{:S(2)}) copy-start(bf16[8,256,256]{2,1,0:T(8,128)(2,1)} %param.14) | copy-start | bytes 3145732
  22.6 4.3 %collective-permute-start.6 = (bf16[4,256,256]{2,1,0:T(8,128)(2,1)S(1)}, bf16[4,256,256]{2,1,0:T(8,128)(2,1)S(1)}, u32[]{:S(2)}, u32[]{:S(2)}) collective-permute-start(bf16[4,256,256]{2,1,0:T(8,128)(2,1)S(1)} %broadcast_select_fusion.1), channel_id=1, source_target_pairs={{0,8},{1,9},{10,2},{11,3},{4,12},{5,13},{14,6},{15,7},{16,24},{17,... | collective-permute-start | bytes 1572872 | tf_op jit(solution)/shard_map/ppermute | solution.py:80
  24.0 2.9 %copy-start.6 = (bf16[8,4,256,256]{3,2,1,0:T(8,128)(2,1)S(1)}, bf16[8,4,256,256]{3,2,1,0:T(8,128)(2,1)}, u32[]{:S(2)}) copy-start(bf16[8,4,256,256]{3,2,1,0:T(8,128)(2,1)} %param.9) | copy-start | bytes 12582916
  24.1 14.3 %collective-permute-start.2 = (bf16[4,256,256]{2,1,0:T(8,128)(2,1)S(1)}, bf16[4,256,256]{2,1,0:T(8,128)(2,1)S(1)}, u32[]{:S(2)}, u32[]{:S(2)}) collective-permute-start(bf16[4,256,256]{2,1,0:T(8,128)(2,1)S(1)} %get-tuple-element.37), channel_id=1, source_target_pairs={{0,1},{1,0},{2,3},{3,2},{4,5},{5,4},{6,7},{7,6},{8,9},{9,8},{10,11... | collective-permute-start | bytes 1572872 | tf_op jit(solution)/shard_map/ppermute | solution.py:83
  29.1 1.5 %collective-permute-start.7 = (bf16[384,256]{1,0:T(8,128)(2,1)S(1)}, bf16[384,256]{1,0:T(8,128)(2,1)S(1)}, u32[]{:S(2)}, u32[]{:S(2)}) collective-permute-start(bf16[384,256]{1,0:T(8,128)(2,1)S(1)} %dynamic-slice_convert_fusion), channel_id=1, source_target_pairs={{0,8},{1,9},{2,10},{3,11},{4,12},{5,13},{6,14},{7,15},{8,0},{9,1},... | collective-permute-start | bytes 589832 | tf_op jit(solution)/shard_map/ppermute | solution.py:86
  29.3 25.0 %collective-permute-start.11 = (bf16[4,256,256]{2,1,0:T(8,128)(2,1)S(1)}, bf16[4,256,256]{2,1,0:T(8,128)(2,1)S(1)}, u32[]{:S(2)}, u32[]{:S(2)}) collective-permute-start(bf16[4,256,256]{2,1,0:T(8,128)(2,1)S(1)} %get-tuple-element.36), channel_id=1, source_target_pairs={{0,1},{1,0},{2,3},{3,2},{4,5},{5,4},{6,7},{7,6},{8,9},{9,8},{10,11... | collective-permute-start | bytes 1572872 | tf_op jit(solution)/shard_map/ppermute | solution.py:83
  30.6 8.0 %collective-permute-start.8 = (bf16[192,256]{1,0:T(8,128)(2,1)S(1)}, bf16[192,256]{1,0:T(8,128)(2,1)S(1)}, u32[]{:S(2)}, u32[]{:S(2)}) collective-permute-start(bf16[192,256]{1,0:T(8,128)(2,1)S(1)} %dynamic-slice_convert_fusion.1), channel_id=1, source_target_pairs={{0,16},{1,17},{2,18},{3,19},{4,20},{5,21},{6,22},{7,23},{8,24},{9,... | collective-permute-start | bytes 294920 | tf_op jit(solution)/shard_map/ppermute | solution.py:86
  38.5 32.1 %copy-start.2 = (bf16[256,256]{1,0:T(8,128)(2,1)S(1)}, bf16[256,256]{1,0:T(8,128)(2,1)}, u32[]{:S(2)}) copy-start(bf16[256,256]{1,0:T(8,128)(2,1)} %link.1) | copy-start | bytes 393220
  38.6 12.4 %collective-permute-start.3 = (bf16[2,256,256]{2,1,0:T(8,128)(2,1)S(1)}, bf16[2,256,256]{2,1,0:T(8,128)(2,1)S(1)}, u32[]{:S(2)}, u32[]{:S(2)}) collective-permute-start(bf16[2,256,256]{2,1,0:T(8,128)(2,1)S(1)} %get-tuple-element.33), channel_id=1, source_target_pairs={{0,2},{1,3},{2,0},{3,1},{4,6},{5,7},{6,4},{7,5},{8,10},{9,11},{10,... | collective-permute-start | bytes 786440 | tf_op jit(solution)/shard_map/ppermute | solution.py:83
  38.7 8.2 %collective-permute-start.9 = (bf16[192,256]{1,0:T(8,128)(2,1)S(1)}, bf16[192,256]{1,0:T(8,128)(2,1)S(1)}, u32[]{:S(2)}, u32[]{:S(2)}) collective-permute-start(bf16[192,256]{1,0:T(8,128)(2,1)S(1)} %add_convert_fusion.4), channel_id=1, source_target_pairs={{0,4},{1,5},{2,6},{3,7},{4,0},{5,1},{6,2},{7,3},{8,12},{9,13},{10,... | collective-permute-start | bytes 294920 | tf_op jit(solution)/shard_map/ppermute | solution.py:83
  46.9 7.3 %collective-permute-start.10 = (bf16[192,256]{1,0:T(8,128)(2,1)S(1)}, bf16[192,256]{1,0:T(8,128)(2,1)S(1)}, u32[]{:S(2)}, u32[]{:S(2)}) collective-permute-start(bf16[192,256]{1,0:T(8,128)(2,1)S(1)} %add_convert_fusion.3), channel_id=1, source_target_pairs={{0,2},{1,3},{2,0},{3,1},{4,6},{5,7},{6,4},{7,5},{8,10},{9,11},{10,... | collective-permute-start | bytes 294920 | tf_op jit(solution)/shard_map/ppermute | solution.py:83
  51.0 9.0 %collective-permute-start.4 = (bf16[1,256,256]{2,1,0:T(8,128)(2,1)S(1)}, bf16[1,256,256]{2,1,0:T(8,128)(2,1)S(1)}, u32[]{:S(2)}, u32[]{:S(2)}) collective-permute-start(bf16[1,256,256]{2,1,0:T(8,128)(2,1)S(1)} %fusion.30), channel_id=1, source_target_pairs={{0,4},{1,5},{2,6},{3,7},{4,0},{5,1},{6,2},{7,3},{8,12},{9,13},{10,... | collective-permute-start | bytes 393224 | tf_op jit(solution)/shard_map/ppermute | solution.py:83
  54.3 4.7 %collective-permute-start.12 = (bf16[192,256]{1,0:T(8,128)(2,1)S(1)}, bf16[192,256]{1,0:T(8,128)(2,1)S(1)}, u32[]{:S(2)}, u32[]{:S(2)}) collective-permute-start(bf16[192,256]{1,0:T(8,128)(2,1)S(1)} %add_convert_fusion.2), channel_id=1, source_target_pairs={{0,1},{1,0},{2,3},{3,2},{4,5},{5,4},{6,7},{7,6},{8,9},{9,8},{10,11... | collective-permute-start | bytes 294920 | tf_op jit(solution)/shard_map/ppermute | solution.py:83
  55.8 8.2 %collective-permute-start.13 = (bf16[2,256,256]{2,1,0:T(8,128)(2,1)S(1)}, bf16[2,256,256]{2,1,0:T(8,128)(2,1)S(1)}, u32[]{:S(2)}, u32[]{:S(2)}) collective-permute-start(bf16[2,256,256]{2,1,0:T(8,128)(2,1)S(1)} %fusion.26), channel_id=1, source_target_pairs={{0,2},{1,3},{2,0},{3,1},{4,6},{5,7},{6,4},{7,5},{8,10},{9,11},{10,... | collective-permute-start | bytes 786440 | tf_op jit(solution)/shard_map/ppermute | solution.py:83
  59.0 8.7 %collective-permute-start.15 = (bf16[192,256]{1,0:T(8,128)(2,1)S(1)}, bf16[192,256]{1,0:T(8,128)(2,1)S(1)}, u32[]{:S(2)}, u32[]{:S(2)}) collective-permute-start(bf16[192,256]{1,0:T(8,128)(2,1)S(1)} %add_convert_fusion.1), channel_id=1, source_target_pairs={{0,16},{1,17},{2,18},{3,19},{4,20},{5,21},{6,22},{7,23},{8,24},{9,... | collective-permute-start | bytes 294920 | tf_op jit(solution)/shard_map/ppermute | solution.py:86
  60.0 14.5 %copy-start.1 = (bf16[1,256,256]{2,1,0:T(8,128)(2,1)}, bf16[1,256,256]{2,1,0:T(8,128)(2,1)S(1)}, u32[]{:S(2)}) copy-start(bf16[1,256,256]{2,1,0:T(8,128)(2,1)S(1)} %fusion.33) | copy-start | bytes 393220
  64.0 6.6 %collective-permute-start.14 = (bf16[1,256,256]{2,1,0:T(8,128)(2,1)S(1)}, bf16[1,256,256]{2,1,0:T(8,128)(2,1)S(1)}, u32[]{:S(2)}, u32[]{:S(2)}) collective-permute-start(bf16[1,256,256]{2,1,0:T(8,128)(2,1)S(1)} %fusion.29), channel_id=1, source_target_pairs={{0,4},{1,5},{2,6},{3,7},{4,0},{5,1},{6,2},{7,3},{8,12},{9,13},{10,... | collective-permute-start | bytes 393224 | tf_op jit(solution)/shard_map/ppermute | solution.py:83
  67.7 3.8 %copy-start = (bf16[384,256]{1,0:T(8,128)(2,1)}, bf16[384,256]{1,0:T(8,128)(2,1)S(1)}, u32[]{:S(2)}) copy-start(bf16[384,256]{1,0:T(8,128)(2,1)S(1)} %pad_maximum_fusion.1.mine) | copy-start | bytes 589828
  67.8 3.8 %collective-permute-start.16 = (bf16[384,256]{1,0:T(8,128)(2,1)S(1)}, bf16[384,256]{1,0:T(8,128)(2,1)S(1)}, u32[]{:S(2)}, u32[]{:S(2)}) collective-permute-start(bf16[384,256]{1,0:T(8,128)(2,1)S(1)} %pad_maximum_fusion.1.mine), channel_id=1, source_target_pairs={{0,8},{1,9},{2,10},{3,11},{4,12},{5,13},{6,14},{7,15},{8,0},{9,1},... | collective-permute-start | bytes 589832 | tf_op jit(solution)/shard_map/ppermute | solution.py:86
  71.5 0.7 copy-start.5

commit v7 on v3

--- a/solution.py
+++ b/solution.py
@@ -137,18 +137,18 @@
         got = swap_rows(lax.dynamic_slice_in_dim(part, (1 - mine) * half, half, 0).astype(BF16), bit)
         part = lax.dynamic_slice_in_dim(part, mine * half, half, 0) + got.astype(F32)
     part = part.astype(BF16)
-    gates = [one[0], *one[1:-1], two[0]]
+    gates = [one[0], two[0], *one[1:]]
     for bit, gate in zip(reversed(range(bits)), gates):
         got = swap(after(part, gate), bit)
         part = (part.astype(F32) + got.astype(F32)).astype(BF16)
     for bit in reversed(range(row_bits)):
-        got = swap_rows(after(part, *((one[-1], two[-2]) if bit == 0 else ())), bit)
+        got = swap_rows(after(part, *((two[-2], one[-1]) if bit == 0 else ())), bit)
         if bit:
             low = (row >> bit & 1) == 0
             part = jnp.concatenate([jnp.where(low, part, got), jnp.where(low, got, part)])
 
     member_one, member_two = (m[row * rows + col].astype(F32) for m in (member_one, member_two))
-    column_one = (-member_one * (keep_one[0] + one[-1][0].astype(F32))).astype(BF16)
+    column_one = (-member_one * (keep_one[0] + after(one[-1], got)[0].astype(F32))).astype(BF16)
     linked = jnp.dot(column_one, link_block, preferred_element_type=F32) + keep_two[0]
     column_two = (-member_two * (linked + two[-1][0].astype(F32))).astype(BF16)
     diag_one, cross_block, diag_two = small_kernel(
@@ -156,7 +156,7 @@
         3,
         3,
         tile,
-        ((row & 1)[None], part, got, link_block, inverse_one, inverse_two),
+        ((row & 1)[None], part, after(got, column_two), link_block, inverse_one, inverse_two),
         1,
     )
     return (column_one[None], column_two[None], diag_one, cross_block, diag_two)

time: 77.6 us -> 80.7 us (1.040)
  starting transfers between devices: 27.8 us -> 30.9 us
    ppermute x9, waiting for transfers between devices: 20.6 us -> 24.6 us  [swap(): lax.ppermute(array, BOTH, [(at(r, c), at(r, c ^ 1 << bit)) for r, c in ev...]
    ppermute x4, waiting for transfers between devices: 5.41 us -> 2.12 us  [swap_rows(): lax.ppermute(array, BOTH, [(at(r, c), at(r ^ 1 << bit, c)) for r, c in ev...]
    ppermute x9, starting transfers between devices: 15.3 us -> 17.4 us  [swap(): lax.ppermute(array, BOTH, [(at(r, c), at(r, c ^ 1 << bit)) for r, c in ev...]
    ppermute x4, starting transfers between devices: 3.46 us -> 4.57 us  [swap_rows(): lax.ppermute(array, BOTH, [(at(r, c), at(r ^ 1 << bit, c)) for r, c in ev...]
  transfers between devices with their start and end apart: 17 -> 17, of which waited for: 9 -> 12; matrix products, arithmetic and copies ran while one was open for 15% -> 14% of each run, Pallas kernels for 0% -> 0%
where the time goes in v7:
time: 80.7 us; the launch traced here: 80.3 us
  starting transfers between devices  30.9 us (38%)
  waiting for transfers between devices  28.2 us (35%)
  matrix products  7.62 us (9%)
  local copies, waits for them, and re-layouts  6.53 us (8%)
  other arithmetic  2.39 us (3%)
  between operations  2.34 us (3%)
  Pallas kernels  2.33 us (3%)
    ppermute x9, waiting for transfers between devices, swap(): lax.ppermute(array, BOTH, [(at(r, c), at(r, c ^ 1 << bit)) for r, c in ev...  24.6 us
    ppermute x9, starting transfers between devices, swap(): lax.ppermute(array, BOTH, [(at(r, c), at(r, c ^ 1 << bit)) for r, c in ev...  17.4 us
    ppermute x2, starting transfers between devices, over_chips(): got = after(lax.ppermute(piece, BOTH, perm), *earlier)  6.23 us
    dot_general x2, matrix products, products(): jnp.einsum('ijab,jbc->iac', kept, column, preferred_element_type=F32)  4.91 us
    ppermute x4, starting transfers between devices, swap_rows(): lax.ppermute(array, BOTH, [(at(r, c), at(r ^ 1 << bit, c)) for r, c in ev...  4.57 us
    dynamic_slice x4, local copies, waits for them, and re-layouts, part_of(): return lax.dynamic_slice_in_dim(array, start, size, 0)  3.63 us
    ppermute x2, starting transfers between devices, over_cores(): lax.ppermute(have, BOTH, perm)  2.78 us
    dynamic_slice x2, local copies, waits for them, and re-layouts, shards(): m[row * rows + col].astype(F32)  2.48 us
  transfers between devices with their start and end apart: 17, of which 12 were waited for; matrix products, arithmetic and copies ran while one was open for 14% of the time, Pallas kernels for 0%

profile of v7, /device:TPU:0, one launch (start us, length us, event | category | flops | bytes accessed | tf_op | source)
XLA Modules:
  0.0 80.3 jit_solution(10739246433999455217)
XLA Ops:
  0.6 1.1 %constant_dynamic-slice_fusion.3 = bf16[4,256,256]{2,1,0:T(8,128)(2,1)S(1)} fusion(bf16[8,256,256]{2,1,0:T(8,128)(2,1)} %param.13, s32[]{:T(128)S(6)} %select_n.145), kind=kLoop, calls=%fused_computation.68 | loop fusion | bytes 1048580 | tf_op jit(solution)/shard_map/dynamic_slice | solution.py:103
  1.7 4.9 %collective-permute-start = (bf16[4,256,256]{2,1,0:T(8,128)(2,1)S(1)}, bf16[4,256,256]{2,1,0:T(8,128)(2,1)S(1)}, u32[]{:S(2)}, u32[]{:S(2)}) collective-permute-start(bf16[4,256,256]{2,1,0:T(8,128)(2,1)S(1)} %constant_dynamic-slice_fusion.3), channel_id=1, source_target_pairs={{0,16},{1,17},{10,26},{11,27},{20,4},{21,5},{30,14},{31,15}} | collective-permute-start | bytes 1572872 | tf_op jit(solution)/shard_map/ppermute | solution.py:70
  6.6 1.1 %constant_dynamic-slice_fusion.1 = bf16[4,256,256]{2,1,0:T(8,128)(2,1)S(1)} fusion(bf16[8,256,256]{2,1,0:T(8,128)(2,1)} %param.14, s32[]{:T(128)S(6)} %select_n.145), kind=kLoop, calls=%fused_computation.66 | loop fusion | bytes 1048580 | tf_op jit(solution)/shard_map/dynamic_slice | solution.py:103
  7.7 1.3 %collective-permute-start.5 = (bf16[4,256,256]{2,1,0:T(8,128)(2,1)S(1)}, bf16[4,256,256]{2,1,0:T(8,128)(2,1)S(1)}, u32[]{:S(2)}, u32[]{:S(2)}) collective-permute-start(bf16[4,256,256]{2,1,0:T(8,128)(2,1)S(1)} %constant_dynamic-slice_fusion.1), channel_id=1, source_target_pairs={{0,16},{1,17},{10,26},{11,27},{20,4},{21,5},{30,14},{31,15}} | collective-permute-start | bytes 1572872 | tf_op jit(solution)/shard_map/ppermute | solution.py:70
  12.1 1.2 %collective-permute-done = bf16[4,256,256]{2,1,0:T(8,128)(2,1)S(1)} collective-permute-done((bf16[4,256,256]{2,1,0:T(8,128)(2,1)S(1)}, bf16[4,256,256]{2,1,0:T(8,128)(2,1)S(1)}, u32[]{:S(2)}, u32[]{:S(2)}) %collective-permute-start) | collective-permute-done | bytes 524320 | tf_op jit(solution)/shard_map/ppermute | solution.py:70
  13.4 1.3 %collective-permute-start.1 = (bf16[4,256,256]{2,1,0:T(8,128)(2,1)S(1)}, bf16[4,256,256]{2,1,0:T(8,128)(2,1)S(1)}, u32[]{:S(2)}, u32[]{:S(2)}) collective-permute-start(bf16[4,256,256]{2,1,0:T(8,128)(2,1)S(1)} %broadcast_select_fusion.2), channel_id=1, source_target_pairs={{0,8},{1,9},{10,2},{11,3},{4,12},{5,13},{14,6},{15,7},{16,24},{17,... | collective-permute-start | bytes 1572872 | tf_op jit(solution)/shard_map/ppermute | solution.py:80
  14.7 1.2 %dynamic_slice.101 = s32[1]{0:T(128)} dynamic-slice(s32[32]{0:T(128)} %param.12, s32[]{:T(128)S(6)} %select_n.136), dynamic_slice_sizes={1} | dynamic-slice | bytes 12 | tf_op jit(solution)/shard_map/dynamic_slice | solution.py:150
  16.0 1.2 %dynamic_slice.80 = s32[1]{0:T(128)} dynamic-slice(s32[32]{0:T(128)} %param.11, s32[]{:T(128)S(6)} %select_n.136), dynamic_slice_sizes={1} | dynamic-slice | bytes 12 | tf_op jit(solution)/shard_map/dynamic_slice | solution.py:150
  19.0 3.6 %bitcast_convert_fusion.1 = bf16[8,256,256]{2,1,0:T(8,128)(2,1)S(1)} fusion(bf16[8,4,256,256]{3,2,1,0:T(8,128)(2,1)} %param.9, pred[8,4]{1,0:T(8,128)(4,1)S(1)} %copy.19, bf16[4,256,256]{2,1,0:T(8,128)(2,1)S(1)} %broadcast_select_fusion.2, bf16[4,256,256]{2,1,0:T(8,128)(2,1)S(1)} %collective-permute-done.1, pred[]{:T(512)S(6)} %eq.18), kind=kOutput, calls=%fused_computation.7 | convolution fusion | flops 1076625408 | bytes 6291489 | tf_op jit(solution)/shard_map/ijab,jbc->iac/dot_general | solution.py:110
  22.6 1.5 %collective-permute-start.6 = (bf16[4,256,256]{2,1,0:T(8,128)(2,1)S(1)}, bf16[4,256,256]{2,1,0:T(8,128)(2,1)S(1)}, u32[]{:S(2)}, u32[]{:S(2)}) collective-permute-start(bf16[4,256,256]{2,1,0:T(8,128)(2,1)S(1)} %broadcast_select_fusion.1), channel_id=1, source_target_pairs={{0,8},{1,9},{10,2},{11,3},{4,12},{5,13},{14,6},{15,7},{16,24},{17,... | collective-permute-start | bytes 1572872 | tf_op jit(solution)/shard_map/ppermute | solution.py:80
  24.1 1.6 %collective-permute-start.2 = (bf16[4,256,256]{2,1,0:T(8,128)(2,1)S(1)}, bf16[4,256,256]{2,1,0:T(8,128)(2,1)S(1)}, u32[]{:S(2)}, u32[]{:S(2)}) collective-permute-start(bf16[4,256,256]{2,1,0:T(8,128)(2,1)S(1)} %get-tuple-element.41), channel_id=1, source_target_pairs={{0,1},{1,0},{2,3},{3,2},{4,5},{5,4},{6,7},{7,6},{8,9},{9,8},{10,11... | collective-permute-start | bytes 1572872 | tf_op jit(solution)/shard_map/ppermute | solution.py:83
  26.9 1.3 %bitcast_convert_fusion = bf16[8,256,256]{2,1,0:T(8,128)(2,1)S(1)} fusion(bf16[8,4,256,256]{3,2,1,0:T(8,128)(2,1)S(1)} %copy-done.6, pred[8,4]{1,0:T(8,128)(4,1)S(1)} %copy.23, bf16[4,256,256]{2,1,0:T(8,128)(2,1)S(1)} %broadcast_select_fusion.1, bf16[4,256,256]{2,1,0:T(8,128)(2,1)S(1)} %collective-permute-done.6, pred[]{:T(512)S(6)} %eq.18), kind=kOutput, calls=%fused_computation.6 | convolution fusion | flops 1076625408 | bytes 6291489 | tf_op jit(solution)/shard_map/ijab,jbc->iac/dot_general | solution.py:110
  29.2 1.3 %collective-permute-done.7 = bf16[384,256]{1,0:T(8,128)(2,1)S(1)} collective-permute-done((bf16[384,256]{1,0:T(8,128)(2,1)S(1)}, bf16[384,256]{1,0:T(8,128)(2,1)S(1)}, u32[]{:S(2)}, u32[]{:S(2)}) %collective-permute-start.7) | collective-permute-done | bytes 196640 | tf_op jit(solution)/shard_map/ppermute | solution.py:86
  30.6 2.5 %collective-permute-start.8 = (bf16[192,256]{1,0:T(8,128)(2,1)S(1)}, bf16[192,256]{1,0:T(8,128)(2,1)S(1)}, u32[]{:S(2)}, u32[]{:S(2)}) collective-permute-start(bf16[192,256]{1,0:T(8,128)(2,1)S(1)} %dynamic-slice_convert_fusion.1), channel_id=1, source_target_pairs={{0,16},{1,17},{2,18},{3,19},{4,20},{5,21},{6,22},{7,23},{8,24},{9,... | collective-permute-start | bytes 294920 | tf_op jit(solution)/shard_map/ppermute | solution.py:86
  33.2 2.2 %collective-permute-done.2 = bf16[4,256,256]{2,1,0:T(8,128)(2,1)S(1)} collective-permute-done((bf16[4,256,256]{2,1,0:T(8,128)(2,1)S(1)}, bf16[4,256,256]{2,1,0:T(8,128)(2,1)S(1)}, u32[]{:S(2)}, u32[]{:S(2)}) %collective-permute-start.2) | collective-permute-done | bytes 524320 | tf_op jit(solution)/shard_map/ppermute | solution.py:83
  35.5 1.8 %collective-permute-start.10 = (bf16[4,256,256]{2,1,0:T(8,128)(2,1)S(1)}, bf16[4,256,256]{2,1,0:T(8,128)(2,1)S(1)}, u32[]{:S(2)}, u32[]{:S(2)}) collective-permute-start(bf16[4,256,256]{2,1,0:T(8,128)(2,1)S(1)} %get-tuple-element.20), channel_id=1, source_target_pairs={{0,1},{1,0},{2,3},{3,2},{4,5},{5,4},{6,7},{7,6},{8,9},{9,8},{10,11... | collective-permute-start | bytes 1572872 | tf_op jit(solution)/shard_map/ppermute | solution.py:83
  37.3 4.1 %collective-permute-start.9 = (bf16[192,256]{1,0:T(8,128)(2,1)S(1)}, bf16[192,256]{1,0:T(8,128)(2,1)S(1)}, u32[]{:S(2)}, u32[]{:S(2)}) collective-permute-start(bf16[192,256]{1,0:T(8,128)(2,1)S(1)} %add_convert_fusion.4), channel_id=1, source_target_pairs={{0,4},{1,5},{2,6},{3,7},{4,0},{5,1},{6,2},{7,3},{8,12},{9,13},{10,... | collective-permute-start | bytes 294920 | tf_op jit(solution)/shard_map/ppermute | solution.py:83
  41.7 3.0 %collective-permute-done.9 = bf16[192,256]{1,0:T(8,128)(2,1)S(1)} collective-permute-done((bf16[192,256]{1,0:T(8,128)(2,1)S(1)}, bf16[192,256]{1,0:T(8,128)(2,1)S(1)}, u32[]{:S(2)}, u32[]{:S(2)}) %collective-permute-start.9) | collective-permute-done | bytes 98336 | tf_op jit(solution)/shard_map/ppermute | solution.py:83
  44.7 2.3 %collective-permute-done.10 = bf16[4,256,256]{2,1,0:T(8,128)(2,1)S(1)} collective-permute-done((bf16[4,256,256]{2,1,0:T(8,128)(2,1)S(1)}, bf16[4,256,256]{2,1,0:T(8,128)(2,1)S(1)}, u32[]{:S(2)}, u32[]{:S(2)}) %collective-permute-start.10) | collective-permute-done | bytes 524320 | tf_op jit(solution)/shard_map/ppermute | solution.py:83
  47.0 1.1 %collective-permute-start.11 = (bf16[192,256]{1,0:T(8,128)(2,1)S(1)}, bf16[192,256]{1,0:T(8,128)(2,1)S(1)}, u32[]{:S(2)}, u32[]{:S(2)}) collective-permute-start(bf16[192,256]{1,0:T(8,128)(2,1)S(1)} %add_convert_fusion.3), channel_id=1, source_target_pairs={{0,2},{1,3},{2,0},{3,1},{4,6},{5,7},{6,4},{7,5},{8,10},{9,11},{10,... | collective-permute-start | bytes 294920 | tf_op jit(solution)/shard_map/ppermute | solution.py:83
  48.2 4.0 %collective-permute-done.11 = bf16[192,256]{1,0:T(8,128)(2,1)S(1)} collective-permute-done((bf16[192,256]{1,0:T(8,128)(2,1)S(1)}, bf16[192,256]{1,0:T(8,128)(2,1)S(1)}, u32[]{:S(2)}, u32[]{:S(2)}) %collective-permute-start.11) | collective-permute-done | bytes 98336 | tf_op jit(solution)/shard_map/ppermute | solution.py:83
  52.2 1.5 %collective-permute-start.12 = (bf16[192,256]{1,0:T(8,128)(2,1)S(1)}, bf16[192,256]{1,0:T(8,128)(2,1)S(1)}, u32[]{:S(2)}, u32[]{:S(2)}) collective-permute-start(bf16[192,256]{1,0:T(8,128)(2,1)S(1)} %add_convert_fusion.2), channel_id=1, source_target_pairs={{0,1},{1,0},{2,3},{3,2},{4,5},{5,4},{6,7},{7,6},{8,9},{9,8},{10,11... | collective-permute-start | bytes 294920 | tf_op jit(solution)/shard_map/ppermute | solution.py:83
  53.8 3.0 %collective-permute-start.4 = (bf16[1,256,256]{2,1,0:T(8,128)(2,1)S(1)}, bf16[1,256,256]{2,1,0:T(8,128)(2,1)S(1)}, u32[]{:S(2)}, u32[]{:S(2)}) collective-permute-start(bf16[1,256,256]{2,1,0:T(8,128)(2,1)S(1)} %fusion.30), channel_id=1, source_target_pairs={{0,4},{1,5},{2,6},{3,7},{4,0},{5,1},{6,2},{7,3},{8,12},{9,13},{10,... | collective-permute-start | bytes 393224 | tf_op jit(solution)/shard_map/ppermute | solution.py:83
  56.9 2.0 %collective-permute-start.13 = (bf16[192,256]{1,0:T(8,128)(2,1)S(1)}, bf16[192,256]{1,0:T(8,128)(2,1)S(1)}, u32[]{:S(2)}, u32[]{:S(2)}) collective-permute-start(bf16[192,256]{1,0:T(8,128)(2,1)S(1)} %add_convert_fusion.1), channel_id=1, source_target_pairs={{0,16},{1,17},{2,18},{3,19},{4,20},{5,21},{6,22},{7,23},{8,24},{9,... | collective-permute-start | bytes 294920 | tf_op jit(solution)/shard_map/ppermute | solution.py:86
  59.0 1.9 %collective-permute-start.14 = (bf16[2,256,256]{2,1,0:T(8,128)(2,1)S(1)}, bf16[2,256,256]{2,1,0:T(8,128)(2,1)S(1)}, u32[]{:S(2)}, u32[]{:S(2)}) collective-permute-start(bf16[2,256,256]{2,1,0:T(8,128)(2,1)S(1)} %fusion.26), channel_id=1, source_target_pairs={{0,2},{1,3},{2,0},{3,1},{4,6},{5,7},{6,4},{7,5},{8,10},{9,11},{10,... | collective-permute-start | bytes 786440 | tf_op jit(solution)/shard_map/ppermute | solution.py:83
  60.8 0.8 collective-permute-done.13
  61.7 1.0 %collective-permute-done.4 = bf16[1,256,256]{2,1,0:T(8,128)(2,1)S(1)} collective-permute-done((bf16[1,256,256]{2,1,0:T(8,128)(2,1)S(1)}, bf16[1,256,256]{2,1,0:T(8,128)(2,1)S(1)}, u32[]{:S(2)}, u32[]{:S(2)}) %collective-permute-start.4) | collective-permute-done | bytes 131104 | tf_op jit(solution)/shard_map/ppermute | solution.py:83
  62.7 4.6 %collective-permute-done.14 = bf16[2,256,256]{2,1,0:T(8,128)(2,1)S(1)} collective-permute-done((bf16[2,256,256]{2,1,0:T(8,128)(2,1)S(1)}, bf16[2,256,256]{2,1,0:T(8,128)(2,1)S(1)}, u32[]{:S(2)}, u32[]{:S(2)}) %collective-permute-start.14) | collective-permute-done | bytes 262176 | tf_op jit(solution)/shard_map/ppermute | solution.py:83
  67.4 2.3 %collective-permute-start.16 = (bf16[1,256,256]{2,1,0:T(8,128)(2,1)S(1)}, bf16[1,256,256]{2,1,0:T(8,128)(2,1)S(1)}, u32[]{:S(2)}, u32[]{:S(2)}) collective-permute-start(bf16[1,256,256]{2,1,0:T(8,128)(2,1)S(1)} %fusion.29), channel_id=1, source_target_pairs={{0,4},{1,5},{2,6},{3,7},{4,0},{5,1},{6,2},{7,3},{8,12},{9,13},{10,... | collective-permute-start | bytes 393224 | tf_op jit(solution)/shard_map/ppermute | solution.py:83
  69.7 7.4 %collective-permute-done.16 = bf16[1,256,256]{2,1,0:T(8,128)(2,1)S(1)} collective-permute-done((bf16[1,256,256]{2,1,0:T(8,128)(2,1)S(1)}, bf16[1,256,256]{2,1,0:T(8,128)(2,1)S(1)}, u32[]{:S(2)}, u32[]{:S(2)}) %collective-permute-start.16) | collective-permute-done | bytes 131104 | tf_op jit(solution)/shard_map/ppermute | solution.py:83
  77.1 0.9 %fusion.28 = bf16[256,256]{1,0:T(8,128)(2,1)} fusion(f32[2,1,256,256]{3,2,1,0:T(8,128)S(1)} %convert_add_fusion, s32[]{:T(128)S(6)} %select_n.152, bf16[1,256,256]{2,1,0:T(8,128)(2,1)S(1)} %collective-permute-done.16, bf16[256,256]{1,0:T(8,128)(2,1)S(1)} %copy-done.2, bf16[1,256,256]{2,1,0:T(8,128)(2,1)S(1)} %fusion.33, ...), kind=kOutput, calls=%fused_computation.44 | convolution fusion | flops 34013184 | bytes 917512 | tf_op jit(solution)/shard_map/dot_general | solution.py:152
  78.0 2.3 %shard_map.128 = (bf16[256,256]{1,0:T(8,128)(2,1)}, bf16[256,256]{1,0:T(8,128)(2,1)}, bf16[256,256]{1,0:T(8,128)(2,1)}) custom-call(s32[1]{0:T(128)} %bitcast.35.place, bf16[384,256]{1,0:T(8,128)(2,1)} %copy-done, bf16[384,256]{1,0:T(8,128)(2,1)} %copy-done.5, bf16[256,256]{1,0:T(8,128)(2,1)} %link.1, f32[256,256]{1,0:T(8,128)} %inverse_one.1, ...), custom_call_target="tpu_custom_call" | custom-call | flops 100663296 | bytes 1572864 | tf_op jit(solution)/shard_map/pallas_call | solution.py:29
  (55 shorter events, 6.6 us)
Async XLA Ops:
  1.7 11.6 %collective-permute-start = (bf16[4,256,256]{2,1,0:T(8,128)(2,1)S(1)}, bf16[4,256,256]{2,1,0:T(8,128)(2,1)S(1)}, u32[]{:S(2)}, u32[]{:S(2)}) collective-permute-start(bf16[4,256,256]{2,1,0:T(8,128)(2,1)S(1)} %constant_dynamic-slice_fusion.3), channel_id=1, source_target_pairs={{0,16},{1,17},{10,26},{11,27},{20,4},{21,5},{30,14},{31,15}} | collective-permute-start | bytes 1572872 | tf_op jit(solution)/shard_map/ppermute | solution.py:70
  7.7 11.2 %collective-permute-start.5 = (bf16[4,256,256]{2,1,0:T(8,128)(2,1)S(1)}, bf16[4,256,256]{2,1,0:T(8,128)(2,1)S(1)}, u32[]{:S(2)}, u32[]{:S(2)}) collective-permute-start(bf16[4,256,256]{2,1,0:T(8,128)(2,1)S(1)} %constant_dynamic-slice_fusion.1), channel_id=1, source_target_pairs={{0,16},{1,17},{10,26},{11,27},{20,4},{21,5},{30,14},{31,15}} | collective-permute-start | bytes 1572872 | tf_op jit(solution)/shard_map/ppermute | solution.py:70
  13.4 5.6 %collective-permute-start.1 = (bf16[4,256,256]{2,1,0:T(8,128)(2,1)S(1)}, bf16[4,256,256]{2,1,0:T(8,128)(2,1)S(1)}, u32[]{:S(2)}, u32[]{:S(2)}) collective-permute-start(bf16[4,256,256]{2,1,0:T(8,128)(2,1)S(1)} %broadcast_select_fusion.2), channel_id=1, source_target_pairs={{0,8},{1,9},{10,2},{11,3},{4,12},{5,13},{14,6},{15,7},{16,24},{17,... | collective-permute-start | bytes 1572872 | tf_op jit(solution)/shard_map/ppermute | solution.py:80
  19.0 6.7 %copy-start.3 = (bf16[8,256,256]{2,1,0:T(8,128)(2,1)S(1)}, bf16[8,256,256]{2,1,0:T(8,128)(2,1)}, u32[]{:S(2)}) copy-start(bf16[8,256,256]{2,1,0:T(8,128)(2,1)} %param.13) | copy-start | bytes 3145732
  22.6 3.8 %copy-start.4 = (bf16[8,256,256]{2,1,0:T(8,128)(2,1)S(1)}, bf16[8,256,256]{2,1,0:T(8,128)(2,1)}, u32[]{:S(2)}) copy-start(bf16[8,256,256]{2,1,0:T(8,128)(2,1)} %param.14) | copy-start | bytes 3145732
  22.6 4.3 %collective-permute-start.6 = (bf16[4,256,256]{2,1,0:T(8,128)(2,1)S(1)}, bf16[4,256,256]{2,1,0:T(8,128)(2,1)S(1)}, u32[]{:S(2)}, u32[]{:S(2)}) collective-permute-start(bf16[4,256,256]{2,1,0:T(8,128)(2,1)S(1)} %broadcast_select_fusion.1), channel_id=1, source_target_pairs={{0,8},{1,9},{10,2},{11,3},{4,12},{5,13},{14,6},{15,7},{16,24},{17,... | collective-permute-start | bytes 1572872 | tf_op jit(solution)/shard_map/ppermute | solution.py:80
  24.0 2.9 %copy-start.6 = (bf16[8,4,256,256]{3,2,1,0:T(8,128)(2,1)S(1)}, bf16[8,4,256,256]{3,2,1,0:T(8,128)(2,1)}, u32[]{:S(2)}) copy-start(bf16[8,4,256,256]{3,2,1,0:T(8,128)(2,1)} %param.9) | copy-start | bytes 12582916
  24.1 11.3 %collective-permute-start.2 = (bf16[4,256,256]{2,1,0:T(8,128)(2,1)S(1)}, bf16[4,256,256]{2,1,0:T(8,128)(2,1)S(1)}, u32[]{:S(2)}, u32[]{:S(2)}) collective-permute-start(bf16[4,256,256]{2,1,0:T(8,128)(2,1)S(1)} %get-tuple-element.41), channel_id=1, source_target_pairs={{0,1},{1,0},{2,3},{3,2},{4,5},{5,4},{6,7},{7,6},{8,9},{9,8},{10,11... | collective-permute-start | bytes 1572872 | tf_op jit(solution)/shard_map/ppermute | solution.py:83
  29.1 1.5 %collective-permute-start.7 = (bf16[384,256]{1,0:T(8,128)(2,1)S(1)}, bf16[384,256]{1,0:T(8,128)(2,1)S(1)}, u32[]{:S(2)}, u32[]{:S(2)}) collective-permute-start(bf16[384,256]{1,0:T(8,128)(2,1)S(1)} %dynamic-slice_convert_fusion), channel_id=1, source_target_pairs={{0,8},{1,9},{2,10},{3,11},{4,12},{5,13},{6,14},{7,15},{8,0},{9,1},... | collective-permute-start | bytes 589832 | tf_op jit(solution)/shard_map/ppermute | solution.py:86
  30.6 6.7 %collective-permute-start.8 = (bf16[192,256]{1,0:T(8,128)(2,1)S(1)}, bf16[192,256]{1,0:T(8,128)(2,1)S(1)}, u32[]{:S(2)}, u32[]{:S(2)}) collective-permute-start(bf16[192,256]{1,0:T(8,128)(2,1)S(1)} %dynamic-slice_convert_fusion.1), channel_id=1, source_target_pairs={{0,16},{1,17},{2,18},{3,19},{4,20},{5,21},{6,22},{7,23},{8,24},{9,... | collective-permute-start | bytes 294920 | tf_op jit(solution)/shard_map/ppermute | solution.py:86
  35.5 11.5 %collective-permute-start.10 = (bf16[4,256,256]{2,1,0:T(8,128)(2,1)S(1)}, bf16[4,256,256]{2,1,0:T(8,128)(2,1)S(1)}, u32[]{:S(2)}, u32[]{:S(2)}) collective-permute-start(bf16[4,256,256]{2,1,0:T(8,128)(2,1)S(1)} %get-tuple-element.20), channel_id=1, source_target_pairs={{0,1},{1,0},{2,3},{3,2},{4,5},{5,4},{6,7},{7,6},{8,9},{9,8},{10,11... | collective-permute-start | bytes 1572872 | tf_op jit(solution)/shard_map/ppermute | solution.py:83
  37.3 7.4 %collective-permute-start.9 = (bf16[192,256]{1,0:T(8,128)(2,1)S(1)}, bf16[192,256]{1,0:T(8,128)(2,1)S(1)}, u32[]{:S(2)}, u32[]{:S(2)}) collective-permute-start(bf16[192,256]{1,0:T(8,128)(2,1)S(1)} %add_convert_fusion.4), channel_id=1, source_target_pairs={{0,4},{1,5},{2,6},{3,7},{4,0},{5,1},{6,2},{7,3},{8,12},{9,13},{10,... | collective-permute-start | bytes 294920 | tf_op jit(solution)/shard_map/ppermute | solution.py:83
  41.6 35.5 %copy-start.2 = (bf16[256,256]{1,0:T(8,128)(2,1)S(1)}, bf16[256,256]{1,0:T(8,128)(2,1)}, u32[]{:S(2)}) copy-start(bf16[256,256]{1,0:T(8,128)(2,1)} %link.1) | copy-start | bytes 393220
  41.6 10.6 %collective-permute-start.3 = (bf16[2,256,256]{2,1,0:T(8,128)(2,1)S(1)}, bf16[2,256,256]{2,1,0:T(8,128)(2,1)S(1)}, u32[]{:S(2)}, u32[]{:S(2)}) collective-permute-start(bf16[2,256,256]{2,1,0:T(8,128)(2,1)S(1)} %get-tuple-element.37), channel_id=1, source_target_pairs={{0,2},{1,3},{2,0},{3,1},{4,6},{5,7},{6,4},{7,5},{8,10},{9,11},{10,... | collective-permute-start | bytes 786440 | tf_op jit(solution)/shard_map/ppermute | solution.py:83
  47.0 5.2 %collective-permute-start.11 = (bf16[192,256]{1,0:T(8,128)(2,1)S(1)}, bf16[192,256]{1,0:T(8,128)(2,1)S(1)}, u32[]{:S(2)}, u32[]{:S(2)}) collective-permute-start(bf16[192,256]{1,0:T(8,128)(2,1)S(1)} %add_convert_fusion.3), channel_id=1, source_target_pairs={{0,2},{1,3},{2,0},{3,1},{4,6},{5,7},{6,4},{7,5},{8,10},{9,11},{10,... | collective-permute-start | bytes 294920 | tf_op jit(solution)/shard_map/ppermute | solution.py:83
  52.2 4.7 %collective-permute-start.12 = (bf16[192,256]{1,0:T(8,128)(2,1)S(1)}, bf16[192,256]{1,0:T(8,128)(2,1)S(1)}, u32[]{:S(2)}, u32[]{:S(2)}) collective-permute-start(bf16[192,256]{1,0:T(8,128)(2,1)S(1)} %add_convert_fusion.2), channel_id=1, source_target_pairs={{0,1},{1,0},{2,3},{3,2},{4,5},{5,4},{6,7},{7,6},{8,9},{9,8},{10,11... | collective-permute-start | bytes 294920 | tf_op jit(solution)/shard_map/ppermute | solution.py:83
  53.8 8.9 %collective-permute-start.4 = (bf16[1,256,256]{2,1,0:T(8,128)(2,1)S(1)}, bf16[1,256,256]{2,1,0:T(8,128)(2,1)S(1)}, u32[]{:S(2)}, u32[]{:S(2)}) collective-permute-start(bf16[1,256,256]{2,1,0:T(8,128)(2,1)S(1)} %fusion.30), channel_id=1, source_target_pairs={{0,4},{1,5},{2,6},{3,7},{4,0},{5,1},{6,2},{7,3},{8,12},{9,13},{10,... | collective-permute-start | bytes 393224 | tf_op jit(solution)/shard_map/ppermute | solution.py:83
  56.9 4.7 %collective-permute-start.13 = (bf16[192,256]{1,0:T(8,128)(2,1)S(1)}, bf16[192,256]{1,0:T(8,128)(2,1)S(1)}, u32[]{:S(2)}, u32[]{:S(2)}) collective-permute-start(bf16[192,256]{1,0:T(8,128)(2,1)S(1)} %add_convert_fusion.1), channel_id=1, source_target_pairs={{0,16},{1,17},{2,18},{3,19},{4,20},{5,21},{6,22},{7,23},{8,24},{9,... | collective-permute-start | bytes 294920 | tf_op jit(solution)/shard_map/ppermute | solution.py:86
  59.0 8.3 %collective-permute-start.14 = (bf16[2,256,256]{2,1,0:T(8,128)(2,1)S(1)}, bf16[2,256,256]{2,1,0:T(8,128)(2,1)S(1)}, u32[]{:S(2)}, u32[]{:S(2)}) collective-permute-start(bf16[2,256,256]{2,1,0:T(8,128)(2,1)S(1)} %fusion.26), channel_id=1, source_target_pairs={{0,2},{1,3},{2,0},{3,1},{4,6},{5,7},{6,4},{7,5},{8,10},{9,11},{10,... | collective-permute-start | bytes 786440 | tf_op jit(solution)/shard_map/ppermute | solution.py:83
  61.7 16.3 %copy-start = (bf16[384,256]{1,0:T(8,128)(2,1)}, bf16[384,256]{1,0:T(8,128)(2,1)S(1)}, u32[]{:S(2)}) copy-start(bf16[384,256]{1,0:T(8,128)(2,1)S(1)} %pad_maximum_fusion.1.mine) | copy-start | bytes 589828
  67.3 2.4 %collective-permute-start.15 = (bf16[384,256]{1,0:T(8,128)(2,1)S(1)}, bf16[384,256]{1,0:T(8,128)(2,1)S(1)}, u32[]{:S(2)}, u32[]{:S(2)}) collective-permute-start(bf16[384,256]{1,0:T(8,128)(2,1)S(1)} %pad_maximum_fusion.1.mine), channel_id=1, source_target_pairs={{0,8},{1,9},{2,10},{3,11},{4,12},{5,13},{6,14},{7,15},{8,0},{9,1},... | collective-permute-start | bytes 589832 | tf_op jit(solution)/shard_map/ppermute | solution.py:86
  67.4 9.7 %collective-permute-start.16 = (bf16[1,256,256]{2,1,0:T(8,128)(2,1)S(1)}, bf16[1,256,256]{2,1,0:T(8,128)(2,1)S(1)}, u32[]{:S(2)}, u32[]{:S(2)}) collective-permute-start(bf16[1,256,256]{2,1,0:T(8,128)(2,1)S(1)} %fusion.29), channel_id=1, source_target_pairs={{0,4},{1,5},{2,6},{3,7},{4,0},{5,1},{6,2},{7,3},{8,12},{9,13},{10,... | collective-permute-start | bytes 393224 | tf_op jit(solution)/shard_map/ppermute | solution.py:83
  69.7 8.3 %copy-start.5 = (bf16[384,256]{1,0:T(8,128)(2,1)}, bf16[384,256]{1,0:T(8,128)(2,1)S(1)}, u32[]{:S(2)}) copy-start(bf16[384,256]{1,0:T(8,128)(2,1)S(1)} %collective-permute-done.15.other) | copy-start | bytes 589828
  69.7 10.6 %copy-start.1 = (bf16[1,256,256]{2,1,0:T(8,128)(2,1)}, bf16[1,256,256]{2,1,0:T(8,128)(2,1)S(1)}, u32[]{:S(2)}) copy-start(bf16[1,256,256]{2,1,0:T(8,128)(2,1)S(1)} %fusion.33) | copy-start | bytes 393220

commit v8 on v7

--- a/solution.py
+++ b/solution.py
@@ -142,13 +142,13 @@
         got = swap(after(part, gate), bit)
         part = (part.astype(F32) + got.astype(F32)).astype(BF16)
     for bit in reversed(range(row_bits)):
-        got = swap_rows(after(part, *((two[-2], one[-1]) if bit == 0 else ())), bit)
+        got = swap_rows(after(part, one[-1] if bit == 0 else two[-2]), bit)
         if bit:
             low = (row >> bit & 1) == 0
             part = jnp.concatenate([jnp.where(low, part, got), jnp.where(low, got, part)])
 
     member_one, member_two = (m[row * rows + col].astype(F32) for m in (member_one, member_two))
-    column_one = (-member_one * (keep_one[0] + after(one[-1], got)[0].astype(F32))).astype(BF16)
+    column_one = (-member_one * (keep_one[0] + after(one[-1], part)[0].astype(F32))).astype(BF16)
     linked = jnp.dot(column_one, link_block, preferred_element_type=F32) + keep_two[0]
     column_two = (-member_two * (linked + two[-1][0].astype(F32))).astype(BF16)
     diag_one, cross_block, diag_two = small_kernel(

time: 80.7 us -> 76.4 us (0.947)
  starting transfers between devices: 30.9 us -> 27.6 us
  waiting for transfers between devices: 28.2 us -> 26.5 us
    ppermute x9, starting transfers between devices: 17.4 us -> 14 us  [swap(): lax.ppermute(array, BOTH, [(at(r, c), at(r, c ^ 1 << bit)) for r, c in ev...]
    ppermute x9, waiting for transfers between devices: 24.6 us -> 22.1 us  [swap(): lax.ppermute(array, BOTH, [(at(r, c), at(r, c ^ 1 << bit)) for r, c in ev...]
    ppermute x4, waiting for transfers between devices: 2.12 us -> 2.98 us  [swap_rows(): lax.ppermute(array, BOTH, [(at(r, c), at(r ^ 1 << bit, c)) for r, c in ev...]
  transfers between devices with their start and end apart: 17 -> 17, of which waited for: 12 -> 10; matrix products, arithmetic and copies ran while one was open for 14% -> 15% of each run, Pallas kernels for 0% -> 0%
where the time goes in v8:
time: 76.4 us; the launch traced here: 76 us
  starting transfers between devices  27.6 us (36%)
  waiting for transfers between devices  26.5 us (35%)
  matrix products  7.62 us (10%)
  local copies, waits for them, and re-layouts  7.21 us (9%)
  between operations  2.39 us (3%)
  other arithmetic  2.38 us (3%)
  Pallas kernels  2.32 us (3%)
    ppermute x9, waiting for transfers between devices, swap(): lax.ppermute(array, BOTH, [(at(r, c), at(r, c ^ 1 << bit)) for r, c in ev...  22.1 us
    ppermute x9, starting transfers between devices, swap(): lax.ppermute(array, BOTH, [(at(r, c), at(r, c ^ 1 << bit)) for r, c in ev...  14 us
    ppermute x2, starting transfers between devices, over_chips(): got = after(lax.ppermute(piece, BOTH, perm), *earlier)  6.23 us
    dot_general x2, matrix products, products(): jnp.einsum('ijab,jbc->iac', kept, column, preferred_element_type=F32)  4.91 us
    ppermute x4, starting transfers between devices, swap_rows(): lax.ppermute(array, BOTH, [(at(r, c), at(r ^ 1 << bit, c)) for r, c in ev...  4.43 us
    dynamic_slice x4, local copies, waits for them, and re-layouts, part_of(): return lax.dynamic_slice_in_dim(array, start, size, 0)  3.63 us
    ppermute x4, waiting for transfers between devices, swap_rows(): lax.ppermute(array, BOTH, [(at(r, c), at(r ^ 1 << bit, c)) for r, c in ev...  2.98 us
    ppermute x2, starting transfers between devices, over_cores(): lax.ppermute(have, BOTH, perm)  2.91 us
  transfers between devices with their start and end apart: 17, of which 10 were waited for; matrix products, arithmetic and copies ran while one was open for 15% of the time, Pallas kernels for 0%

profile of v8, /device:TPU:0, one launch (start us, length us, event | category | flops | bytes accessed | tf_op | source)
XLA Modules:
  0.0 76.0 jit_solution(5745201583493866641)
XLA Ops:
  0.6 1.1 %constant_dynamic-slice_fusion.3 = bf16[4,256,256]{2,1,0:T(8,128)(2,1)S(1)} fusion(bf16[8,256,256]{2,1,0:T(8,128)(2,1)} %param.13, s32[]{:T(128)S(6)} %select_n.145), kind=kLoop, calls=%fused_computation.68 | loop fusion | bytes 1048580 | tf_op jit(solution)/shard_map/dynamic_slice | solution.py:103
  1.7 4.9 %collective-permute-start = (bf16[4,256,256]{2,1,0:T(8,128)(2,1)S(1)}, bf16[4,256,256]{2,1,0:T(8,128)(2,1)S(1)}, u32[]{:S(2)}, u32[]{:S(2)}) collective-permute-start(bf16[4,256,256]{2,1,0:T(8,128)(2,1)S(1)} %constant_dynamic-slice_fusion.3), channel_id=1, source_target_pairs={{0,16},{1,17},{10,26},{11,27},{20,4},{21,5},{30,14},{31,15}} | collective-permute-start | bytes 1572872 | tf_op jit(solution)/shard_map/ppermute | solution.py:70
  6.6 1.1 %constant_dynamic-slice_fusion.1 = bf16[4,256,256]{2,1,0:T(8,128)(2,1)S(1)} fusion(bf16[8,256,256]{2,1,0:T(8,128)(2,1)} %param.14, s32[]{:T(128)S(6)} %select_n.145), kind=kLoop, calls=%fused_computation.66 | loop fusion | bytes 1048580 | tf_op jit(solution)/shard_map/dynamic_slice | solution.py:103
  7.7 1.3 %collective-permute-start.5 = (bf16[4,256,256]{2,1,0:T(8,128)(2,1)S(1)}, bf16[4,256,256]{2,1,0:T(8,128)(2,1)S(1)}, u32[]{:S(2)}, u32[]{:S(2)}) collective-permute-start(bf16[4,256,256]{2,1,0:T(8,128)(2,1)S(1)} %constant_dynamic-slice_fusion.1), channel_id=1, source_target_pairs={{0,16},{1,17},{10,26},{11,27},{20,4},{21,5},{30,14},{31,15}} | collective-permute-start | bytes 1572872 | tf_op jit(solution)/shard_map/ppermute | solution.py:70
  9.1 0.7 dynamic_slice.81
  10.6 0.7 broadcast_compare_fusion.2
  11.3 0.8 broadcast_compare_fusion
  12.1 1.2 %collective-permute-done = bf16[4,256,256]{2,1,0:T(8,128)(2,1)S(1)} collective-permute-done((bf16[4,256,256]{2,1,0:T(8,128)(2,1)S(1)}, bf16[4,256,256]{2,1,0:T(8,128)(2,1)S(1)}, u32[]{:S(2)}, u32[]{:S(2)}) %collective-permute-start) | collective-permute-done | bytes 524320 | tf_op jit(solution)/shard_map/ppermute | solution.py:70
  13.4 1.3 %collective-permute-start.1 = (bf16[4,256,256]{2,1,0:T(8,128)(2,1)S(1)}, bf16[4,256,256]{2,1,0:T(8,128)(2,1)S(1)}, u32[]{:S(2)}, u32[]{:S(2)}) collective-permute-start(bf16[4,256,256]{2,1,0:T(8,128)(2,1)S(1)} %broadcast_select_fusion.2), channel_id=1, source_target_pairs={{0,8},{1,9},{10,2},{11,3},{4,12},{5,13},{14,6},{15,7},{16,24},{17,... | collective-permute-start | bytes 1572872 | tf_op jit(solution)/shard_map/ppermute | solution.py:80
  14.7 1.2 %dynamic_slice.101 = s32[1]{0:T(128)} dynamic-slice(s32[32]{0:T(128)} %param.12, s32[]{:T(128)S(6)} %select_n.136), dynamic_slice_sizes={1} | dynamic-slice | bytes 12 | tf_op jit(solution)/shard_map/dynamic_slice | solution.py:150
  16.0 1.2 %dynamic_slice.80 = s32[1]{0:T(128)} dynamic-slice(s32[32]{0:T(128)} %param.11, s32[]{:T(128)S(6)} %select_n.136), dynamic_slice_sizes={1} | dynamic-slice | bytes 12 | tf_op jit(solution)/shard_map/dynamic_slice | solution.py:150
  19.0 3.6 %bitcast_convert_fusion.1 = bf16[8,256,256]{2,1,0:T(8,128)(2,1)S(1)} fusion(bf16[8,4,256,256]{3,2,1,0:T(8,128)(2,1)} %param.9, pred[8,4]{1,0:T(8,128)(4,1)S(1)} %copy.19, bf16[4,256,256]{2,1,0:T(8,128)(2,1)S(1)} %broadcast_select_fusion.2, bf16[4,256,256]{2,1,0:T(8,128)(2,1)S(1)} %collective-permute-done.1, pred[]{:T(512)S(6)} %eq.18), kind=kOutput, calls=%fused_computation.7 | convolution fusion | flops 1076625408 | bytes 6291489 | tf_op jit(solution)/shard_map/ijab,jbc->iac/dot_general | solution.py:110
  23.3 1.6 %collective-permute-start.6 = (bf16[4,256,256]{2,1,0:T(8,128)(2,1)S(1)}, bf16[4,256,256]{2,1,0:T(8,128)(2,1)S(1)}, u32[]{:S(2)}, u32[]{:S(2)}) collective-permute-start(bf16[4,256,256]{2,1,0:T(8,128)(2,1)S(1)} %broadcast_select_fusion.1), channel_id=1, source_target_pairs={{0,8},{1,9},{10,2},{11,3},{4,12},{5,13},{14,6},{15,7},{16,24},{17,... | collective-permute-start | bytes 1572872 | tf_op jit(solution)/shard_map/ppermute | solution.py:80
  25.0 1.6 %collective-permute-start.2 = (bf16[4,256,256]{2,1,0:T(8,128)(2,1)S(1)}, bf16[4,256,256]{2,1,0:T(8,128)(2,1)S(1)}, u32[]{:S(2)}, u32[]{:S(2)}) collective-permute-start(bf16[4,256,256]{2,1,0:T(8,128)(2,1)S(1)} %get-tuple-element.43), channel_id=1, source_target_pairs={{0,1},{1,0},{2,3},{3,2},{4,5},{5,4},{6,7},{7,6},{8,9},{9,8},{10,11... | collective-permute-start | bytes 1572872 | tf_op jit(solution)/shard_map/ppermute | solution.py:83
  27.2 1.3 %bitcast_convert_fusion = bf16[8,256,256]{2,1,0:T(8,128)(2,1)S(1)} fusion(bf16[8,4,256,256]{3,2,1,0:T(8,128)(2,1)S(1)} %copy-done.6, pred[8,4]{1,0:T(8,128)(4,1)S(1)} %copy.23, bf16[4,256,256]{2,1,0:T(8,128)(2,1)S(1)} %broadcast_select_fusion.1, bf16[4,256,256]{2,1,0:T(8,128)(2,1)S(1)} %collective-permute-done.6, pred[]{:T(512)S(6)} %eq.18), kind=kOutput, calls=%fused_computation.6 | convolution fusion | flops 1076625408 | bytes 6291489 | tf_op jit(solution)/shard_map/ijab,jbc->iac/dot_general | solution.py:110
  29.4 6.9 %collective-permute-done.2 = bf16[4,256,256]{2,1,0:T(8,128)(2,1)S(1)} collective-permute-done((bf16[4,256,256]{2,1,0:T(8,128)(2,1)S(1)}, bf16[4,256,256]{2,1,0:T(8,128)(2,1)S(1)}, u32[]{:S(2)}, u32[]{:S(2)}) %collective-permute-start.2) | collective-permute-done | bytes 524320 | tf_op jit(solution)/shard_map/ppermute | solution.py:83
  36.7 2.5 %collective-permute-start.8 = (bf16[192,256]{1,0:T(8,128)(2,1)S(1)}, bf16[192,256]{1,0:T(8,128)(2,1)S(1)}, u32[]{:S(2)}, u32[]{:S(2)}) collective-permute-start(bf16[192,256]{1,0:T(8,128)(2,1)S(1)} %dynamic-slice_convert_fusion.1), channel_id=1, source_target_pairs={{0,16},{1,17},{2,18},{3,19},{4,20},{5,21},{6,22},{7,23},{8,24},{9,... | collective-permute-start | bytes 294920 | tf_op jit(solution)/shard_map/ppermute | solution.py:86
  39.3 1.6 %collective-permute-start.10 = (bf16[4,256,256]{2,1,0:T(8,128)(2,1)S(1)}, bf16[4,256,256]{2,1,0:T(8,128)(2,1)S(1)}, u32[]{:S(2)}, u32[]{:S(2)}) collective-permute-start(bf16[4,256,256]{2,1,0:T(8,128)(2,1)S(1)} %get-tuple-element.21), channel_id=1, source_target_pairs={{0,1},{1,0},{2,3},{3,2},{4,5},{5,4},{6,7},{7,6},{8,9},{9,8},{10,11... | collective-permute-start | bytes 1572872 | tf_op jit(solution)/shard_map/ppermute | solution.py:83
  40.9 1.5 %collective-permute-done.8 = bf16[192,256]{1,0:T(8,128)(2,1)S(1)} collective-permute-done((bf16[192,256]{1,0:T(8,128)(2,1)S(1)}, bf16[192,256]{1,0:T(8,128)(2,1)S(1)}, u32[]{:S(2)}, u32[]{:S(2)}) %collective-permute-start.8) | collective-permute-done | bytes 98336 | tf_op jit(solution)/shard_map/ppermute | solution.py:86
  42.5 2.9 %collective-permute-start.9 = (bf16[192,256]{1,0:T(8,128)(2,1)S(1)}, bf16[192,256]{1,0:T(8,128)(2,1)S(1)}, u32[]{:S(2)}, u32[]{:S(2)}) collective-permute-start(bf16[192,256]{1,0:T(8,128)(2,1)S(1)} %add_convert_fusion.4), channel_id=1, source_target_pairs={{0,4},{1,5},{2,6},{3,7},{4,0},{5,1},{6,2},{7,3},{8,12},{9,13},{10,... | collective-permute-start | bytes 294920 | tf_op jit(solution)/shard_map/ppermute | solution.py:83
  45.4 2.8 %collective-permute-start.4 = (bf16[1,256,256]{2,1,0:T(8,128)(2,1)S(1)}, bf16[1,256,256]{2,1,0:T(8,128)(2,1)S(1)}, u32[]{:S(2)}, u32[]{:S(2)}) collective-permute-start(bf16[1,256,256]{2,1,0:T(8,128)(2,1)S(1)} %fusion.30), channel_id=1, source_target_pairs={{0,4},{1,5},{2,6},{3,7},{4,0},{5,1},{6,2},{7,3},{8,12},{9,13},{10,... | collective-permute-start | bytes 393224 | tf_op jit(solution)/shard_map/ppermute | solution.py:83
  48.2 4.7 %collective-permute-done.9 = bf16[192,256]{1,0:T(8,128)(2,1)S(1)} collective-permute-done((bf16[192,256]{1,0:T(8,128)(2,1)S(1)}, bf16[192,256]{1,0:T(8,128)(2,1)S(1)}, u32[]{:S(2)}, u32[]{:S(2)}) %collective-permute-start.9) | collective-permute-done | bytes 98336 | tf_op jit(solution)/shard_map/ppermute | solution.py:83
  53.7 1.6 %collective-permute-start.13 = (bf16[2,256,256]{2,1,0:T(8,128)(2,1)S(1)}, bf16[2,256,256]{2,1,0:T(8,128)(2,1)S(1)}, u32[]{:S(2)}, u32[]{:S(2)}) collective-permute-start(bf16[2,256,256]{2,1,0:T(8,128)(2,1)S(1)} %fusion.26), channel_id=1, source_target_pairs={{0,2},{1,3},{2,0},{3,1},{4,6},{5,7},{6,4},{7,5},{8,10},{9,11},{10,... | collective-permute-start | bytes 786440 | tf_op jit(solution)/shard_map/ppermute | solution.py:83
  55.3 3.6 %collective-permute-done.11 = bf16[192,256]{1,0:T(8,128)(2,1)S(1)} collective-permute-done((bf16[192,256]{1,0:T(8,128)(2,1)S(1)}, bf16[192,256]{1,0:T(8,128)(2,1)S(1)}, u32[]{:S(2)}, u32[]{:S(2)}) %collective-permute-start.11) | collective-permute-done | bytes 98336 | tf_op jit(solution)/shard_map/ppermute | solution.py:83
  58.9 1.6 %collective-permute-start.12 = (bf16[192,256]{1,0:T(8,128)(2,1)S(1)}, bf16[192,256]{1,0:T(8,128)(2,1)S(1)}, u32[]{:S(2)}, u32[]{:S(2)}) collective-permute-start(bf16[192,256]{1,0:T(8,128)(2,1)S(1)} %add_convert_fusion.2), channel_id=1, source_target_pairs={{0,1},{1,0},{2,3},{3,2},{4,5},{5,4},{6,7},{7,6},{8,9},{9,8},{10,11... | collective-permute-start | bytes 294920 | tf_op jit(solution)/shard_map/ppermute | solution.py:83
  60.6 3.1 %collective-permute-done.12 = bf16[192,256]{1,0:T(8,128)(2,1)S(1)} collective-permute-done((bf16[192,256]{1,0:T(8,128)(2,1)S(1)}, bf16[192,256]{1,0:T(8,128)(2,1)S(1)}, u32[]{:S(2)}, u32[]{:S(2)}) %collective-permute-start.12) | collective-permute-done | bytes 98336 | tf_op jit(solution)/shard_map/ppermute | solution.py:83
  63.7 1.7 %collective-permute-start.14 = (bf16[192,256]{1,0:T(8,128)(2,1)S(1)}, bf16[192,256]{1,0:T(8,128)(2,1)S(1)}, u32[]{:S(2)}, u32[]{:S(2)}) collective-permute-start(bf16[192,256]{1,0:T(8,128)(2,1)S(1)} %add_convert_fusion.1), channel_id=1, source_target_pairs={{0,16},{1,17},{2,18},{3,19},{4,20},{5,21},{6,22},{7,23},{8,24},{9,... | collective-permute-start | bytes 294920 | tf_op jit(solution)/shard_map/ppermute | solution.py:86
  65.4 1.5 %collective-permute-start.15 = (bf16[1,256,256]{2,1,0:T(8,128)(2,1)S(1)}, bf16[1,256,256]{2,1,0:T(8,128)(2,1)S(1)}, u32[]{:S(2)}, u32[]{:S(2)}) collective-permute-start(bf16[1,256,256]{2,1,0:T(8,128)(2,1)S(1)} %fusion.29), channel_id=1, source_target_pairs={{0,4},{1,5},{2,6},{3,7},{4,0},{5,1},{6,2},{7,3},{8,12},{9,13},{10,... | collective-permute-start | bytes 393224 | tf_op jit(solution)/shard_map/ppermute | solution.py:83
  66.9 1.4 %collective-permute-done.14 = bf16[192,256]{1,0:T(8,128)(2,1)S(1)} collective-permute-done((bf16[192,256]{1,0:T(8,128)(2,1)S(1)}, bf16[192,256]{1,0:T(8,128)(2,1)S(1)}, u32[]{:S(2)}, u32[]{:S(2)}) %collective-permute-start.14) | collective-permute-done | bytes 98336 | tf_op jit(solution)/shard_map/ppermute | solution.py:86
  68.6 3.6 %collective-permute-done.15 = bf16[1,256,256]{2,1,0:T(8,128)(2,1)S(1)} collective-permute-done((bf16[1,256,256]{2,1,0:T(8,128)(2,1)S(1)}, bf16[1,256,256]{2,1,0:T(8,128)(2,1)S(1)}, u32[]{:S(2)}, u32[]{:S(2)}) %collective-permute-start.15) | collective-permute-done | bytes 131104 | tf_op jit(solution)/shard_map/ppermute | solution.py:83
  72.2 0.9 %fusion.28 = bf16[256,256]{1,0:T(8,128)(2,1)} fusion(f32[2,1,256,256]{3,2,1,0:T(8,128)S(1)} %convert_add_fusion, s32[]{:T(128)S(6)} %select_n.152, bf16[1,256,256]{2,1,0:T(8,128)(2,1)S(1)} %collective-permute-done.15, bf16[256,256]{1,0:T(8,128)(2,1)S(1)} %copy-done.2, bf16[1,256,256]{2,1,0:T(8,128)(2,1)S(1)} %fusion.33, ...), kind=kOutput, calls=%fused_computation.44 | convolution fusion | flops 34013184 | bytes 917512 | tf_op jit(solution)/shard_map/dot_general | solution.py:152
  73.7 2.3 %shard_map.128 = (bf16[256,256]{1,0:T(8,128)(2,1)}, bf16[256,256]{1,0:T(8,128)(2,1)}, bf16[256,256]{1,0:T(8,128)(2,1)}) custom-call(s32[1]{0:T(128)} %bitcast.35.place, bf16[384,256]{1,0:T(8,128)(2,1)} %copy-done, bf16[384,256]{1,0:T(8,128)(2,1)} %copy-done.5, bf16[256,256]{1,0:T(8,128)(2,1)} %link.1, f32[256,256]{1,0:T(8,128)} %inverse_one.1, ...), custom_call_target="tpu_custom_call" | custom-call | flops 100663296 | bytes 1572864 | tf_op jit(solution)/shard_map/pallas_call | solution.py:29
  (55 shorter events, 5.7 us)
Async XLA Ops:
  1.7 11.6 %collective-permute-start = (bf16[4,256,256]{2,1,0:T(8,128)(2,1)S(1)}, bf16[4,256,256]{2,1,0:T(8,128)(2,1)S(1)}, u32[]{:S(2)}, u32[]{:S(2)}) collective-permute-start(bf16[4,256,256]{2,1,0:T(8,128)(2,1)S(1)} %constant_dynamic-slice_fusion.3), channel_id=1, source_target_pairs={{0,16},{1,17},{10,26},{11,27},{20,4},{21,5},{30,14},{31,15}} | collective-permute-start | bytes 1572872 | tf_op jit(solution)/shard_map/ppermute | solution.py:70
  7.7 11.2 %collective-permute-start.5 = (bf16[4,256,256]{2,1,0:T(8,128)(2,1)S(1)}, bf16[4,256,256]{2,1,0:T(8,128)(2,1)S(1)}, u32[]{:S(2)}, u32[]{:S(2)}) collective-permute-start(bf16[4,256,256]{2,1,0:T(8,128)(2,1)S(1)} %constant_dynamic-slice_fusion.1), channel_id=1, source_target_pairs={{0,16},{1,17},{10,26},{11,27},{20,4},{21,5},{30,14},{31,15}} | collective-permute-start | bytes 1572872 | tf_op jit(solution)/shard_map/ppermute | solution.py:70
  13.4 5.6 %collective-permute-start.1 = (bf16[4,256,256]{2,1,0:T(8,128)(2,1)S(1)}, bf16[4,256,256]{2,1,0:T(8,128)(2,1)S(1)}, u32[]{:S(2)}, u32[]{:S(2)}) collective-permute-start(bf16[4,256,256]{2,1,0:T(8,128)(2,1)S(1)} %broadcast_select_fusion.2), channel_id=1, source_target_pairs={{0,8},{1,9},{10,2},{11,3},{4,12},{5,13},{14,6},{15,7},{16,24},{17,... | collective-permute-start | bytes 1572872 | tf_op jit(solution)/shard_map/ppermute | solution.py:80
  19.0 3.6 %copy-start.3 = (bf16[8,256,256]{2,1,0:T(8,128)(2,1)S(1)}, bf16[8,256,256]{2,1,0:T(8,128)(2,1)}, u32[]{:S(2)}) copy-start(bf16[8,256,256]{2,1,0:T(8,128)(2,1)} %param.13) | copy-start | bytes 3145732
  22.6 4.0 %copy-start.4 = (bf16[8,256,256]{2,1,0:T(8,128)(2,1)S(1)}, bf16[8,256,256]{2,1,0:T(8,128)(2,1)}, u32[]{:S(2)}) copy-start(bf16[8,256,256]{2,1,0:T(8,128)(2,1)} %param.14) | copy-start | bytes 3145732
  23.3 3.9 %copy-start.6 = (bf16[8,4,256,256]{3,2,1,0:T(8,128)(2,1)S(1)}, bf16[8,4,256,256]{3,2,1,0:T(8,128)(2,1)}, u32[]{:S(2)}) copy-start(bf16[8,4,256,256]{3,2,1,0:T(8,128)(2,1)} %param.9) | copy-start | bytes 12582916
  23.3 3.9 %collective-permute-start.6 = (bf16[4,256,256]{2,1,0:T(8,128)(2,1)S(1)}, bf16[4,256,256]{2,1,0:T(8,128)(2,1)S(1)}, u32[]{:S(2)}, u32[]{:S(2)}) collective-permute-start(bf16[4,256,256]{2,1,0:T(8,128)(2,1)S(1)} %broadcast_select_fusion.1), channel_id=1, source_target_pairs={{0,8},{1,9},{10,2},{11,3},{4,12},{5,13},{14,6},{15,7},{16,24},{17,... | collective-permute-start | bytes 1572872 | tf_op jit(solution)/shard_map/ppermute | solution.py:80
  25.0 11.3 %collective-permute-start.2 = (bf16[4,256,256]{2,1,0:T(8,128)(2,1)S(1)}, bf16[4,256,256]{2,1,0:T(8,128)(2,1)S(1)}, u32[]{:S(2)}, u32[]{:S(2)}) collective-permute-start(bf16[4,256,256]{2,1,0:T(8,128)(2,1)S(1)} %get-tuple-element.43), channel_id=1, source_target_pairs={{0,1},{1,0},{2,3},{3,2},{4,5},{5,4},{6,7},{7,6},{8,9},{9,8},{10,11... | collective-permute-start | bytes 1572872 | tf_op jit(solution)/shard_map/ppermute | solution.py:83
  29.3 7.3 %collective-permute-start.7 = (bf16[384,256]{1,0:T(8,128)(2,1)S(1)}, bf16[384,256]{1,0:T(8,128)(2,1)S(1)}, u32[]{:S(2)}, u32[]{:S(2)}) collective-permute-start(bf16[384,256]{1,0:T(8,128)(2,1)S(1)} %dynamic-slice_convert_fusion), channel_id=1, source_target_pairs={{0,8},{1,9},{2,10},{3,11},{4,12},{5,13},{6,14},{7,15},{8,0},{9,1},... | collective-permute-start | bytes 589832 | tf_op jit(solution)/shard_map/ppermute | solution.py:86
  36.4 8.9 %collective-permute-start.3 = (bf16[2,256,256]{2,1,0:T(8,128)(2,1)S(1)}, bf16[2,256,256]{2,1,0:T(8,128)(2,1)S(1)}, u32[]{:S(2)}, u32[]{:S(2)}) collective-permute-start(bf16[2,256,256]{2,1,0:T(8,128)(2,1)S(1)} %get-tuple-element.39), channel_id=1, source_target_pairs={{0,2},{1,3},{2,0},{3,1},{4,6},{5,7},{6,4},{7,5},{8,10},{9,11},{10,... | collective-permute-start | bytes 786440 | tf_op jit(solution)/shard_map/ppermute | solution.py:83
  36.6 35.5 %copy-start.2 = (bf16[256,256]{1,0:T(8,128)(2,1)S(1)}, bf16[256,256]{1,0:T(8,128)(2,1)}, u32[]{:S(2)}) copy-start(bf16[256,256]{1,0:T(8,128)(2,1)} %link.1) | copy-start | bytes 393220
  36.7 5.7 %collective-permute-start.8 = (bf16[192,256]{1,0:T(8,128)(2,1)S(1)}, bf16[192,256]{1,0:T(8,128)(2,1)S(1)}, u32[]{:S(2)}, u32[]{:S(2)}) collective-permute-start(bf16[192,256]{1,0:T(8,128)(2,1)S(1)} %dynamic-slice_convert_fusion.1), channel_id=1, source_target_pairs={{0,16},{1,17},{2,18},{3,19},{4,20},{5,21},{6,22},{7,23},{8,24},{9,... | collective-permute-start | bytes 294920 | tf_op jit(solution)/shard_map/ppermute | solution.py:86
  39.3 13.8 %collective-permute-start.10 = (bf16[4,256,256]{2,1,0:T(8,128)(2,1)S(1)}, bf16[4,256,256]{2,1,0:T(8,128)(2,1)S(1)}, u32[]{:S(2)}, u32[]{:S(2)}) collective-permute-start(bf16[4,256,256]{2,1,0:T(8,128)(2,1)S(1)} %get-tuple-element.21), channel_id=1, source_target_pairs={{0,1},{1,0},{2,3},{3,2},{4,5},{5,4},{6,7},{7,6},{8,9},{9,8},{10,11... | collective-permute-start | bytes 1572872 | tf_op jit(solution)/shard_map/ppermute | solution.py:83
  42.5 10.5 %collective-permute-start.9 = (bf16[192,256]{1,0:T(8,128)(2,1)S(1)}, bf16[192,256]{1,0:T(8,128)(2,1)S(1)}, u32[]{:S(2)}, u32[]{:S(2)}) collective-permute-start(bf16[192,256]{1,0:T(8,128)(2,1)S(1)} %add_convert_fusion.4), channel_id=1, source_target_pairs={{0,4},{1,5},{2,6},{3,7},{4,0},{5,1},{6,2},{7,3},{8,12},{9,13},{10,... | collective-permute-start | bytes 294920 | tf_op jit(solution)/shard_map/ppermute | solution.py:83
  45.4 23.0 %collective-permute-start.4 = (bf16[1,256,256]{2,1,0:T(8,128)(2,1)S(1)}, bf16[1,256,256]{2,1,0:T(8,128)(2,1)S(1)}, u32[]{:S(2)}, u32[]{:S(2)}) collective-permute-start(bf16[1,256,256]{2,1,0:T(8,128)(2,1)S(1)} %fusion.30), channel_id=1, source_target_pairs={{0,4},{1,5},{2,6},{3,7},{4,0},{5,1},{6,2},{7,3},{8,12},{9,13},{10,... | collective-permute-start | bytes 393224 | tf_op jit(solution)/shard_map/ppermute | solution.py:83
  53.2 5.7 %collective-permute-start.11 = (bf16[192,256]{1,0:T(8,128)(2,1)S(1)}, bf16[192,256]{1,0:T(8,128)(2,1)S(1)}, u32[]{:S(2)}, u32[]{:S(2)}) collective-permute-start(bf16[192,256]{1,0:T(8,128)(2,1)S(1)} %add_convert_fusion.3), channel_id=1, source_target_pairs={{0,2},{1,3},{2,0},{3,1},{4,6},{5,7},{6,4},{7,5},{8,10},{9,11},{10,... | collective-permute-start | bytes 294920 | tf_op jit(solution)/shard_map/ppermute | solution.py:83
  53.7 9.9 %collective-permute-start.13 = (bf16[2,256,256]{2,1,0:T(8,128)(2,1)S(1)}, bf16[2,256,256]{2,1,0:T(8,128)(2,1)S(1)}, u32[]{:S(2)}, u32[]{:S(2)}) collective-permute-start(bf16[2,256,256]{2,1,0:T(8,128)(2,1)S(1)} %fusion.26), channel_id=1, source_target_pairs={{0,2},{1,3},{2,0},{3,1},{4,6},{5,7},{6,4},{7,5},{8,10},{9,11},{10,... | collective-permute-start | bytes 786440 | tf_op jit(solution)/shard_map/ppermute | solution.py:83
  58.9 4.7 %collective-permute-start.12 = (bf16[192,256]{1,0:T(8,128)(2,1)S(1)}, bf16[192,256]{1,0:T(8,128)(2,1)S(1)}, u32[]{:S(2)}, u32[]{:S(2)}) collective-permute-start(bf16[192,256]{1,0:T(8,128)(2,1)S(1)} %add_convert_fusion.2), channel_id=1, source_target_pairs={{0,1},{1,0},{2,3},{3,2},{4,5},{5,4},{6,7},{7,6},{8,9},{9,8},{10,11... | collective-permute-start | bytes 294920 | tf_op jit(solution)/shard_map/ppermute | solution.py:83
  63.7 4.7 %collective-permute-start.14 = (bf16[192,256]{1,0:T(8,128)(2,1)S(1)}, bf16[192,256]{1,0:T(8,128)(2,1)S(1)}, u32[]{:S(2)}, u32[]{:S(2)}) collective-permute-start(bf16[192,256]{1,0:T(8,128)(2,1)S(1)} %add_convert_fusion.1), channel_id=1, source_target_pairs={{0,16},{1,17},{2,18},{3,19},{4,20},{5,21},{6,22},{7,23},{8,24},{9,... | collective-permute-start | bytes 294920 | tf_op jit(solution)/shard_map/ppermute | solution.py:86
  65.4 6.7 %collective-permute-start.15 = (bf16[1,256,256]{2,1,0:T(8,128)(2,1)S(1)}, bf16[1,256,256]{2,1,0:T(8,128)(2,1)S(1)}, u32[]{:S(2)}, u32[]{:S(2)}) collective-permute-start(bf16[1,256,256]{2,1,0:T(8,128)(2,1)S(1)} %fusion.29), channel_id=1, source_target_pairs={{0,4},{1,5},{2,6},{3,7},{4,0},{5,1},{6,2},{7,3},{8,12},{9,13},{10,... | collective-permute-start | bytes 393224 | tf_op jit(solution)/shard_map/ppermute | solution.py:83
  68.4 4.6 %copy-start = (bf16[384,256]{1,0:T(8,128)(2,1)}, bf16[384,256]{1,0:T(8,128)(2,1)S(1)}, u32[]{:S(2)}) copy-start(bf16[384,256]{1,0:T(8,128)(2,1)S(1)} %pad_maximum_fusion.1.mine) | copy-start | bytes 589828
  68.4 4.6 %collective-permute-start.16 = (bf16[384,256]{1,0:T(8,128)(2,1)S(1)}, bf16[384,256]{1,0:T(8,128)(2,1)S(1)}, u32[]{:S(2)}, u32[]{:S(2)}) collective-permute-start(bf16[384,256]{1,0:T(8,128)(2,1)S(1)} %pad_maximum_fusion.1.mine), channel_id=1, source_target_pairs={{0,8},{1,9},{2,10},{3,11},{4,12},{5,13},{6,14},{7,15},{8,0},{9,1},... | collective-permute-start | bytes 589832 | tf_op jit(solution)/shard_map/ppermute | solution.py:86
  68.6 7.5 %copy-start.1 = (bf16[1,256,256]{2,1,0:T(8,128)(2,1)}, bf16[1,256,256]{2,1,0:T(8,128)(2,1)S(1)}, u32[]{:S(2)}) copy-start(bf16[1,256,256]{2,1,0:T(8,128)(2,1)S(1)} %fusion.33) | copy-start | bytes 393220
  73.0 0.7 copy-start.5

commit v9 on v4

--- a/solution.py
+++ b/solution.py
@@ -124,6 +124,7 @@
     keep_one, one = first_swap(all_one)
     all_two = products(marks[1], over_cores(after(have_two, all_one)))
     keep_two, two = first_swap(all_two, one[0])
+    all_one = after(all_one, all_two)
     sums = contraction(first, all_one), contraction(all_one, second_in_one), contraction(second, all_two)
     for _ in range(1, bits):
         keep_one = next_swap(keep_one, one)

time: 74.2 us -> 76 us (1.024)
  matrix products: 7.62 us -> 9.86 us
  waiting for transfers between devices: 25.2 us -> 26.9 us
  local copies, waits for them, and re-layouts: 7.21 us -> 5.9 us
    ppermute x2, waiting for transfers between devices: 1.41 us -> 5.34 us  [over_chips(): got = after(lax.ppermute(piece, BOTH, perm), *earlier)]
    ppermute x9, waiting for transfers between devices: 18.2 us -> 15.6 us  [swap(): lax.ppermute(array, BOTH, [(at(r, c), at(r, c ^ 1 << bit)) for r, c in ev...]
    dot_general x2, matrix products: 4.9 us -> 7.13 us  [products(): jnp.einsum('ijab,jbc->iac', kept, column, preferred_element_type=F32)]
    dynamic_slice x2, local copies, waits for them, and re-layouts: 2.48 us -> 1.17 us  [shards(): m[row * rows + col].astype(F32)]
  transfers between devices with their start and end apart: 17 -> 17, of which waited for: 9 -> 9; matrix products, arithmetic and copies ran while one was open for 15% -> 16% of each run, Pallas kernels for 3% -> 3%
where the time goes in v9:
time: 76 us; the launch traced here: 75.6 us
  waiting for transfers between devices  26.9 us (35%)
  starting transfers between devices  25.9 us (34%)
  matrix products  9.86 us (13%)
  local copies, waits for them, and re-layouts  5.9 us (8%)
  between operations  2.42 us (3%)
  other arithmetic  2.38 us (3%)
  Pallas kernels  2.32 us (3%)
    ppermute x9, waiting for transfers between devices, swap(): lax.ppermute(array, BOTH, [(at(r, c), at(r, c ^ 1 << bit)) for r, c in ev...  15.6 us
    ppermute x9, starting transfers between devices, swap(): lax.ppermute(array, BOTH, [(at(r, c), at(r, c ^ 1 << bit)) for r, c in ev...  12.5 us
    dot_general x2, matrix products, products(): jnp.einsum('ijab,jbc->iac', kept, column, preferred_element_type=F32)  7.13 us
    ppermute x2, starting transfers between devices, over_chips(): got = after(lax.ppermute(piece, BOTH, perm), *earlier)  6.23 us
    ppermute x4, waiting for transfers between devices, swap_rows(): lax.ppermute(array, BOTH, [(at(r, c), at(r ^ 1 << bit, c)) for r, c in ev...  5.87 us
    ppermute x2, waiting for transfers between devices, over_chips(): got = after(lax.ppermute(piece, BOTH, perm), *earlier)  5.34 us
    ppermute x4, starting transfers between devices, swap_rows(): lax.ppermute(array, BOTH, [(at(r, c), at(r ^ 1 << bit, c)) for r, c in ev...  4.47 us
    dynamic_slice x4, local copies, waits for them, and re-layouts, part_of(): return lax.dynamic_slice_in_dim(array, start, size, 0)  3.62 us
  transfers between devices with their start and end apart: 17, of which 9 were waited for; matrix products, arithmetic and copies ran while one was open for 16% of the time, Pallas kernels for 3%

profile of v9, /device:TPU:0, one launch (start us, length us, event | category | flops | bytes accessed | tf_op | source)
XLA Modules:
  0.0 75.6 jit_solution(8604136797462606638)
XLA Ops:
  0.6 1.1 %constant_dynamic-slice_fusion.3 = bf16[4,256,256]{2,1,0:T(8,128)(2,1)S(1)} fusion(bf16[8,256,256]{2,1,0:T(8,128)(2,1)} %param.13, s32[]{:T(128)S(6)} %select_n.145), kind=kLoop, calls=%fused_computation.69 | loop fusion | bytes 1048580 | tf_op jit(solution)/shard_map/dynamic_slice | solution.py:103
  1.7 4.9 %collective-permute-start = (bf16[4,256,256]{2,1,0:T(8,128)(2,1)S(1)}, bf16[4,256,256]{2,1,0:T(8,128)(2,1)S(1)}, u32[]{:S(2)}, u32[]{:S(2)}) collective-permute-start(bf16[4,256,256]{2,1,0:T(8,128)(2,1)S(1)} %constant_dynamic-slice_fusion.3), channel_id=1, source_target_pairs={{0,16},{1,17},{10,26},{11,27},{20,4},{21,5},{30,14},{31,15}} | collective-permute-start | bytes 1572872 | tf_op jit(solution)/shard_map/ppermute | solution.py:70
  6.6 1.1 %constant_dynamic-slice_fusion.1 = bf16[4,256,256]{2,1,0:T(8,128)(2,1)S(1)} fusion(bf16[8,256,256]{2,1,0:T(8,128)(2,1)} %param.14, s32[]{:T(128)S(6)} %select_n.145), kind=kLoop, calls=%fused_computation.67 | loop fusion | bytes 1048580 | tf_op jit(solution)/shard_map/dynamic_slice | solution.py:103
  7.7 1.3 %collective-permute-start.5 = (bf16[4,256,256]{2,1,0:T(8,128)(2,1)S(1)}, bf16[4,256,256]{2,1,0:T(8,128)(2,1)S(1)}, u32[]{:S(2)}, u32[]{:S(2)}) collective-permute-start(bf16[4,256,256]{2,1,0:T(8,128)(2,1)S(1)} %constant_dynamic-slice_fusion.1), channel_id=1, source_target_pairs={{0,16},{1,17},{10,26},{11,27},{20,4},{21,5},{30,14},{31,15}} | collective-permute-start | bytes 1572872 | tf_op jit(solution)/shard_map/ppermute | solution.py:70
  9.1 0.7 dynamic_slice.81
  9.8 0.7 dynamic_slice.83
  10.6 0.7 broadcast_compare_fusion.2
  11.3 0.8 %broadcast_compare_fusion = (pred[8,4]{0,1:T(4,128)(4,1)S(1)}, pred[8,4]{0,1:T(4,128)(4,1)S(1)}) fusion(s32[8,4]{0,1:T(4,128)} %param.10, s32[4]{0:T(128)S(1)} %dynamic_slice.83, s32[4]{0:T(128)S(1)} %dynamic_slice.81), kind=kLoop, calls=%fused_computation.71 | loop fusion | flops 128 | bytes 224 | tf_op jit(solution)/shard_map/gt | solution.py:106
  12.1 1.2 %collective-permute-done = bf16[4,256,256]{2,1,0:T(8,128)(2,1)S(1)} collective-permute-done((bf16[4,256,256]{2,1,0:T(8,128)(2,1)S(1)}, bf16[4,256,256]{2,1,0:T(8,128)(2,1)S(1)}, u32[]{:S(2)}, u32[]{:S(2)}) %collective-permute-start) | collective-permute-done | bytes 524320 | tf_op jit(solution)/shard_map/ppermute | solution.py:70
  13.4 1.3 %collective-permute-start.1 = (bf16[4,256,256]{2,1,0:T(8,128)(2,1)S(1)}, bf16[4,256,256]{2,1,0:T(8,128)(2,1)S(1)}, u32[]{:S(2)}, u32[]{:S(2)}) collective-permute-start(bf16[4,256,256]{2,1,0:T(8,128)(2,1)S(1)} %broadcast_select_fusion.2), channel_id=1, source_target_pairs={{0,8},{1,9},{10,2},{11,3},{4,12},{5,13},{14,6},{15,7},{16,24},{17,... | collective-permute-start | bytes 1572872 | tf_op jit(solution)/shard_map/ppermute | solution.py:80
  14.8 4.1 %collective-permute-done.5 = bf16[4,256,256]{2,1,0:T(8,128)(2,1)S(1)} collective-permute-done((bf16[4,256,256]{2,1,0:T(8,128)(2,1)S(1)}, bf16[4,256,256]{2,1,0:T(8,128)(2,1)S(1)}, u32[]{:S(2)}, u32[]{:S(2)}) %collective-permute-start.5) | collective-permute-done | bytes 524320 | tf_op jit(solution)/shard_map/ppermute | solution.py:70
  19.0 3.5 %bitcast_convert_fusion.1 = bf16[8,256,256]{2,1,0:T(8,128)(2,1)S(1)} fusion(bf16[8,4,256,256]{3,2,1,0:T(8,128)(2,1)} %param.9, pred[8,4]{1,0:T(8,128)(4,1)S(1)} %copy.19, bf16[4,256,256]{2,1,0:T(8,128)(2,1)S(1)} %broadcast_select_fusion.2, bf16[4,256,256]{2,1,0:T(8,128)(2,1)S(1)} %collective-permute-done.1, pred[]{:T(512)S(6)} %eq.18), kind=kOutput, calls=%fused_computation.7 | convolution fusion | flops 1076625408 | bytes 6291489 | tf_op jit(solution)/shard_map/ijab,jbc->iac/dot_general | solution.py:110
  22.5 1.3 %collective-permute-start.6 = (bf16[4,256,256]{2,1,0:T(8,128)(2,1)S(1)}, bf16[4,256,256]{2,1,0:T(8,128)(2,1)S(1)}, u32[]{:S(2)}, u32[]{:S(2)}) collective-permute-start(bf16[4,256,256]{2,1,0:T(8,128)(2,1)S(1)} %broadcast_select_fusion.1), channel_id=1, source_target_pairs={{0,8},{1,9},{10,2},{11,3},{4,12},{5,13},{14,6},{15,7},{16,24},{17,... | collective-permute-start | bytes 1572872 | tf_op jit(solution)/shard_map/ppermute | solution.py:80
  26.6 1.6 %collective-permute-start.2 = (bf16[4,256,256]{2,1,0:T(8,128)(2,1)S(1)}, bf16[4,256,256]{2,1,0:T(8,128)(2,1)S(1)}, u32[]{:S(2)}, u32[]{:S(2)}) collective-permute-start(bf16[4,256,256]{2,1,0:T(8,128)(2,1)S(1)} %get-tuple-element.43), channel_id=1, source_target_pairs={{0,1},{1,0},{2,3},{3,2},{4,5},{5,4},{6,7},{7,6},{8,9},{9,8},{10,11... | collective-permute-start | bytes 1572872 | tf_op jit(solution)/shard_map/ppermute | solution.py:83
  28.2 3.6 %bitcast_convert_fusion = bf16[8,256,256]{2,1,0:T(8,128)(2,1)S(1)} fusion(bf16[8,4,256,256]{3,2,1,0:T(8,128)(2,1)} %param.9, pred[8,4]{1,0:T(8,128)(4,1)S(1)} %copy.21, bf16[4,256,256]{2,1,0:T(8,128)(2,1)S(1)} %broadcast_select_fusion.1, bf16[4,256,256]{2,1,0:T(8,128)(2,1)S(1)} %collective-permute-done.6, pred[]{:T(512)S(6)} %eq.18), kind=kOutput, calls=%fused_computation.6 | convolution fusion | flops 1076625408 | bytes 6291489 | tf_op jit(solution)/shard_map/ijab,jbc->iac/dot_general | solution.py:110
  34.1 4.6 %collective-permute-done.2 = bf16[4,256,256]{2,1,0:T(8,128)(2,1)S(1)} collective-permute-done((bf16[4,256,256]{2,1,0:T(8,128)(2,1)S(1)}, bf16[4,256,256]{2,1,0:T(8,128)(2,1)S(1)}, u32[]{:S(2)}, u32[]{:S(2)}) %collective-permute-start.2) | collective-permute-done | bytes 524320 | tf_op jit(solution)/shard_map/ppermute | solution.py:83
  38.6 1.6 %collective-permute-start.7 = (bf16[4,256,256]{2,1,0:T(8,128)(2,1)S(1)}, bf16[4,256,256]{2,1,0:T(8,128)(2,1)S(1)}, u32[]{:S(2)}, u32[]{:S(2)}) collective-permute-start(bf16[4,256,256]{2,1,0:T(8,128)(2,1)S(1)} %get-tuple-element.20), channel_id=1, source_target_pairs={{0,1},{1,0},{2,3},{3,2},{4,5},{5,4},{6,7},{7,6},{8,9},{9,8},{10,11... | collective-permute-start | bytes 1572872 | tf_op jit(solution)/shard_map/ppermute | solution.py:83
  40.5 2.5 %collective-permute-start.11 = (bf16[192,256]{1,0:T(8,128)(2,1)S(1)}, bf16[192,256]{1,0:T(8,128)(2,1)S(1)}, u32[]{:S(2)}, u32[]{:S(2)}) collective-permute-start(bf16[192,256]{1,0:T(8,128)(2,1)S(1)} %dynamic-slice_convert_fusion.1), channel_id=1, source_target_pairs={{0,16},{1,17},{2,18},{3,19},{4,20},{5,21},{6,22},{7,23},{8,24},{9,... | collective-permute-start | bytes 294920 | tf_op jit(solution)/shard_map/ppermute | solution.py:86
  43.1 2.5 %collective-permute-done.11 = bf16[192,256]{1,0:T(8,128)(2,1)S(1)} collective-permute-done((bf16[192,256]{1,0:T(8,128)(2,1)S(1)}, bf16[192,256]{1,0:T(8,128)(2,1)S(1)}, u32[]{:S(2)}, u32[]{:S(2)}) %collective-permute-start.11) | collective-permute-done | bytes 98336 | tf_op jit(solution)/shard_map/ppermute | solution.py:86
  45.7 3.2 %collective-permute-start.12 = (bf16[192,256]{1,0:T(8,128)(2,1)S(1)}, bf16[192,256]{1,0:T(8,128)(2,1)S(1)}, u32[]{:S(2)}, u32[]{:S(2)}) collective-permute-start(bf16[192,256]{1,0:T(8,128)(2,1)S(1)} %add_convert_fusion.4), channel_id=1, source_target_pairs={{0,4},{1,5},{2,6},{3,7},{4,0},{5,1},{6,2},{7,3},{8,12},{9,13},{10,... | collective-permute-start | bytes 294920 | tf_op jit(solution)/shard_map/ppermute | solution.py:83
  48.8 2.7 %collective-permute-start.4 = (bf16[1,256,256]{2,1,0:T(8,128)(2,1)S(1)}, bf16[1,256,256]{2,1,0:T(8,128)(2,1)S(1)}, u32[]{:S(2)}, u32[]{:S(2)}) collective-permute-start(bf16[1,256,256]{2,1,0:T(8,128)(2,1)S(1)} %fusion.30), channel_id=1, source_target_pairs={{0,4},{1,5},{2,6},{3,7},{4,0},{5,1},{6,2},{7,3},{8,12},{9,13},{10,... | collective-permute-start | bytes 393224 | tf_op jit(solution)/shard_map/ppermute | solution.py:83
  51.6 3.3 %collective-permute-done.12 = bf16[192,256]{1,0:T(8,128)(2,1)S(1)} collective-permute-done((bf16[192,256]{1,0:T(8,128)(2,1)S(1)}, bf16[192,256]{1,0:T(8,128)(2,1)S(1)}, u32[]{:S(2)}, u32[]{:S(2)}) %collective-permute-start.12) | collective-permute-done | bytes 98336 | tf_op jit(solution)/shard_map/ppermute | solution.py:83
  55.1 2.1 %collective-permute-start.8 = (bf16[2,256,256]{2,1,0:T(8,128)(2,1)S(1)}, bf16[2,256,256]{2,1,0:T(8,128)(2,1)S(1)}, u32[]{:S(2)}, u32[]{:S(2)}) collective-permute-start(bf16[2,256,256]{2,1,0:T(8,128)(2,1)S(1)} %fusion.26), channel_id=1, source_target_pairs={{0,2},{1,3},{2,0},{3,1},{4,6},{5,7},{6,4},{7,5},{8,10},{9,11},{10,... | collective-permute-start | bytes 786440 | tf_op jit(solution)/shard_map/ppermute | solution.py:83
  57.2 3.6 %collective-permute-done.13 = bf16[192,256]{1,0:T(8,128)(2,1)S(1)} collective-permute-done((bf16[192,256]{1,0:T(8,128)(2,1)S(1)}, bf16[192,256]{1,0:T(8,128)(2,1)S(1)}, u32[]{:S(2)}, u32[]{:S(2)}) %collective-permute-start.13) | collective-permute-done | bytes 98336 | tf_op jit(solution)/shard_map/ppermute | solution.py:83
  61.2 4.2 %collective-permute-done.14 = bf16[192,256]{1,0:T(8,128)(2,1)S(1)} collective-permute-done((bf16[192,256]{1,0:T(8,128)(2,1)S(1)}, bf16[192,256]{1,0:T(8,128)(2,1)S(1)}, u32[]{:S(2)}, u32[]{:S(2)}) %collective-permute-start.14) | collective-permute-done | bytes 98336 | tf_op jit(solution)/shard_map/ppermute | solution.py:83
  65.5 1.8 %collective-permute-start.15 = (bf16[192,256]{1,0:T(8,128)(2,1)S(1)}, bf16[192,256]{1,0:T(8,128)(2,1)S(1)}, u32[]{:S(2)}, u32[]{:S(2)}) collective-permute-start(bf16[192,256]{1,0:T(8,128)(2,1)S(1)} %add_convert_fusion.1), channel_id=1, source_target_pairs={{0,16},{1,17},{2,18},{3,19},{4,20},{5,21},{6,22},{7,23},{8,24},{9,... | collective-permute-start | bytes 294920 | tf_op jit(solution)/shard_map/ppermute | solution.py:86
  67.3 0.9 %collective-permute-start.9 = (bf16[1,256,256]{2,1,0:T(8,128)(2,1)S(1)}, bf16[1,256,256]{2,1,0:T(8,128)(2,1)S(1)}, u32[]{:S(2)}, u32[]{:S(2)}) collective-permute-start(bf16[1,256,256]{2,1,0:T(8,128)(2,1)S(1)} %fusion.29), channel_id=1, source_target_pairs={{0,4},{1,5},{2,6},{3,7},{4,0},{5,1},{6,2},{7,3},{8,12},{9,13},{10,... | collective-permute-start | bytes 393224 | tf_op jit(solution)/shard_map/ppermute | solution.py:83
  68.1 2.0 %collective-permute-done.15 = bf16[192,256]{1,0:T(8,128)(2,1)S(1)} collective-permute-done((bf16[192,256]{1,0:T(8,128)(2,1)S(1)}, bf16[192,256]{1,0:T(8,128)(2,1)S(1)}, u32[]{:S(2)}, u32[]{:S(2)}) %collective-permute-start.15) | collective-permute-done | bytes 98336 | tf_op jit(solution)/shard_map/ppermute | solution.py:86
  70.4 1.3 %collective-permute-done.16.other = bf16[384,256]{1,0:T(8,128)(2,1)S(1)} collective-permute-done((bf16[384,256]{1,0:T(8,128)(2,1)S(1)}, bf16[384,256]{1,0:T(8,128)(2,1)S(1)}, u32[]{:S(2)}, u32[]{:S(2)}) %collective-permute-start.16) | collective-permute-done | bytes 196640 | tf_op jit(solution)/shard_map/ppermute | solution.py:86
  71.7 0.7 copy-done.5
  72.4 2.3 %shard_map.128 = (bf16[256,256]{1,0:T(8,128)(2,1)}, bf16[256,256]{1,0:T(8,128)(2,1)}, bf16[256,256]{1,0:T(8,128)(2,1)}) custom-call(s32[1]{0:T(128)} %bitcast.26.place, bf16[384,256]{1,0:T(8,128)(2,1)} %copy-done, bf16[384,256]{1,0:T(8,128)(2,1)} %copy-done.5, bf16[256,256]{1,0:T(8,128)(2,1)} %link.1, f32[256,256]{1,0:T(8,128)} %inverse_one.1, ...), custom_call_target="tpu_custom_call" | custom-call | flops 100663296 | bytes 1572864 | tf_op jit(solution)/shard_map/pallas_call | solution.py:29
  74.7 0.9 %fusion.34 = bf16[1,256,256]{2,1,0:T(8,128)(2,1)} fusion(f32[2,1,256,256]{3,2,1,0:T(8,128)S(1)} %convert_add_fusion, s32[]{:T(128)S(6)} %select_n.152, bf16[1,256,256]{2,1,0:T(8,128)(2,1)S(1)} %collective-permute-done.9, bf16[256,256]{1,0:T(8,128)(2,1)S(1)} %copy-done.2, bf16[1,256,256]{2,1,0:T(8,128)(2,1)S(1)} %fusion.33, ...), kind=kOutput, calls=%fused_computation.61 | convolution fusion | flops 34013184 | bytes 917512 | tf_op jit(solution)/shard_map/dot_general | solution.py:161
  (57 shorter events, 5.1 us)
Async XLA Ops:
  1.7 11.6 %collective-permute-start = (bf16[4,256,256]{2,1,0:T(8,128)(2,1)S(1)}, bf16[4,256,256]{2,1,0:T(8,128)(2,1)S(1)}, u32[]{:S(2)}, u32[]{:S(2)}) collective-permute-start(bf16[4,256,256]{2,1,0:T(8,128)(2,1)S(1)} %constant_dynamic-slice_fusion.3), channel_id=1, source_target_pairs={{0,16},{1,17},{10,26},{11,27},{20,4},{21,5},{30,14},{31,15}} | collective-permute-start | bytes 1572872 | tf_op jit(solution)/shard_map/ppermute | solution.py:70
  7.7 11.2 %collective-permute-start.5 = (bf16[4,256,256]{2,1,0:T(8,128)(2,1)S(1)}, bf16[4,256,256]{2,1,0:T(8,128)(2,1)S(1)}, u32[]{:S(2)}, u32[]{:S(2)}) collective-permute-start(bf16[4,256,256]{2,1,0:T(8,128)(2,1)S(1)} %constant_dynamic-slice_fusion.1), channel_id=1, source_target_pairs={{0,16},{1,17},{10,26},{11,27},{20,4},{21,5},{30,14},{31,15}} | collective-permute-start | bytes 1572872 | tf_op jit(solution)/shard_map/ppermute | solution.py:70
  13.4 5.6 %collective-permute-start.1 = (bf16[4,256,256]{2,1,0:T(8,128)(2,1)S(1)}, bf16[4,256,256]{2,1,0:T(8,128)(2,1)S(1)}, u32[]{:S(2)}, u32[]{:S(2)}) collective-permute-start(bf16[4,256,256]{2,1,0:T(8,128)(2,1)S(1)} %broadcast_select_fusion.2), channel_id=1, source_target_pairs={{0,8},{1,9},{10,2},{11,3},{4,12},{5,13},{14,6},{15,7},{16,24},{17,... | collective-permute-start | bytes 1572872 | tf_op jit(solution)/shard_map/ppermute | solution.py:80
  19.0 4.9 %copy-start.6 = (s32[32]{0:T(128)S(1)}, s32[32]{0:T(128)}, u32[]{:S(2)}) copy-start(s32[32]{0:T(128)} %param.11) | copy-start | bytes 388
  19.0 5.5 %copy-start.7 = (s32[32]{0:T(128)S(1)}, s32[32]{0:T(128)}, u32[]{:S(2)}) copy-start(s32[32]{0:T(128)} %param.12) | copy-start | bytes 388
  22.5 5.7 %collective-permute-start.6 = (bf16[4,256,256]{2,1,0:T(8,128)(2,1)S(1)}, bf16[4,256,256]{2,1,0:T(8,128)(2,1)S(1)}, u32[]{:S(2)}, u32[]{:S(2)}) collective-permute-start(bf16[4,256,256]{2,1,0:T(8,128)(2,1)S(1)} %broadcast_select_fusion.1), channel_id=1, source_target_pairs={{0,8},{1,9},{10,2},{11,3},{4,12},{5,13},{14,6},{15,7},{16,24},{17,... | collective-permute-start | bytes 1572872 | tf_op jit(solution)/shard_map/ppermute | solution.py:80
  26.6 12.1 %collective-permute-start.2 = (bf16[4,256,256]{2,1,0:T(8,128)(2,1)S(1)}, bf16[4,256,256]{2,1,0:T(8,128)(2,1)S(1)}, u32[]{:S(2)}, u32[]{:S(2)}) collective-permute-start(bf16[4,256,256]{2,1,0:T(8,128)(2,1)S(1)} %get-tuple-element.43), channel_id=1, source_target_pairs={{0,1},{1,0},{2,3},{3,2},{4,5},{5,4},{6,7},{7,6},{8,9},{9,8},{10,11... | collective-permute-start | bytes 1572872 | tf_op jit(solution)/shard_map/ppermute | solution.py:83
  28.2 3.7 %copy-start.3 = (bf16[8,256,256]{2,1,0:T(8,128)(2,1)S(1)}, bf16[8,256,256]{2,1,0:T(8,128)(2,1)}, u32[]{:S(2)}) copy-start(bf16[8,256,256]{2,1,0:T(8,128)(2,1)} %param.13) | copy-start | bytes 3145732
  28.2 4.4 %copy-start.4 = (bf16[8,256,256]{2,1,0:T(8,128)(2,1)S(1)}, bf16[8,256,256]{2,1,0:T(8,128)(2,1)}, u32[]{:S(2)}) copy-start(bf16[8,256,256]{2,1,0:T(8,128)(2,1)} %param.14) | copy-start | bytes 3145732
  33.9 6.5 %collective-permute-start.10 = (bf16[384,256]{1,0:T(8,128)(2,1)S(1)}, bf16[384,256]{1,0:T(8,128)(2,1)S(1)}, u32[]{:S(2)}, u32[]{:S(2)}) collective-permute-start(bf16[384,256]{1,0:T(8,128)(2,1)S(1)} %dynamic-slice_convert_fusion), channel_id=1, source_target_pairs={{0,8},{1,9},{2,10},{3,11},{4,12},{5,13},{6,14},{7,15},{8,0},{9,1},... | collective-permute-start | bytes 589832 | tf_op jit(solution)/shard_map/ppermute | solution.py:86
  38.6 16.3 %collective-permute-start.7 = (bf16[4,256,256]{2,1,0:T(8,128)(2,1)S(1)}, bf16[4,256,256]{2,1,0:T(8,128)(2,1)S(1)}, u32[]{:S(2)}, u32[]{:S(2)}) collective-permute-start(bf16[4,256,256]{2,1,0:T(8,128)(2,1)S(1)} %get-tuple-element.20), channel_id=1, source_target_pairs={{0,1},{1,0},{2,3},{3,2},{4,5},{5,4},{6,7},{7,6},{8,9},{9,8},{10,11... | collective-permute-start | bytes 1572872 | tf_op jit(solution)/shard_map/ppermute | solution.py:83
  40.3 8.5 %collective-permute-start.3 = (bf16[2,256,256]{2,1,0:T(8,128)(2,1)S(1)}, bf16[2,256,256]{2,1,0:T(8,128)(2,1)S(1)}, u32[]{:S(2)}, u32[]{:S(2)}) collective-permute-start(bf16[2,256,256]{2,1,0:T(8,128)(2,1)S(1)} %get-tuple-element.39), channel_id=1, source_target_pairs={{0,2},{1,3},{2,0},{3,1},{4,6},{5,7},{6,4},{7,5},{8,10},{9,11},{10,... | collective-permute-start | bytes 786440 | tf_op jit(solution)/shard_map/ppermute | solution.py:83
  40.5 5.1 %collective-permute-start.11 = (bf16[192,256]{1,0:T(8,128)(2,1)S(1)}, bf16[192,256]{1,0:T(8,128)(2,1)S(1)}, u32[]{:S(2)}, u32[]{:S(2)}) collective-permute-start(bf16[192,256]{1,0:T(8,128)(2,1)S(1)} %dynamic-slice_convert_fusion.1), channel_id=1, source_target_pairs={{0,16},{1,17},{2,18},{3,19},{4,20},{5,21},{6,22},{7,23},{8,24},{9,... | collective-permute-start | bytes 294920 | tf_op jit(solution)/shard_map/ppermute | solution.py:86
  43.0 31.7 %copy-start.2 = (bf16[256,256]{1,0:T(8,128)(2,1)S(1)}, bf16[256,256]{1,0:T(8,128)(2,1)}, u32[]{:S(2)}) copy-start(bf16[256,256]{1,0:T(8,128)(2,1)} %link.1) | copy-start | bytes 393220
  45.7 9.2 %collective-permute-start.12 = (bf16[192,256]{1,0:T(8,128)(2,1)S(1)}, bf16[192,256]{1,0:T(8,128)(2,1)S(1)}, u32[]{:S(2)}, u32[]{:S(2)}) collective-permute-start(bf16[192,256]{1,0:T(8,128)(2,1)S(1)} %add_convert_fusion.4), channel_id=1, source_target_pairs={{0,4},{1,5},{2,6},{3,7},{4,0},{5,1},{6,2},{7,3},{8,12},{9,13},{10,... | collective-permute-start | bytes 294920 | tf_op jit(solution)/shard_map/ppermute | solution.py:83
  48.8 21.4 %collective-permute-start.4 = (bf16[1,256,256]{2,1,0:T(8,128)(2,1)S(1)}, bf16[1,256,256]{2,1,0:T(8,128)(2,1)S(1)}, u32[]{:S(2)}, u32[]{:S(2)}) collective-permute-start(bf16[1,256,256]{2,1,0:T(8,128)(2,1)S(1)} %fusion.30), channel_id=1, source_target_pairs={{0,4},{1,5},{2,6},{3,7},{4,0},{5,1},{6,2},{7,3},{8,12},{9,13},{10,... | collective-permute-start | bytes 393224 | tf_op jit(solution)/shard_map/ppermute | solution.py:83
  54.9 5.8 %collective-permute-start.13 = (bf16[192,256]{1,0:T(8,128)(2,1)S(1)}, bf16[192,256]{1,0:T(8,128)(2,1)S(1)}, u32[]{:S(2)}, u32[]{:S(2)}) collective-permute-start(bf16[192,256]{1,0:T(8,128)(2,1)S(1)} %add_convert_fusion.3), channel_id=1, source_target_pairs={{0,2},{1,3},{2,0},{3,1},{4,6},{5,7},{6,4},{7,5},{8,10},{9,11},{10,... | collective-permute-start | bytes 294920 | tf_op jit(solution)/shard_map/ppermute | solution.py:83
  55.1 10.4 %collective-permute-start.8 = (bf16[2,256,256]{2,1,0:T(8,128)(2,1)S(1)}, bf16[2,256,256]{2,1,0:T(8,128)(2,1)S(1)}, u32[]{:S(2)}, u32[]{:S(2)}) collective-permute-start(bf16[2,256,256]{2,1,0:T(8,128)(2,1)S(1)} %fusion.26), channel_id=1, source_target_pairs={{0,2},{1,3},{2,0},{3,1},{4,6},{5,7},{6,4},{7,5},{8,10},{9,11},{10,... | collective-permute-start | bytes 786440 | tf_op jit(solution)/shard_map/ppermute | solution.py:83
  60.8 4.7 %collective-permute-start.14 = (bf16[192,256]{1,0:T(8,128)(2,1)S(1)}, bf16[192,256]{1,0:T(8,128)(2,1)S(1)}, u32[]{:S(2)}, u32[]{:S(2)}) collective-permute-start(bf16[192,256]{1,0:T(8,128)(2,1)S(1)} %add_convert_fusion.2), channel_id=1, source_target_pairs={{0,1},{1,0},{2,3},{3,2},{4,5},{5,4},{6,7},{7,6},{8,9},{9,8},{10,11... | collective-permute-start | bytes 294920 | tf_op jit(solution)/shard_map/ppermute | solution.py:83
  65.5 4.7 %collective-permute-start.15 = (bf16[192,256]{1,0:T(8,128)(2,1)S(1)}, bf16[192,256]{1,0:T(8,128)(2,1)S(1)}, u32[]{:S(2)}, u32[]{:S(2)}) collective-permute-start(bf16[192,256]{1,0:T(8,128)(2,1)S(1)} %add_convert_fusion.1), channel_id=1, source_target_pairs={{0,16},{1,17},{2,18},{3,19},{4,20},{5,21},{6,22},{7,23},{8,24},{9,... | collective-permute-start | bytes 294920 | tf_op jit(solution)/shard_map/ppermute | solution.py:86
  67.3 7.4 %collective-permute-start.9 = (bf16[1,256,256]{2,1,0:T(8,128)(2,1)S(1)}, bf16[1,256,256]{2,1,0:T(8,128)(2,1)S(1)}, u32[]{:S(2)}, u32[]{:S(2)}) collective-permute-start(bf16[1,256,256]{2,1,0:T(8,128)(2,1)S(1)} %fusion.29), channel_id=1, source_target_pairs={{0,4},{1,5},{2,6},{3,7},{4,0},{5,1},{6,2},{7,3},{8,12},{9,13},{10,... | collective-permute-start | bytes 393224 | tf_op jit(solution)/shard_map/ppermute | solution.py:83
  70.2 1.5 %copy-start = (bf16[384,256]{1,0:T(8,128)(2,1)}, bf16[384,256]{1,0:T(8,128)(2,1)S(1)}, u32[]{:S(2)}) copy-start(bf16[384,256]{1,0:T(8,128)(2,1)S(1)} %pad_maximum_fusion.1.mine) | copy-start | bytes 589828
  70.2 1.5 %collective-permute-start.16 = (bf16[384,256]{1,0:T(8,128)(2,1)S(1)}, bf16[384,256]{1,0:T(8,128)(2,1)S(1)}, u32[]{:S(2)}, u32[]{:S(2)}) collective-permute-start(bf16[384,256]{1,0:T(8,128)(2,1)S(1)} %pad_maximum_fusion.1.mine), channel_id=1, source_target_pairs={{0,8},{1,9},{2,10},{3,11},{4,12},{5,13},{6,14},{7,15},{8,0},{9,1},... | collective-permute-start | bytes 589832 | tf_op jit(solution)/shard_map/ppermute | solution.py:86
  70.4 5.2 %copy-start.1 = (bf16[1,256,256]{2,1,0:T(8,128)(2,1)}, bf16[1,256,256]{2,1,0:T(8,128)(2,1)S(1)}, u32[]{:S(2)}) copy-start(bf16[1,256,256]{2,1,0:T(8,128)(2,1)S(1)} %fusion.33) | copy-start | bytes 393220
  71.7 0.7 copy-start.5
